TPU v7x, 32 devices: a whole 2x2x4 slice. The times are simulated.
32 devices in a mesh: dp: 2 (over x), ctx: 16 (over z, y, core).
Axes of the slice: x: 2, y: 2, z: 4, core: 2. Of those that a mesh axis runs over, the one named last changes fastest.
Arguments:
- tokens: bfloat16 [2, 2048, 1024], P('dp', 'ctx'), may hold values from -6 to 6
- segments: int32 [2, 2048], P('dp', 'ctx'), may hold values from 0 to 7
- cotangent: bfloat16 [2, 2048, 1024], P('dp', 'ctx'), may hold values from -6 to 6
- w_query: bfloat16 [1024, 1024], P(('dp', 'ctx')), may hold values from -0.1875 to 0.1875
- w_key: bfloat16 [1024, 1024], P(('dp', 'ctx')), may hold values from -0.1875 to 0.1875
- w_value: bfloat16 [1024, 1024], P(('dp', 'ctx')), may hold values from -0.1875 to 0.1875
- w_out: bfloat16 [1024, 1024], P(('dp', 'ctx')), may hold values from -0.1875 to 0.1875
- w_up: bfloat16 [1024, 4096], P(('dp', 'ctx')), may hold values from -0.1875 to 0.1875
- w_down: bfloat16 [4096, 1024], P(('dp', 'ctx')), may hold values from -0.09375 to 0.09375
- gain_attn_in: bfloat16 [1024], P(('dp', 'ctx')), may hold values from 0.5 to 1.5
- bias_attn_in: bfloat16 [1024], P(('dp', 'ctx')), may hold values from -1 to 1
- gain_attn_out: bfloat16 [1024], P(('dp', 'ctx')), may hold values from 0.5 to 1.5
- bias_attn_out: bfloat16 [1024], P(('dp', 'ctx')), may hold values from -1 to 1
- gain_mlp_in: bfloat16 [1024], P(('dp', 'ctx')), may hold values from 0.5 to 1.5
- bias_mlp_in: bfloat16 [1024], P(('dp', 'ctx')), may hold values from -1 to 1
- gain_mlp_out: bfloat16 [1024], P(('dp', 'ctx')), may hold values from 0.5 to 1.5
- bias_mlp_out: bfloat16 [1024], P(('dp', 'ctx')), may hold values from -1 to 1
Outputs:
- activations: bfloat16 [2, 2048, 1024], P('dp', 'ctx')
- input_grad: float32 [2, 2048, 1024], P('dp', 'ctx')
- grad_query: float32 [1024, 1024], P(('dp', 'ctx'))
- grad_key: float32 [1024, 1024], P(('dp', 'ctx'))
- grad_value: float32 [1024, 1024], P(('dp', 'ctx'))
- grad_out: float32 [1024, 1024], P(('dp', 'ctx'))
- grad_up: float32 [1024, 4096], P(('dp', 'ctx'))
- grad_down: float32 [4096, 1024], P(('dp', 'ctx'))
- grad_gain_attn_in: float32 [1024], P(('dp', 'ctx'))
- grad_bias_attn_in: float32 [1024], P(('dp', 'ctx'))
- grad_gain_attn_out: float32 [1024], P(('dp', 'ctx'))
- grad_bias_attn_out: float32 [1024], P(('dp', 'ctx'))
- grad_gain_mlp_in: float32 [1024], P(('dp', 'ctx'))
- grad_bias_mlp_in: float32 [1024], P(('dp', 'ctx'))
- grad_gain_mlp_out: float32 [1024], P(('dp', 'ctx'))
- grad_bias_mlp_out: float32 [1024], P(('dp', 'ctx'))
All inputs are finite; a program needn't handle non-finite values.
Results may differ from a plain program's by a relative error of at most 0.018.
Values may be sent and summed in bfloat16 or wider, within the bound.
A program may use at most 384 MiB of HBM per device.

v0:
```python
import math

import jax
import jax.numpy as jnp
from jax import lax
from jax.sharding import PartitionSpec as P

HEADS = 16
HD = 64


norm_eps = 1e-05
masked_value = -1e30


def layer_norm(value, gain, bias):
    row_mean = jnp.mean(value, -1, keepdims=True)
    centred = value - row_mean
    scaled = centred * lax.rsqrt(jnp.mean(centred * centred, -1, keepdims=True) + norm_eps)
    return scaled * gain + bias


def norm_back(value, gain, upstream):
    row_mean = jnp.mean(value, -1, keepdims=True)
    centred = value - row_mean
    inv_std = lax.rsqrt(jnp.mean(centred * centred, -1, keepdims=True) + norm_eps)
    normed = centred * inv_std
    d_normed = upstream * gain
    d_value = inv_std * (
        d_normed
        - jnp.mean(d_normed, -1, keepdims=True)
        - normed * jnp.mean(d_normed * normed, -1, keepdims=True)
    )
    return (d_value, jnp.sum(upstream * normed, 0), jnp.sum(upstream, 0))


def rope_tables(offsets, head_dim):
    freq = 10000.0 ** (-jnp.arange(head_dim // 2, dtype=jnp.float32) / (head_dim // 2))
    angle = offsets.astype(jnp.float32)[..., None] * freq
    return (jnp.cos(angle)[..., None, :], jnp.sin(angle)[..., None, :])


def rotate(values, cos_t, sin_t):
    half_dim = values.shape[-1] // 2
    first = values[..., :half_dim]
    second = values[..., half_dim:]
    return jnp.concatenate([first * cos_t - second * sin_t, second * cos_t + first * sin_t], -1)


def unrotate(grads, cos_t, sin_t):
    half_dim = grads.shape[-1] // 2
    first = grads[..., :half_dim]
    second = grads[..., half_dim:]
    return jnp.concatenate([first * cos_t + second * sin_t, second * cos_t - first * sin_t], -1)


def true_position(flat_index, row_count, ctx_size):
    device_of = flat_index // row_count
    offset_in = flat_index % row_count
    half_rows = row_count // 2
    return jnp.where(
        offset_in < half_rows,
        device_of * half_rows + offset_in,
        (2 * ctx_size - 1 - device_of) * half_rows + offset_in - half_rows,
    )


def split_blocks(array, block_rows):
    return array.reshape((array.shape[0] // block_rows, block_rows) + array.shape[1:])


def score_block(queries, keys, query_pos, query_seg, key_pos, key_seg):
    scores = jnp.einsum(
        "qhd,khd->hqk", queries, keys, preferred_element_type=jnp.float32
    ) * queries.shape[-1] ** (-0.5)
    allowed = (query_seg[:, None] == key_seg[None, :]) & (key_pos[None, :] <= query_pos[:, None])
    return (scores, allowed[None])


def grad_block(queries, d_attn, lse, delta, keys, values, query_pos, query_seg, key_pos, key_seg):
    scores, allowed = score_block(queries, keys, query_pos, query_seg, key_pos, key_seg)
    attn_probs = jnp.where(allowed, jnp.exp(scores - lse[:, :, None]), 0.0)
    d_probs = jnp.einsum("qhd,khd->hqk", d_attn, values, preferred_element_type=jnp.float32)
    d_scores = (attn_probs * (d_probs - delta[:, :, None])).astype(jnp.bfloat16)
    return (attn_probs, d_scores)


def key_terms(
    query_rows,
    dattn_rows,
    lse_rows,
    delta_rows,
    query_pos,
    query_seg,
    key_block,
    value_block,
    key_pos,
    key_seg,
):
    attn_probs, d_scores = grad_block(
        query_rows,
        dattn_rows,
        lse_rows,
        delta_rows,
        key_block,
        value_block,
        query_pos,
        query_seg,
        key_pos,
        key_seg,
    )
    d_keys = jnp.einsum(
        "hqk,qhd->khd", d_scores, query_rows, preferred_element_type=jnp.float32
    ) * query_rows.shape[-1] ** (-0.5)
    d_values = jnp.einsum(
        "hqk,qhd->khd",
        attn_probs.astype(jnp.bfloat16),
        dattn_rows,
        preferred_element_type=jnp.float32,
    )
    return (d_keys, d_values)


def on_device(
    tokens,
    segments,
    cotangent,
    w_query,
    w_key,
    w_value,
    w_out,
    w_up,
    w_down,
    gain_attn_in,
    bias_attn_in,
    gain_attn_out,
    bias_attn_out,
    gain_mlp_in,
    bias_mlp_in,
    gain_mlp_out,
    bias_mlp_out,
):
    whole = (
        lax.all_gather(w_query, ("dp", "ctx"), axis=0, tiled=True),
        lax.all_gather(w_key, ("dp", "ctx"), axis=0, tiled=True),
        lax.all_gather(w_value, ("dp", "ctx"), axis=0, tiled=True),
        lax.all_gather(w_out, ("dp", "ctx"), axis=0, tiled=True),
        lax.all_gather(w_up, ("dp", "ctx"), axis=0, tiled=True),
        lax.all_gather(w_down, ("dp", "ctx"), axis=0, tiled=True),
        lax.all_gather(gain_attn_in, ("dp", "ctx"), axis=0, tiled=True),
        lax.all_gather(bias_attn_in, ("dp", "ctx"), axis=0, tiled=True),
        lax.all_gather(gain_attn_out, ("dp", "ctx"), axis=0, tiled=True),
        lax.all_gather(bias_attn_out, ("dp", "ctx"), axis=0, tiled=True),
        lax.all_gather(gain_mlp_in, ("dp", "ctx"), axis=0, tiled=True),
        lax.all_gather(bias_mlp_in, ("dp", "ctx"), axis=0, tiled=True),
        lax.all_gather(gain_mlp_out, ("dp", "ctx"), axis=0, tiled=True),
        lax.all_gather(bias_mlp_out, ("dp", "ctx"), axis=0, tiled=True),
    )
    query_w, key_w, value_w, out_w, up_w, down_w = whole[:6]
    gain_ai, bias_ai, gain_ao, bias_ao, gain_mi, bias_mi, gain_mo, bias_mo = [
        entry.astype(jnp.float32) for entry in whole[6:]
    ]
    row_count = tokens.shape[1]
    model_width = tokens.shape[2]
    ctx_size = lax.axis_size("ctx")
    seq_length = row_count * ctx_size
    score_scale = HD ** (-0.5)
    seg_all = lax.all_gather(segments, "ctx", axis=1, tiled=True)[0]
    my_seg = segments[0]
    all_pos = true_position(jnp.arange(seq_length, dtype=jnp.int32), row_count, ctx_size)
    my_pos = true_position(
        lax.axis_index("ctx") * row_count + jnp.arange(row_count, dtype=jnp.int32),
        row_count,
        ctx_size,
    )
    doc_first = jnp.min(
        jnp.where(seg_all[None, :] == my_seg[:, None], all_pos[None, :], seq_length), axis=1
    )
    cos_t, sin_t = rope_tables(my_pos - doc_first, HD)
    inputs = tokens[0].astype(jnp.float32)
    attn_in = layer_norm(inputs, gain_ai, bias_ai).astype(jnp.bfloat16)
    query_pre = jnp.dot(attn_in, query_w, preferred_element_type=jnp.float32).reshape(
        row_count, HEADS, HD
    )
    key_pre = jnp.dot(attn_in, key_w, preferred_element_type=jnp.float32).reshape(
        row_count, HEADS, HD
    )
    queries = rotate(query_pre, cos_t, sin_t).astype(jnp.bfloat16)
    keys_rot = rotate(key_pre, cos_t, sin_t).astype(jnp.bfloat16)
    values_flat = jnp.dot(attn_in, value_w, preferred_element_type=jnp.float32).astype(jnp.bfloat16)
    values_heads = values_flat.reshape(row_count, HEADS, HD)
    keys_flat = keys_rot.reshape(row_count, model_width)
    start_state = (
        jnp.full((HEADS, row_count), masked_value, jnp.float32),
        jnp.zeros((HEADS, row_count), jnp.float32),
        jnp.zeros((row_count, HEADS, HD), jnp.float32),
    )
    key_rows = lax.all_gather(keys_flat, "ctx", axis=0, tiled=True)
    value_rows = lax.all_gather(values_flat, "ctx", axis=0, tiled=True)
    span = key_rows.shape[0]
    block_rows = math.gcd(span, 1024)
    key_pos = true_position(jnp.arange(span, dtype=jnp.int32), row_count, ctx_size)
    key_seg = seg_all

    def visit(state_now, parts):
        row_top, row_total, weighted = state_now
        key_block = parts[0].reshape(block_rows, HEADS, HD)
        value_block = parts[1].reshape(block_rows, HEADS, HD)
        scores, allowed = score_block(queries, key_block, my_pos, my_seg, parts[2], parts[3])
        top_new = jnp.maximum(row_top, jnp.max(jnp.where(allowed, scores, masked_value), -1))
        fade = jnp.exp(row_top - top_new)
        attn_probs = jnp.where(allowed, jnp.exp(scores - top_new[:, :, None]), 0.0)
        row_total = row_total * fade + jnp.sum(attn_probs, -1)
        weighted = weighted * fade.T[:, :, None] + jnp.einsum(
            "hqk,khd->qhd",
            attn_probs.astype(jnp.bfloat16),
            value_block,
            preferred_element_type=jnp.float32,
        )
        return ((top_new, row_total, weighted), None)

    blocks = (
        split_blocks(key_rows, block_rows),
        split_blocks(value_rows, block_rows),
        split_blocks(key_pos, block_rows),
        split_blocks(key_seg, block_rows),
    )
    row_top, row_total, weighted = lax.scan(visit, start_state, blocks)[0]
    lse = row_top + jnp.log(row_total)
    attn_f = weighted / row_total.T[:, :, None]
    attn_b = attn_f.reshape(row_count, model_width).astype(jnp.bfloat16)
    branch = jnp.dot(attn_b, out_w, preferred_element_type=jnp.float32)
    resid = inputs + layer_norm(branch, gain_ao, bias_ao)
    mlp_in = layer_norm(resid, gain_mi, bias_mi).astype(jnp.bfloat16)
    hidden_pre = jnp.dot(mlp_in, up_w, preferred_element_type=jnp.float32)
    hidden = jax.nn.gelu(hidden_pre, approximate=True).astype(jnp.bfloat16)
    mlp_out = jnp.dot(hidden, down_w, preferred_element_type=jnp.float32)
    result = resid + layer_norm(mlp_out, gain_mo, bias_mo)
    upstream = cotangent[0].astype(jnp.float32)
    d_mlp_out, dgain_mo, dbias_mo = norm_back(mlp_out, gain_mo, upstream)
    d_mlp_b = d_mlp_out.astype(jnp.bfloat16)
    grad_down = jnp.dot(hidden.T, d_mlp_b, preferred_element_type=jnp.float32)
    d_hidden = jnp.dot(d_mlp_b, down_w.T, preferred_element_type=jnp.float32)
    gelu_back = jax.vjp(lambda pre: jax.nn.gelu(pre, approximate=True), hidden_pre)[1]
    d_pre = gelu_back(d_hidden)[0].astype(jnp.bfloat16)
    grad_up = jnp.dot(mlp_in.T, d_pre, preferred_element_type=jnp.float32)
    d_mlp_in = jnp.dot(d_pre, up_w.T, preferred_element_type=jnp.float32)
    d_resid_n, dgain_mi, dbias_mi = norm_back(resid, gain_mi, d_mlp_in)
    d_resid = upstream + d_resid_n
    d_branch, dgain_ao, dbias_ao = norm_back(branch, gain_ao, d_resid)
    d_branch_b = d_branch.astype(jnp.bfloat16)
    grad_out = jnp.dot(attn_b.T, d_branch_b, preferred_element_type=jnp.float32)
    d_attn_flat = jnp.dot(d_branch_b, out_w.T, preferred_element_type=jnp.float32).astype(
        jnp.bfloat16
    )
    d_attn = d_attn_flat.reshape(row_count, HEADS, HD)
    delta = jnp.sum(d_attn.astype(jnp.float32) * attn_f, -1).T
    zero_heads = jnp.zeros((row_count, HEADS, HD), jnp.float32)

    def query_grad(dq_now, key_rows, value_rows, key_pos, key_seg):
        block_rows = math.gcd(key_rows.shape[0], 1024)

        def visit(dq_run, parts):
            key_block = parts[0].reshape(block_rows, HEADS, HD)
            value_block = parts[1].reshape(block_rows, HEADS, HD)
            d_scores = grad_block(
                queries,
                d_attn,
                lse,
                delta,
                key_block,
                value_block,
                my_pos,
                my_seg,
                parts[2],
                parts[3],
            )[1]
            return (
                dq_run
                + jnp.einsum(
                    "hqk,khd->qhd", d_scores, key_block, preferred_element_type=jnp.float32
                )
                * score_scale,
                None,
            )

        blocks = (
            split_blocks(key_rows, block_rows),
            split_blocks(value_rows, block_rows),
            split_blocks(key_pos, block_rows),
            split_blocks(key_seg, block_rows),
        )
        return lax.scan(visit, dq_now, blocks)[0]

    lse_all, delta_all = (
        lax.all_gather(lse.T, "ctx", axis=0, tiled=True),
        lax.all_gather(delta.T, "ctx", axis=0, tiled=True),
    )
    query_rows = lax.all_gather(queries.reshape(row_count, model_width), "ctx", axis=0, tiled=True)
    dattn_rows = lax.all_gather(d_attn_flat, "ctx", axis=0, tiled=True)
    span = query_rows.shape[0]
    query_block_rows = math.gcd(span, 1024)
    query_pos = true_position(jnp.arange(span, dtype=jnp.int32), row_count, ctx_size)

    def visit(sums, parts):
        d_keys, d_values = key_terms(
            parts[0].reshape(query_block_rows, HEADS, HD),
            parts[1].reshape(query_block_rows, HEADS, HD),
            parts[2].T,
            parts[3].T,
            parts[4],
            parts[5],
            keys_rot,
            values_heads,
            my_pos,
            my_seg,
        )
        return ((sums[0] + d_keys, sums[1] + d_values), None)

    blocks = (
        split_blocks(query_rows, query_block_rows),
        split_blocks(dattn_rows, query_block_rows),
        split_blocks(lse_all, query_block_rows),
        split_blocks(delta_all, query_block_rows),
        split_blocks(query_pos, query_block_rows),
        split_blocks(seg_all, query_block_rows),
    )
    dk_rot, dv_sum = lax.scan(visit, (zero_heads, zero_heads), blocks)[0]
    pieces = (
        lax.all_gather(keys_flat, "ctx", axis=0, tiled=True),
        lax.all_gather(values_flat, "ctx", axis=0, tiled=True),
    )
    span = pieces[0].shape[0]
    key_pos = true_position(jnp.arange(span, dtype=jnp.int32), row_count, ctx_size)
    key_seg = seg_all
    dq_rot = query_grad(zero_heads, pieces[0], pieces[1], key_pos, key_seg)
    d_query = unrotate(dq_rot, cos_t, sin_t).reshape(row_count, model_width).astype(jnp.bfloat16)
    d_key = unrotate(dk_rot, cos_t, sin_t).reshape(row_count, model_width).astype(jnp.bfloat16)
    d_value = dv_sum.reshape(row_count, model_width).astype(jnp.bfloat16)
    grad_query = jnp.dot(attn_in.T, d_query, preferred_element_type=jnp.float32)
    grad_key = jnp.dot(attn_in.T, d_key, preferred_element_type=jnp.float32)
    grad_value = jnp.dot(attn_in.T, d_value, preferred_element_type=jnp.float32)
    d_attn_in = (
        jnp.dot(d_query, query_w.T, preferred_element_type=jnp.float32)
        + jnp.dot(d_key, key_w.T, preferred_element_type=jnp.float32)
        + jnp.dot(d_value, value_w.T, preferred_element_type=jnp.float32)
    )
    d_inputs_n, dgain_ai, dbias_ai = norm_back(inputs, gain_ai, d_attn_in)
    input_grad = (d_resid + d_inputs_n)[None]
    shares = (
        lax.psum_scatter(grad_query, ("dp", "ctx"), scatter_dimension=0, tiled=True),
        lax.psum_scatter(grad_key, ("dp", "ctx"), scatter_dimension=0, tiled=True),
        lax.psum_scatter(grad_value, ("dp", "ctx"), scatter_dimension=0, tiled=True),
        lax.psum_scatter(grad_out, ("dp", "ctx"), scatter_dimension=0, tiled=True),
        lax.psum_scatter(grad_up, ("dp", "ctx"), scatter_dimension=0, tiled=True),
        lax.psum_scatter(grad_down, ("dp", "ctx"), scatter_dimension=0, tiled=True),
        lax.psum_scatter(dgain_ai, ("dp", "ctx"), scatter_dimension=0, tiled=True),
        lax.psum_scatter(dbias_ai, ("dp", "ctx"), scatter_dimension=0, tiled=True),
        lax.psum_scatter(dgain_ao, ("dp", "ctx"), scatter_dimension=0, tiled=True),
        lax.psum_scatter(dbias_ao, ("dp", "ctx"), scatter_dimension=0, tiled=True),
        lax.psum_scatter(dgain_mi, ("dp", "ctx"), scatter_dimension=0, tiled=True),
        lax.psum_scatter(dbias_mi, ("dp", "ctx"), scatter_dimension=0, tiled=True),
        lax.psum_scatter(dgain_mo, ("dp", "ctx"), scatter_dimension=0, tiled=True),
        lax.psum_scatter(dbias_mo, ("dp", "ctx"), scatter_dimension=0, tiled=True),
    )
    return (result.astype(jnp.bfloat16)[None], input_grad) + tuple(shares)


def solution(mesh):
    in_specs = (
        P("dp", "ctx", None),
        P("dp", "ctx"),
        P("dp", "ctx", None),
        P(("dp", "ctx"), None),
        P(("dp", "ctx"), None),
        P(("dp", "ctx"), None),
        P(("dp", "ctx"), None),
        P(("dp", "ctx"), None),
        P(("dp", "ctx"), None),
        P(("dp", "ctx")),
        P(("dp", "ctx")),
        P(("dp", "ctx")),
        P(("dp", "ctx")),
        P(("dp", "ctx")),
        P(("dp", "ctx")),
        P(("dp", "ctx")),
        P(("dp", "ctx")),
    )
    out_specs = (
        P("dp", "ctx", None),
        P("dp", "ctx", None),
        P(("dp", "ctx"), None),
        P(("dp", "ctx"), None),
        P(("dp", "ctx"), None),
        P(("dp", "ctx"), None),
        P(("dp", "ctx"), None),
        P(("dp", "ctx"), None),
        P(("dp", "ctx")),
        P(("dp", "ctx")),
        P(("dp", "ctx")),
        P(("dp", "ctx")),
        P(("dp", "ctx")),
        P(("dp", "ctx")),
        P(("dp", "ctx")),
        P(("dp", "ctx")),
    )
    return jax.shard_map(
        on_device, mesh=mesh, in_specs=in_specs, out_specs=out_specs, check_vma=False
    )
```

profile of v0, /device:TPU:0, one launch (start us, length us, event | category | flops | bytes accessed | tf_op | source)
XLA Modules:
  0.0 1549.5 jit_solution(9376066112478635910)
XLA Ops:
  16.2 42.4 %all-reduce.17 = (bf16[1024]{0:T(1024)(128)(2,1)S(1)}, bf16[1024]{0:T(1024)(128)(2,1)S(1)}, bf16[1024]{0:T(1024)(128)(2,1)S(1)}, bf16[1024]{0:T(1024)(128)(2,1)S...) all-reduce(bf16[1024]{0:T(1024)(128)(2,1)S(1)} %dynamic-update-slic, ...), channel_id=1, replica_groups=mesh['dp'=2,'ctx'=16] {'dp','ctx'}, use_global_device_ids=true, to_apply=%add.1 | all-reduce | flops 8192 | bytes 32768
  58.6 21.1 %all_gather.65 = s32[1,2048]{1,0:T(1,128)S(1)} all-gather(s32[1,128]{1,0:T(1,128)} %param.24), channel_id=1, replica_groups=mesh['dp'=2,'ctx'=16] {'ctx'}, dimensions={1}, use_global_device_ids=true | all-gather | bytes 8704 | tf_op jit(solution)/shard_map/all_gather | solution.py:168
  86.0 42.4 %all-gather.11.cloned.1.call-done = bf16[1024,1024]{1,0:T(8,128)(2,1)} async-done(((bf16[32,1024]{1,0:T(8,128)(2,1)}), bf16[1024,1024]{1,0:T(8,128)(2,1)}) %all-gather.11.cloned.1.call-update) | async-done | bytes 2097168 | tf_op jit(solution)/shard_map/all_gather | solution.py:145
  135.9 50.7 %all-gather.17.cloned.1.call-done = bf16[1024,1024]{1,0:T(8,128)(2,1)} async-done(((bf16[32,1024]{1,0:T(8,128)(2,1)}), bf16[1024,1024]{1,0:T(8,128)(2,1)}) %all-gather.17.cloned.1.call-update) | async-done | bytes 2097168 | tf_op jit(solution)/shard_map/all_gather | solution.py:146
  194.2 44.4 %all-gather.13.cloned.1.call-done = bf16[2048,1024]{1,0:T(8,128)(2,1)} async-done(((bf16[128,1024]{1,0:T(8,128)(2,1)}), bf16[2048,1024]{1,0:T(8,128)(2,1)}) %all-gather.13.cloned.1.call-update) | async-done | bytes 4194320 | tf_op jit(solution)/shard_map/all_gather | solution.py:198
  238.6 6.2 copy.80
  244.8 44.9 %all-gather.19.cloned.1.call-done = bf16[2048,1024]{1,0:T(8,128)(2,1)} async-done(((bf16[128,1024]{1,0:T(8,128)(2,1)}), bf16[2048,1024]{1,0:T(8,128)(2,1)}) %all-gather.19.cloned.1.call-update) | async-done | bytes 4194320 | tf_op jit(solution)/shard_map/all_gather | solution.py:199
  289.7 6.3 copy.81
  296.0 32.0 %while.39 = (s32[]{:T(128)}, f32[16,128]{1,0:T(8,128)S(1)}, f32[16,128]{1,0:T(8,128)S(1)}, f32[128,16,64]{0,2,1:T(8,128)S(1)}, s32[1,128]{1,0:T(1,128)S(1)}, /*i...) while((s32[]{:T(128)}, f32[16,128]{1,0:T(8,128)S(1)}, ...), condition=%wide.region_6.7_spmd.clone, body=%wide.region_3.6_spmd.clone.sunk | while | flops 560741888 | bytes 73295536 | solution.py:228
  328.0 19.4 %all-gather.21.cloned.1.call-done = bf16[1024,1024]{1,0:T(8,128)(2,1)} async-done(((bf16[32,1024]{1,0:T(8,128)(2,1)}), bf16[1024,1024]{1,0:T(8,128)(2,1)}) %all-gather.21.cloned.1.call-update) | async-done | bytes 2097168 | tf_op jit(solution)/shard_map/all_gather | solution.py:147
  350.3 76.4 %all-gather.23.cloned.1.call-done = bf16[1024,4096]{1,0:T(8,128)(2,1)} async-done(((bf16[32,4096]{1,0:T(8,128)(2,1)}), bf16[1024,4096]{1,0:T(8,128)(2,1)}) %all-gather.23.cloned.1.call-update) | async-done | bytes 8388624 | tf_op jit(solution)/shard_map/all_gather | solution.py:148
  426.7 6.1 fusion.136
  432.8 73.0 %all-gather.25.cloned.1.call-done = bf16[4096,1024]{1,0:T(8,128)(2,1)} async-done(((bf16[128,1024]{1,0:T(8,128)(2,1)}), bf16[4096,1024]{1,0:T(8,128)(2,1)}) %all-gather.25.cloned.1.call-update) | async-done | bytes 8388624 | tf_op jit(solution)/shard_map/all_gather | solution.py:149
  505.8 5.8 fusion.153
  525.2 21.0 %all_gather.83 = f32[2048,16]{0,1:T(8,128)S(1)} all-gather(f32[128,16]{0,1:T(8,128)S(1)} %bitcast.361), channel_id=1, replica_groups=mesh['dp'=2,'ctx'=16] {'ctx'}, dimensions={0}, use_global_device_ids=true | all-gather | bytes 139264 | tf_op jit(solution)/shard_map/all_gather | solution.py:296
  551.2 35.1 %while.40 = (s32[]{:T(128)}, f32[128,16,64]{0,2,1:T(8,128)}, bf16[2,1024,1024]{1,2,0:T(8,128)(2,1)}, s32[1,128]{1,0:T(1,128)S(1)}, s32[2,1024]{1,0:T(2,128)S(1)}...) while((s32[]{:T(128)}, f32[128,16,64]{0,2,1:T(8,128)}, ...), condition=%wide.region_21.22_spmd.clone, body=%wide.region_20.21_spmd.clone.sunk | while | flops 818679296 | bytes 33334936 | solution.py:293
  560.2 8.6 fusion.239
  577.7 8.6 fusion.239
  586.3 18.6 %all_gather.85 = f32[2048,16]{0,1:T(8,128)S(1)} all-gather(f32[128,16]{0,1:T(8,128)S(1)} %bitcast.360), channel_id=1, replica_groups=mesh['dp'=2,'ctx'=16] {'ctx'}, dimensions={0}, use_global_device_ids=true | all-gather | bytes 139264 | tf_op jit(solution)/shard_map/all_gather | solution.py:297
  610.0 67.5 %while.41 = (s32[]{:T(128)}, f32[128,16,64]{0,2,1:T(8,128)}, f32[128,16,64]{0,2,1:T(8,128)}, bf16[2,1024,1024]{2,1,0:T(8,128)(2,1)}, s32[2,1024]{1,0:T(2,128)S(1...) while((s32[]{:T(128)}, f32[128,16,64]{0,2,1:T(8,128)}, ...), condition=%wide.region_23.24_spmd.clone, body=%wide.region_22.23_spmd.clone.sunk | while | flops 1095765504 | bytes 55142080 | solution.py:328
  626.7 6.2 fusion.249
  632.9 10.8 fusion.248
  660.3 6.3 fusion.249
  666.7 10.8 fusion.248
  692.0 8.3 fusion.137
  701.8 8.2 fusion.135
  715.8 39.8 %all-reduce.16 = (f32[1024]{0:T(1024)S(1)}, f32[1024]{0:T(1024)S(1)}, f32[1024]{0:T(1024)S(1)}, f32[1024]{0:T(1024)S(1)}, f32[1024]{0:T(1024)S(1)}, /*index=5*/f...) all-reduce(f32[1024]{0:T(1024)S(1)} %get-tuple-element.487, ...), channel_id=8, replica_groups=mesh['dp'=2,'ctx'=16] {'dp','ctx'}, use_global_device_ids=true, to_apply=%region_33.34.clone | all-reduce | flops 8192 | bytes 65536
  762.4 130.3 %reduce-scatter.9.cloned.1.call-done = f32[32,1024]{1,0:T(8,128)} async-done(((f32[1024,1024]{1,0:T(8,128)}), f32[32,1024]{1,0:T(8,128)}) %reduce-scatter.9.cloned.1.call-update) | async-done | bytes 131088 | tf_op jit(solution)/shard_map/reduce_scatter | solution.py:352
  892.7 140.2 %reduce-scatter.7.cloned.1.call-done = f32[32,1024]{1,0:T(8,128)} async-done(((f32[1024,1024]{1,0:T(8,128)}), f32[32,1024]{1,0:T(8,128)}) %reduce-scatter.7.cloned.1.call-update) | async-done | bytes 131088 | tf_op jit(solution)/shard_map/reduce_scatter | solution.py:351
  1032.8 140.1 %reduce-scatter.11.cloned.1.call-done = f32[32,1024]{1,0:T(8,128)} async-done(((f32[1024,1024]{1,0:T(8,128)}), f32[32,1024]{1,0:T(8,128)}) %reduce-scatter.11.cloned.1.call-update) | async-done | bytes 131088 | tf_op jit(solution)/shard_map/reduce_scatter | solution.py:353
  1172.9 183.0 %reduce-scatter.17.cloned.1.call-done = f32[128,1024]{1,0:T(8,128)} async-done(((f32[4096,1024]{1,0:T(8,128)}), f32[128,1024]{1,0:T(8,128)}) %reduce-scatter.17.cloned.1.call-update) | async-done | bytes 524304 | tf_op jit(solution)/shard_map/reduce_scatter | solution.py:356
  1355.9 186.8 %reduce-scatter.15.cloned.1.call-done = f32[32,4096]{1,0:T(8,128)} async-done(((f32[1024,4096]{1,0:T(8,128)}), f32[32,4096]{1,0:T(8,128)}) %reduce-scatter.15.cloned.1.call-update) | async-done | bytes 524304 | tf_op jit(solution)/shard_map/reduce_scatter | solution.py:355
  (336 shorter events, 167.1 us)
Async XLA Ops:
  7.2 75.9 %all-gather.15.cloned.1.call-start = ((), (), s32[]{:S(2)}) async-start(), calls=%async_computation.8 | async-start | bytes 2162688 | tf_op jit(solution)/shard_map/all_gather | solution.py:144
  7.9 120.5 %all-gather.11.cloned.1.call-start = ((), (), s32[]{:S(2)}) async-start(), calls=%async_computation.6 | async-start | bytes 2162688 | tf_op jit(solution)/shard_map/all_gather | solution.py:145
  8.7 177.9 %all-gather.17.cloned.1.call-start = ((), (), s32[]{:S(2)}) async-start(), calls=%async_computation.9 | async-start | bytes 2162688 | tf_op jit(solution)/shard_map/all_gather | solution.py:146
  9.4 229.2 %all-gather.13.cloned.1.call-start = ((), (), s32[]{:S(2)}) async-start(), calls=%async_computation.7 | async-start | bytes 4456448 | tf_op jit(solution)/shard_map/all_gather | solution.py:198
  58.5 128.0 %copy-start.35 = (f32[1024]{0:T(1024)}, f32[1024]{0:T(1024)S(1)}, u32[]{:S(2)}) copy-start(f32[1024]{0:T(1024)S(1)} %convert_element_type.154) | copy-start | bytes 12292
  58.5 128.0 %copy-start.42 = (f32[1024]{0:T(1024)}, f32[1024]{0:T(1024)S(1)}, u32[]{:S(2)}) copy-start(f32[1024]{0:T(1024)S(1)} %convert_element_type.155) | copy-start | bytes 12292
  80.7 105.8 %copy-start.46 = (f32[128]{0:T(128)}, f32[128]{0:T(128)S(1)}, u32[]{:S(2)}) copy-start(f32[128]{0:T(128)S(1)} %broadcast_multiply_fusion.11) | copy-start | bytes 1540
  82.9 103.7 %copy-start.50 = (f32[128]{0:T(128)}, f32[128]{0:T(128)S(1)}, u32[]{:S(2)}) copy-start(f32[128]{0:T(128)S(1)} %add_rsqrt_fusion.3) | copy-start | bytes 1540
  83.0 51.7 %copy-start.38 = (f32[128,32]{0,1:T(8,128)}, f32[128,32]{0,1:T(8,128)S(1)}, u32[]{:S(2)}) copy-start(f32[128,32]{0,1:T(8,128)S(1)} %get-tuple-element.618) | copy-start | bytes 49156
  135.0 56.6 %copy-start.5 = (bf16[128,16,64]{0,2,1:T(8,128)(2,1)}, bf16[128,16,64]{0,2,1:T(8,128)(2,1)S(1)}, u32[]{:S(2)}) copy-start(bf16[128,16,64]{0,2,1:T(8,128)(2,1)S(1)} %maximum_convert_fusion) | copy-start | bytes 786436
  135.8 153.9 %all-gather.19.cloned.1.call-start = ((), (), s32[]{:S(2)}) async-start(), calls=%async_computation.10 | async-start | bytes 4456448 | tf_op jit(solution)/shard_map/all_gather | solution.py:199
  189.4 157.9 %all-gather.21.cloned.1.call-start = ((), (), s32[]{:S(2)}) async-start(), calls=%async_computation.11 | async-start | bytes 2162688 | tf_op jit(solution)/shard_map/all_gather | solution.py:147
  190.0 236.7 %all-gather.23.cloned.1.call-start = ((), (), s32[]{:S(2)}) async-start(), calls=%async_computation.12 | async-start | bytes 8650752 | tf_op jit(solution)/shard_map/all_gather | solution.py:148
  190.8 315.0 %all-gather.25.cloned.1.call-start = ((), (), s32[]{:S(2)}) async-start(), calls=%async_computation.13 | async-start | bytes 8650752 | tf_op jit(solution)/shard_map/all_gather | solution.py:149
  191.5 413.6 %all-gather.27.cloned.1.call-start = ((), (), s32[]{:S(2)}) async-start(), calls=%async_computation.14 | async-start | bytes 4456448 | tf_op jit(solution)/shard_map/all_gather | solution.py:299
  192.8 328.2 %copy-start.30 = (f32[1024]{0:T(1024)}, f32[1024]{0:T(1024)S(1)}, u32[]{:S(2)}) copy-start(f32[1024]{0:T(1024)S(1)} %convert_element_type.168) | copy-start | bytes 12292
  192.8 233.9 %copy-start.32 = (f32[1024]{0:T(1024)}, f32[1024]{0:T(1024)S(1)}, u32[]{:S(2)}) copy-start(f32[1024]{0:T(1024)S(1)} %convert_element_type.169) | copy-start | bytes 12292
  192.9 320.5 %copy-start.44 = (f32[1024]{0:T(1024)}, f32[1024]{0:T(1024)S(1)}, u32[]{:S(2)}) copy-start(f32[1024]{0:T(1024)S(1)} %convert_element_type.172) | copy-start | bytes 12292
  193.9 416.2 %all-gather.29.cloned.1.call-start = ((), (), s32[]{:S(2)}) async-start(), calls=%async_computation.15 | async-start | bytes 4456448 | tf_op jit(solution)/shard_map/all_gather | solution.py:300
  350.0 171.0 %copy-start.1 = (f32[128,1024]{1,0:T(8,128)}, f32[128,1024]{1,0:T(8,128)S(1)}, u32[]{:S(2)}) copy-start(f32[128,1024]{1,0:T(8,128)S(1)} %get-tuple-element.588) | copy-start | bytes 1572868
  350.0 171.0 %copy-start.48 = (f32[128]{0:T(128)}, f32[128]{0:T(128)S(1)}, u32[]{:S(2)}) copy-start(f32[128]{0:T(128)S(1)} %broadcast_multiply_fusion.9) | copy-start | bytes 1540
  350.3 170.8 %copy-start.52 = (f32[128]{0:T(128)}, f32[128]{0:T(128)S(1)}, u32[]{:S(2)}) copy-start(f32[128]{0:T(128)S(1)} %add_rsqrt_fusion.1) | copy-start | bytes 1540
  432.8 79.0 %copy-start.17 = (bf16[1,128,1024]{2,1,0:T(8,128)(2,1)S(1)}, bf16[1,128,1024]{2,1,0:T(8,128)(2,1)}, u32[]{:S(2)}) copy-start(bf16[1,128,1024]{2,1,0:T(8,128)(2,1)} %param.25) | copy-start | bytes 786436
  524.2 238.1 %reduce-scatter.13.cloned.1.call-start = ((), (), s32[]{:S(2)}) async-start(), calls=%async_computation.19 | async-start | bytes 4325376 | tf_op jit(solution)/shard_map/reduce_scatter | solution.py:354
  550.3 342.4 %reduce-scatter.9.cloned.1.call-start = ((), (), s32[]{:S(2)}) async-start(), calls=%async_computation.17 | async-start | bytes 4325376 | tf_op jit(solution)/shard_map/reduce_scatter | solution.py:352
  551.2 58.8 %copy-start.6 = (bf16[128,16,64]{0,2,1:T(8,128)(2,1)S(1)}, bf16[128,16,64]{0,2,1:T(8,128)(2,1)}, u32[]{:S(2)}) copy-start(bf16[128,16,64]{0,2,1:T(8,128)(2,1)} %copy-done.5) | copy-start | bytes 786436
  610.0 67.5 %copy-start.39 = (f32[128,32]{0,1:T(8,128)S(1)}, f32[128,32]{0,1:T(8,128)}, u32[]{:S(2)}) copy-start(f32[128,32]{0,1:T(8,128)} %copy-done.38) | copy-start | bytes 49156
  610.0 67.5 %copy-start.41 = (f32[128,32]{0,1:T(8,128)S(1)}, f32[128,32]{0,1:T(8,128)}, u32[]{:S(2)}) copy-start(f32[128,32]{0,1:T(8,128)} %copy-done.40) | copy-start | bytes 49156
  682.5 350.3 %reduce-scatter.7.cloned.1.call-start = ((), (), s32[]{:S(2)}) async-start(), calls=%async_computation.16 | async-start | bytes 4325376 | tf_op jit(solution)/shard_map/reduce_scatter | solution.py:351
  686.4 486.5 %reduce-scatter.11.cloned.1.call-start = ((), (), s32[]{:S(2)}) async-start(), calls=%async_computation.18 | async-start | bytes 4325376 | tf_op jit(solution)/shard_map/reduce_scatter | solution.py:353
  690.3 665.6 %reduce-scatter.17.cloned.1.call-start = ((), (), s32[]{:S(2)}) async-start(), calls=%async_computation.21 | async-start | bytes 17301504 | tf_op jit(solution)/shard_map/reduce_scatter | solution.py:356
  700.4 842.3 %reduce-scatter.15.cloned.1.call-start = ((), (), s32[]{:S(2)}) async-start(), calls=%async_computation.20 | async-start | bytes 17301504 | tf_op jit(solution)/shard_map/reduce_scatter | solution.py:355
  (56 other events, 245.4 us)
Sparse Core Ops, SparseCore 0:
  10.9 59.1 all-gather.14
  73.0 55.3 all-gather.10
  131.3 55.2 all-gather.16
  189.2 49.3 all-gather.12
  240.6 49.0 all-gather.18
  292.4 54.9 all-gather.20
  350.2 76.4 all-gather.22
  429.6 76.1 all-gather.24
  507.9 49.7 all-gather.26
  559.7 50.2 all-gather.28
  612.9 139.7 reduce-scatter.12
  755.4 137.2 reduce-scatter.8
  895.5 137.2 reduce-scatter.6
  1035.5 137.3 reduce-scatter.10
  1175.6 180.2 reduce-scatter.16
  1358.7 184.0 reduce-scatter.14
where the time goes:
time: 1560 us; the launch traced here: 1550 us
  waiting for transfers between devices  1140 us (73%)
  matrix products  149 us (10%)
  blocking collectives  143 us (9%)
  local copies, waits for them, and re-layouts  82.2 us (5%)
  other arithmetic  17.4 us (1%)
    reduce_scatter x1, waiting for transfers between devices, on_device(): lax.psum_scatter(grad_up, ('dp', 'ctx'), scatter_dimension=0, tiled=True)  187 us
    reduce_scatter x1, waiting for transfers between devices, on_device(): lax.psum_scatter(grad_down, ('dp', 'ctx'), scatter_dimension=0, tiled=True)  183 us
    reduce_scatter x1, waiting for transfers between devices, on_device(): lax.psum_scatter(grad_query, ('dp', 'ctx'), scatter_dimension=0, tiled=True)  140 us
    reduce_scatter x1, waiting for transfers between devices, on_device(): lax.psum_scatter(grad_value, ('dp', 'ctx'), scatter_dimension=0, tiled=True)  140 us
    reduce_scatter x1, waiting for transfers between devices, on_device(): lax.psum_scatter(grad_key, ('dp', 'ctx'), scatter_dimension=0, tiled=True)  130 us
    unnamed x2, blocking collectives  82.2 us
    all_gather x1, waiting for transfers between devices, on_device(): lax.all_gather(w_up, ('dp', 'ctx'), axis=0, tiled=True)  76.4 us
    all_gather x1, waiting for transfers between devices, on_device(): lax.all_gather(w_down, ('dp', 'ctx'), axis=0, tiled=True)  73 us
  transfers between devices with their start and end apart: 16, of which 13 were waited for; matrix products, arithmetic and copies ran while one was open for 15% of the time, Pallas kernels for 0%

commit v1 on v0

--- a/solution.py
+++ b/solution.py
@@ -3,6 +3,8 @@
 import jax
 import jax.numpy as jnp
 from jax import lax
+from jax.experimental import pallas as pl
+from jax.experimental.pallas import tpu as pltpu
 from jax.sharding import PartitionSpec as P
 
 HEADS = 16
@@ -366,6 +368,1014 @@
     return (result.astype(jnp.bfloat16)[None], input_grad) + tuple(shares)
 
 
+BF = jnp.bfloat16
+F32 = jnp.float32
+MESH_ID = pl.DeviceIdType.MESH
+GROUP = 4
+SPOTS = 8
+ROWS = 128
+WIDTH = 1024
+VMEM_BYTES = 60 << 20
+
+
+def dot(left, right, left_dim, right_dim):
+    return lax.dot_general(
+        left, right, (((left_dim,), (right_dim,)), ((), ())), preferred_element_type=F32
+    )
+
+
+class Here:
+    def __init__(self):
+        self.x = lax.axis_index("dp")
+        at = lax.axis_index("ctx")
+        self.z, self.y, self.c = at // 4, (at // 2) % 2, at % 2
+        self.member = at % 4
+        self.shard = 4 * self.x + self.z
+        self.spot = self.z + self.x * (7 - 2 * self.z)
+        self.core_mate = self.place(self.x, self.z, self.y, 1 - self.c)
+        self.link_mate = self.place(self.x, self.z, 1 - self.y, self.c)
+        self.far_mate = self.place(self.x, self.z, 1 - self.y, 1 - self.c)
+        self.core_member = 2 * self.y + (1 - self.c)
+        self.link_member = 2 * (1 - self.y) + self.c
+        self.far_member = 2 * (1 - self.y) + (1 - self.c)
+        self.right = self.on_ring(self.spot + 1)
+        self.left = self.on_ring(self.spot + SPOTS - 1)
+
+    @staticmethod
+    def place(x, z, y, c):
+        return (x, 4 * z + 2 * y + c)
+
+    def on_ring(self, spot):
+        spot = lax.rem(spot, SPOTS)
+        x = spot // 4
+        return self.place(x, spot + x * (7 - 2 * spot), self.y, self.c)
+
+    @staticmethod
+    def shard_at(spot):
+        spot = lax.rem(spot, SPOTS)
+        x = spot // 4
+        return 4 * x + spot + x * (7 - 2 * spot)
+
+    def plane(self, step):
+        shard = lax.rem(self.shard + step, SPOTS)
+        return shard, self.place(shard // 4, shard % 4, self.y, self.c)
+
+    def along_z(self, step):
+        z = lax.rem(self.z + step, 4)
+        return z, self.place(self.x, z, self.y, self.c)
+
+    def mates(self):
+        return (
+            (self.core_member, self.core_mate),
+            (self.link_member, self.link_mate),
+            (self.far_member, self.far_mate),
+        )
+
+
+class Post:
+    def __init__(self, send_sems, recv_sems):
+        self.send_sems, self.recv_sems = send_sems, recv_sems
+        self.count = 0
+        self.started = []
+
+    def send(self, src, dst, to):
+        copy = pltpu.make_async_remote_copy(
+            src_ref=src,
+            dst_ref=dst,
+            send_sem=self.send_sems.at[self.count],
+            recv_sem=self.recv_sems.at[self.count],
+            device_id=to,
+            device_id_type=MESH_ID,
+        )
+        copy.start()
+        self.started.append(copy)
+        self.count += 1
+        return self.count - 1, to
+
+    def arrived(self, sent, landing):
+        number, to = sent
+        pltpu.make_async_remote_copy(
+            src_ref=landing,
+            dst_ref=landing,
+            send_sem=self.send_sems.at[number],
+            recv_sem=self.recv_sems.at[number],
+            device_id=to,
+            device_id_type=MESH_ID,
+        ).wait_recv()
+
+    def finish(self):
+        for copy in self.started:
+            copy.wait_send()
+
+
+class Local:
+    def __init__(self, sems):
+        self.sems = sems
+        self.started = []
+
+    def copy(self, src, dst):
+        copy = pltpu.make_async_copy(src, dst, self.sems.at[len(self.started)])
+        copy.start()
+        self.started.append(copy)
+
+    def finish(self):
+        for copy in self.started:
+            copy.wait()
+
+
+def greet(places):
+    barrier = pltpu.get_barrier_semaphore()
+    for place in places:
+        pl.semaphore_signal(barrier, inc=1, device_id=place, device_id_type=MESH_ID)
+    pl.semaphore_wait(barrier, len(places))
+
+
+class RingGather:
+    STREAMS = ((1, 0, 4), (-1, 1, 4), (1, 1, 3), (-1, 0, 3))
+
+    def __init__(self, here, post, held, own):
+        self.here, self.post, self.held, self.own = here, post, held, own
+        self.half = held.shape[1] // 2
+        self.waiting = {}
+        self.hops = 0
+
+    def piece(self, shard, half):
+        return self.held.at[shard, pl.ds(half * self.half, self.half)]
+
+    def hop(self):
+        self.hops += 1
+        for way, half, length in self.STREAMS:
+            if self.hops > length:
+                continue
+            if self.hops > 1:
+                self.take(way, half)
+            origin = self.here.shard_at(self.here.spot + SPOTS - way * (self.hops - 1))
+            src = self.piece(origin, half)
+            if self.hops == 1:
+                src = self.own.at[pl.ds(half * self.half, self.half)]
+            sent = self.post.send(
+                src, self.piece(origin, half), self.here.right if way == 1 else self.here.left
+            )
+            came = self.here.shard_at(self.here.spot + SPOTS - way * self.hops)
+            self.waiting[way, half] = (sent, self.piece(came, half))
+
+    def take(self, way, half):
+        sent, landing = self.waiting.pop((way, half))
+        self.post.arrived(sent, landing)
+
+    def finish(self):
+        while self.hops < 4:
+            self.hop()
+        for key in list(self.waiting):
+            self.take(*key)
+
+
+class RingSum:
+    def __init__(self, here, post, parts, landing):
+        self.here, self.post, self.parts, self.landing = here, post, parts, landing
+        self.half = parts.shape[1] // 2
+        self.waiting = {}
+        self.slots = 0
+        self.hops = 0
+
+    def part(self, distance, half):
+        shard = self.here.shard_at(self.here.spot + SPOTS + distance)
+        return self.parts.at[shard, pl.ds(half * self.half, self.half)]
+
+    def hop(self):
+        self.hops += 1
+        distance = 5 - self.hops
+        for way, half, first in ((1, 0, 1), (-1, 1, 1), (1, 1, 2), (-1, 0, 2)):
+            if self.hops < first:
+                continue
+            src = self.part(way * distance, half)
+            if self.hops > first:
+                held = self.take(way, half)
+                held[...] = (held[...].astype(F32) + src[...].astype(F32)).astype(held.dtype)
+                src = held
+            slot = self.landing.at[self.slots]
+            self.slots += 1
+            sent = self.post.send(src, slot, self.here.right if way == 1 else self.here.left)
+            self.waiting[way, half] = (sent, slot)
+
+    def take(self, way, half):
+        sent, slot = self.waiting.pop((way, half))
+        self.post.arrived(sent, slot)
+        return slot
+
+    def total(self):
+        halves = []
+        for half in (0, 1):
+            value = self.part(0, half)[...].astype(F32)
+            for way in (1, -1):
+                value = value + self.take(way, half)[...].astype(F32)
+            halves.append(value)
+        return halves
+
+
+def group_gather(here, post, held):
+    mine = held.at[here.member]
+    over = post.send(mine, mine, here.link_mate)
+    near = post.send(mine, mine, here.core_mate)
+    linked = held.at[here.link_member]
+    post.arrived(over, linked)
+    passed = post.send(linked, linked, here.core_mate)
+    post.arrived(near, held.at[here.core_member])
+    post.arrived(passed, held.at[here.far_member])
+
+
+class GroupSum:
+    def __init__(self, here, post, near_send, near_in, far_send, far_in):
+        self.here, self.post = here, post
+        self.near_send, self.near_in = near_send, near_in
+        self.far_send, self.far_in = far_send, far_in
+
+    def start(self, term):
+        here, post = self.here, self.post
+        near = []
+        for slot, member in ((0, here.far_member), (1, here.core_member)):
+            self.near_send[slot] = term(member).astype(BF)
+            near.append(
+                post.send(self.near_send.at[slot], self.near_in.at[slot], here.core_mate)
+            )
+        over = term(here.link_member)
+        post.arrived(near[0], self.near_in.at[0])
+        self.far_send[...] = (over + self.near_in[0].astype(F32)).astype(BF)
+        self.far = post.send(self.far_send, self.far_in, here.link_mate)
+        self.near = near[1]
+        self.mine = term(here.member)
+
+    def total(self):
+        self.post.arrived(self.near, self.near_in.at[1])
+        value = self.mine + self.near_in[1].astype(F32)
+        self.post.arrived(self.far, self.far_in)
+        return value + self.far_in[...].astype(F32)
+
+
+def swap_along_z(here, post, local, src, dst):
+    local.copy(src.at[here.z], dst.at[here.z])
+    sent = []
+    for step in (1, 2, 3):
+        z, place = here.along_z(step)
+        came = lax.rem(here.z + 4 - step, 4)
+        sent.append((post.send(src.at[z], dst.at[here.z], place), dst.at[came]))
+    return sent
+
+
+def out_rows_target(here):
+    return here.z % 2, 2 * here.y + here.c, here.z // 2, here.x
+
+
+def out_rows_source(here):
+    return here.c, 2 * here.y + here.x, here.z // 2, here.z % 2
+
+
+def same_place(here, spot):
+    x, z, y, c = spot
+    return (x == here.x) & (z == here.z) & (y == here.y) & (c == here.c)
+
+
+def turn_tables(rot):
+    index = lax.broadcasted_iota(jnp.int32, (HD // 2, 1), 0).astype(F32)
+    angle = rot * jnp.exp(index * (-math.log(10000.0) / (HD // 2)))
+    return jnp.cos(angle), jnp.sin(angle)
+
+
+def norm_parts(value):
+    centred = value - jnp.mean(value, -1, keepdims=True)
+    inv_std = lax.rsqrt(jnp.mean(centred * centred, -1, keepdims=True) + norm_eps)
+    return centred * inv_std, inv_std
+
+
+def norm_pull(normed, inv_std, gain, upstream):
+    d_normed = upstream * gain
+    return inv_std * (
+        d_normed
+        - jnp.mean(d_normed, -1, keepdims=True)
+        - normed * jnp.mean(d_normed * normed, -1, keepdims=True)
+    )
+
+
+def first_kernel(
+    tok, small, wq, wk, wv, wo, wu,
+    qkv_heads, a_t, wqkv_out, wo_all, wu_shard, vectors, starts,
+    x_all, wqkv, wqkv_send, wu_send, wu_in, small_in, small_all, qkv_send, wo_in,
+    send_sems, recv_sems, local_sems, self_sems,
+):
+    here = Here()
+    post = Post(send_sems, recv_sems)
+    local = Local(local_sems)
+    out_to, out_from = out_rows_target(here), out_rows_source(here)
+    out_stays = same_place(here, out_to)
+    barrier = pltpu.get_barrier_semaphore()
+    partners = [place for _, place in here.mates()] + [here.plane(n)[1] for n in range(1, SPOTS)]
+    for place in partners:
+        pl.semaphore_signal(barrier, inc=1, device_id=place, device_id_type=MESH_ID)
+    pl.when(jnp.logical_not(out_stays))(
+        lambda: pl.semaphore_signal(
+            barrier, inc=1, device_id=here.place(*out_from), device_id_type=MESH_ID
+        )
+    )
+    for member in range(GROUP):
+        base = 512 * (member % 2) + 256 * (member // 2)
+        for slot, weight in enumerate((wq, wk, wv)):
+            wqkv_send[member, :, 256 * slot : 256 * (slot + 1)] = weight[:, base : base + 256]
+        for shard in range(SPOTS):
+            at = 512 * shard + 128 * member
+            wu_send[member, :, 128 * shard : 128 * (shard + 1)] = wu[:, at : at + 128]
+    small_in[here.member] = small[...]
+    x_all[here.member] = tok[...]
+    wqkv[here.shard, pl.ds(pl.multiple_of(32 * here.member, 32), 32)] = wqkv_send[here.member]
+    wu_in[here.member] = wu_send[here.member]
+
+    @pl.when(out_stays)
+    def _():
+        pl.semaphore_wait(barrier, len(partners))
+        wo_in[...] = wo[...]
+
+    @pl.when(jnp.logical_not(out_stays))
+    def _():
+        pl.semaphore_wait(barrier, len(partners) + 1)
+
+    wo_copy = pltpu.make_async_remote_copy(
+        src_ref=wo, dst_ref=wo_in, send_sem=self_sems.at[0], recv_sem=self_sems.at[1],
+        device_id=here.place(*out_to), device_id_type=MESH_ID,
+    )
+    small_sent, wqkv_sent, wu_sent = [], [], []
+    for member, place in here.mates():
+        small_sent.append(
+            (post.send(small_in.at[here.member], small_in.at[here.member], place), small_in.at[member])
+        )
+    for member, place in here.mates():
+        mine = wqkv.at[here.shard, pl.ds(pl.multiple_of(32 * here.member, 32), 32)]
+        theirs = wqkv.at[here.shard, pl.ds(pl.multiple_of(32 * member, 32), 32)]
+        wqkv_sent.append((post.send(wqkv_send.at[member], mine, place), theirs))
+    pl.when(jnp.logical_not(out_stays))(wo_copy.start)
+    x_over = post.send(x_all.at[here.member], x_all.at[here.member], here.link_mate)
+    x_near = post.send(x_all.at[here.member], x_all.at[here.member], here.core_mate)
+    for member, place in here.mates():
+        wu_sent.append(
+            (post.send(wu_send.at[member], wu_in.at[here.member], place), wu_in.at[member])
+        )
+
+    for sent, landing in small_sent:
+        post.arrived(sent, landing)
+    small_all[here.shard, 0:8] = (
+        small_in[0, 0:8] + small_in[1, 0:8] + small_in[2, 0:8] + small_in[3, 0:8]
+    )
+    for member in range(GROUP):
+        small_all[here.shard, 8 + member : 9 + member] = small_in[member, 8:9]
+    plane_sent = []
+    for step in range(1, SPOTS):
+        _, place = here.plane(step)
+        came = lax.rem(here.shard + SPOTS - step, SPOTS)
+        mine = small_all.at[here.shard]
+        plane_sent.append((post.send(mine, mine, place), small_all.at[came]))
+
+    for sent, landing in wqkv_sent:
+        post.arrived(sent, landing)
+    qkv_ring = RingGather(here, post, wqkv, wqkv.at[here.shard])
+    qkv_ring.hop()
+
+    @pl.when(jnp.logical_not(out_stays))
+    def _():
+        wo_copy.wait_recv()
+        wo_copy.wait_send()
+
+    out_ring = RingGather(here, post, wo_all, wo_in)
+    local.copy(wo_in, wo_all.at[here.shard])
+    out_ring.hop()
+    post.arrived(x_over, x_all.at[here.link_member])
+    x_pass = post.send(
+        x_all.at[here.link_member], x_all.at[here.link_member], here.core_mate
+    )
+    qkv_ring.hop()
+    out_ring.hop()
+    post.arrived(x_near, x_all.at[here.core_member])
+    post.arrived(x_pass, x_all.at[here.far_member])
+    for sent, landing in plane_sent:
+        post.arrived(sent, landing)
+    for shard in range(SPOTS):
+        vectors[:, 128 * shard : 128 * (shard + 1)] = small_all[shard, 0:8]
+    qkv_ring.hop()
+    out_ring.hop()
+
+    gain, bias = vectors[0:1], vectors[1:2]
+    for member in range(GROUP):
+        normed, _ = norm_parts(x_all[member].astype(F32))
+        a_t[:, 128 * member : 128 * (member + 1)] = (normed * gain + bias).astype(BF).T
+
+    segs = jnp.concatenate([small_all[4 * here.x + z, 8:12] for z in range(4)], 0)
+    start = jnp.zeros_like(segs)
+    for doc in range(1, 8):
+        size = jnp.sum(
+            jnp.sum((segs == doc - 1.0).astype(F32), 1, keepdims=True), 0, keepdims=True
+        )
+        start = start + jnp.where(segs >= doc, size, 0.0)
+    starts[...] = start
+    lane = lax.broadcasted_iota(jnp.int32, (1, ROWS), 1)
+    rots = []
+    for member in range(GROUP):
+        at = 4 * here.z + member
+        position = jnp.where(lane < 64, 64 * at + lane, 64 * (31 - at) + lane - 64)
+        rots.append(position.astype(F32) - starts[pl.ds(at, 1)])
+    cos_t, sin_t = turn_tables(jnp.concatenate(rots, 1))
+
+    qkv_ring.finish()
+    wqkv_flat = wqkv[...].reshape(WIDTH, 768)
+    for part in range(3):
+        product = dot(wqkv_flat[:, 256 * part : 256 * (part + 1)], a_t[...], 0, 0)
+        for head in range(4):
+            rows = product[HD * head : HD * (head + 1)]
+            if part < 2:
+                first, second = rows[: HD // 2], rows[HD // 2 :]
+                rows = jnp.concatenate(
+                    [first * cos_t - second * sin_t, second * cos_t + first * sin_t], 0
+                )
+            qkv_send[head, HD * part : HD * (part + 1)] = rows.astype(BF)
+    swapped = swap_along_z(here, post, local, qkv_send, qkv_heads)
+    local.copy(wqkv, wqkv_out)
+    for sent, landing in wu_sent:
+        post.arrived(sent, landing)
+    local.copy(wu_in, wu_shard)
+    out_ring.finish()
+    for sent, landing in swapped:
+        post.arrived(sent, landing)
+    local.finish()
+    post.finish()
+
+
+def call_first(tok, small, wq, wk, wv, wo, wu):
+    vmem = pl.BlockSpec(memory_space=pltpu.VMEM)
+    anywhere = pl.BlockSpec(memory_space=pl.ANY)
+    shape = jax.ShapeDtypeStruct
+    return pl.pallas_call(
+        first_kernel,
+        out_shape=[
+            shape((4, 192, 512), BF),
+            shape((WIDTH, 512), BF),
+            shape((SPOTS, ROWS, 768), BF),
+            shape((SPOTS, 32, WIDTH), BF),
+            shape((GROUP, 32, WIDTH), BF),
+            shape((8, WIDTH), F32),
+            shape((16, ROWS), F32),
+        ],
+        in_specs=[vmem] * 7,
+        out_specs=[anywhere, vmem, anywhere, anywhere, anywhere, vmem, vmem],
+        scratch_shapes=[
+            pltpu.VMEM((GROUP, ROWS, WIDTH), BF),
+            pltpu.VMEM((SPOTS, ROWS, 768), BF),
+            pltpu.VMEM((GROUP, 32, 768), BF),
+            pltpu.VMEM((GROUP, 32, WIDTH), BF),
+            pltpu.VMEM((GROUP, 32, WIDTH), BF),
+            pltpu.VMEM((GROUP, 16, ROWS), F32),
+            pltpu.VMEM((SPOTS, 16, ROWS), F32),
+            pltpu.VMEM((4, 192, 512), BF),
+            pltpu.VMEM((32, WIDTH), BF),
+            pltpu.SemaphoreType.DMA((64,)),
+            pltpu.SemaphoreType.DMA((64,)),
+            pltpu.SemaphoreType.DMA((8,)),
+            pltpu.SemaphoreType.DMA((2,)),
+        ],
+        compiler_params=pltpu.CompilerParams(
+            collective_id=0, has_side_effects=True, vmem_limit_bytes=VMEM_BYTES
+        ),
+        name="gather_and_project",
+    )(tok, small, wq, wk, wv, wo, wu)
+
+
+def true_group(ref, group):
+    def chunk(at, late):
+        tile = ref[at // 4, :, 128 * (at % 4) : 128 * (at % 4) + 128]
+        return tile[:, 64:] if late else tile[:, :64]
+
+    if group < 8:
+        return jnp.concatenate([chunk(2 * group, False), chunk(2 * group + 1, False)], 1)
+    return jnp.concatenate([chunk(31 - 2 * group, True), chunk(30 - 2 * group, True)], 1)
+
+
+def stored_group(ref, at):
+    def block(number):
+        tile = ref[:, 128 * (number // 2) : 128 * (number // 2) + 128]
+        return tile[:, 64:] if number % 2 else tile[:, :64]
+
+    return jnp.concatenate([block(at), block(31 - at)], 1)
+
+
+STEP = 256
+
+
+def allowed_pairs(query_block, key_block, start):
+    key_pos = STEP * key_block + lax.broadcasted_iota(jnp.int32, (STEP, STEP), 0)
+    query_pos = STEP * query_block + lax.broadcasted_iota(jnp.int32, (STEP, STEP), 1)
+    return (key_pos <= query_pos) & (key_pos >= start)
+
+
+def attend_kernel(low, qkv_heads, start, o_heads, o_true, lse, qkv):
+    for group in range(16):
+        qkv[:, 128 * group : 128 * group + 128] = true_group(qkv_heads, group)
+    for block in range(8):
+        here = slice(STEP * block, STEP * (block + 1))
+        query = qkv[0:HD, here]
+        first = start[:, here]
+
+        def visit(key_block, state, block=block, query=query, first=first):
+            top, total, weighted = state
+            keys = pl.ds(pl.multiple_of(key_block * STEP, STEP), STEP)
+            scores = dot(qkv[HD : 2 * HD, keys], query, 0, 0) * HD**-0.5
+            allowed = allowed_pairs(block, key_block, first)
+            scores = jnp.where(allowed, scores, masked_value)
+            top_new = jnp.maximum(top, jnp.max(scores, 0, keepdims=True))
+            fade = jnp.exp(top - top_new)
+            probs = jnp.where(allowed, jnp.exp(scores - top_new), 0.0)
+            total = total * fade + jnp.sum(probs, 0, keepdims=True)
+            weighted = weighted * fade + dot(qkv[2 * HD :, keys], probs.astype(BF), 1, 0)
+            return top_new, total, weighted
+
+        top, total, weighted = lax.fori_loop(
+            low[block],
+            block + 1,
+            visit,
+            (
+                jnp.full((1, STEP), masked_value, F32),
+                jnp.zeros((1, STEP), F32),
+                jnp.zeros((HD, STEP), F32),
+            ),
+        )
+        o_true[:, here] = weighted / total
+        lse[:, here] = top + jnp.log(total)
+    for at in range(16):
+        o_heads[at // 4, :, 128 * (at % 4) : 128 * (at % 4) + 128] = stored_group(o_true, at).astype(BF)
+
+
+def call_attend(low, qkv_heads, start):
+    vmem = pl.BlockSpec(memory_space=pltpu.VMEM)
+    shape = jax.ShapeDtypeStruct
+    return pl.pallas_call(
+        attend_kernel,
+        out_shape=[
+            shape((4, HD, 512), BF),
+            shape((HD, 2048), F32),
+            shape((1, 2048), F32),
+            shape((192, 2048), BF),
+        ],
+        in_specs=[pl.BlockSpec(memory_space=pltpu.SMEM), vmem, vmem],
+        out_specs=[vmem] * 4,
+        compiler_params=pltpu.CompilerParams(vmem_limit_bytes=VMEM_BYTES),
+        name="attend",
+    )(low, qkv_heads, start)
+
+
+def attend_back_kernel(low, qkv, o_true, lse, start, do_heads, out, d_out, delta, grads):
+    for group in range(16):
+        d_out[:, 128 * group : 128 * group + 128] = true_group(do_heads, group)
+    delta[...] = jnp.sum(d_out[...].astype(F32) * o_true[...], 0, keepdims=True)
+    grads[...] = jnp.zeros_like(grads)
+    for block in range(8):
+        here = slice(STEP * block, STEP * (block + 1))
+        query, d_attn = qkv[0:HD, here], d_out[:, here]
+        first, norm, less = start[:, here], lse[:, here], delta[:, here]
+
+        def visit(
+            key_block, d_query, block=block, query=query, d_attn=d_attn, first=first, norm=norm, less=less
+        ):
+            keys = pl.ds(pl.multiple_of(key_block * STEP, STEP), STEP)
+            key = qkv[HD : 2 * HD, keys]
+            scores = dot(key, query, 0, 0) * HD**-0.5
+            probs = jnp.where(allowed_pairs(block, key_block, first), jnp.exp(scores - norm), 0.0)
+            d_probs = dot(qkv[2 * HD :, keys], d_attn, 0, 0)
+            d_scores = (probs * (d_probs - less)).astype(BF)
+            grads[HD : 2 * HD, keys] += dot(query, d_scores, 1, 1)
+            grads[2 * HD :, keys] += dot(d_attn, probs.astype(BF), 1, 1)
+            return d_query + dot(key, d_scores, 1, 0)
+
+        grads[0:HD, here] = lax.fori_loop(
+            low[block], block + 1, visit, jnp.zeros((HD, STEP), F32)
+        )
+    position = lax.broadcasted_iota(jnp.int32, (1, 2048), 1).astype(F32)
+    cos_t, sin_t = turn_tables(position - start[...])
+    for part in range(2):
+        first = grads[HD * part : HD * part + HD // 2] * HD**-0.5
+        second = grads[HD * part + HD // 2 : HD * (part + 1)] * HD**-0.5
+        grads[HD * part : HD * part + HD // 2] = first * cos_t + second * sin_t
+        grads[HD * part + HD // 2 : HD * (part + 1)] = second * cos_t - first * sin_t
+    for at in range(16):
+        out[at // 4, :, 128 * (at % 4) : 128 * (at % 4) + 128] = stored_group(grads, at).astype(BF)
+
+
+def call_attend_back(low, qkv, o_true, lse, start, do_heads):
+    vmem = pl.BlockSpec(memory_space=pltpu.VMEM)
+    return pl.pallas_call(
+        attend_back_kernel,
+        out_shape=jax.ShapeDtypeStruct((4, 192, 512), BF),
+        in_specs=[pl.BlockSpec(memory_space=pltpu.SMEM)] + [vmem] * 5,
+        out_specs=vmem,
+        scratch_shapes=[
+            pltpu.VMEM((HD, 2048), BF),
+            pltpu.VMEM((1, 2048), F32),
+            pltpu.VMEM((192, 2048), F32),
+        ],
+        compiler_params=pltpu.CompilerParams(vmem_limit_bytes=VMEM_BYTES),
+        name="attend_back",
+    )(low, qkv, o_true, lse, start, do_heads)
+
+
+GELU_K = math.sqrt(2.0 / math.pi)
+
+
+def gelu_and_slope(pre):
+    square = pre * pre
+    bend = jnp.tanh(GELU_K * pre * (1.0 + 0.044715 * square))
+    half = 0.5 * (1.0 + bend)
+    slope = half + 0.5 * pre * (1.0 - bend * bend) * GELU_K * (1.0 + 3 * 0.044715 * square)
+    return pre * half, slope
+
+
+def middle_kernel(
+    o_heads, tok, cot, wo_all, wu_own, wd_own, vectors,
+    act, d_res, do_heads, g_down, g_up, g_out, d_vec,
+    o_all, wu_all, wd_all, c_all, dm_all, dt_all, gl_all, slope_all, du_all, do_send,
+    near_send, near_in, far_send, far_in, down_parts, down_in, res,
+    send_sems, recv_sems, local_sems,
+):
+    here = Here()
+    post = Post(send_sems, recv_sems)
+    local = Local(local_sems)
+    greet([place for _, place in here.mates()] + [here.right, here.left]
+          + [here.along_z(step)[1] for step in (1, 2, 3)])
+    swapped = swap_along_z(here, post, local, o_heads, o_all)
+    up_ring = RingGather(here, post, wu_all, wu_own)
+    down_ring = RingGather(here, post, wd_all, wd_own)
+    local.copy(wu_own, wu_all.at[here.shard])
+    local.copy(wd_own, wd_all.at[here.shard])
+    up_ring.hop()
+    sums = [
+        GroupSum(here, post, near_send.at[n], near_in.at[n], far_send.at[n], far_in.at[n])
+        for n in range(3)
+    ]
+    for sent, landing in swapped:
+        post.arrived(sent, landing)
+    local.finish()
+
+    o_flat = o_all[...].reshape(256, 512)
+    wo_flat = wo_all[...].reshape(256, WIDTH)
+
+    def token_rows(member):
+        return pl.ds(pl.multiple_of(ROWS * member, ROWS), ROWS)
+
+    def out_term(member):
+        heads = [o_all[z, :, token_rows(member)] for z in range(4)]
+        return dot(jnp.concatenate(heads, 0), wo_flat, 0, 0)
+
+    sums[0].start(out_term)
+    up_ring.hop()
+    down_ring.hop()
+    branch = sums[0].total()
+    t_normed, t_inv = norm_parts(branch)
+    hres = tok[...].astype(F32) + t_normed * vectors[2:3] + vectors[3:4]
+    res[0] = t_normed
+    h_normed, h_inv = norm_parts(hres)
+    res[1] = h_normed
+    res[2] = hres
+    c_all[here.member] = (h_normed * vectors[4:5] + vectors[5:6]).astype(BF)
+    group_gather(here, post, c_all)
+    up_ring.finish()
+    down_ring.hop()
+    wu_flat = wu_all[...].reshape(WIDTH, WIDTH)
+    for member in range(GROUP):
+        gl, slope = gelu_and_slope(dot(c_all[member], wu_flat, 1, 0))
+        gl_all[member] = gl.astype(BF)
+        slope_all[member] = slope
+    down_ring.finish()
+    wd_flat = wd_all[...].reshape(WIDTH, WIDTH)
+    sums[1].start(lambda member: dot(gl_all[member], wd_flat, 1, 0))
+    branch = sums[1].total()
+    m_normed, m_inv = norm_parts(branch)
+    act[...] = (res[2] + m_normed * vectors[6:7] + vectors[7:8]).astype(BF)
+    upstream = cot[...].astype(F32)
+    dm_all[here.member] = norm_pull(m_normed, m_inv, vectors[6:7], upstream).astype(BF)
+    d_vec[0:2] = jnp.zeros((2, WIDTH), F32)
+    d_vec[6:7] = jnp.sum(upstream * m_normed, 0, keepdims=True)
+    d_vec[7:8] = jnp.sum(upstream, 0, keepdims=True)
+    group_gather(here, post, dm_all)
+    for member in range(GROUP):
+        du_all[member] = (dot(dm_all[member], wd_flat, 1, 1) * slope_all[member]).astype(BF)
+    sums[2].start(lambda member: dot(du_all[member], wu_flat, 1, 1))
+    gl_flat = gl_all[...].reshape(512, WIDTH)
+    dm_flat = dm_all[...].reshape(512, WIDTH)
+    for shard in range(SPOTS):
+        down_parts[shard] = dot(gl_flat[:, ROWS * shard : ROWS * (shard + 1)], dm_flat, 0, 0).astype(BF)
+    down_sum = RingSum(here, post, down_parts, down_in)
+    down_sum.hop()
+    du_flat = du_all[...].reshape(512, WIDTH)
+    c_flat = c_all[...].reshape(512, WIDTH)
+    for shard in range(SPOTS):
+        g_up[shard] = dot(c_flat[:, ROWS * shard : ROWS * (shard + 1)], du_flat, 0, 0).astype(BF)
+    d_c = sums[2].total()
+    h_normed = res[1]
+    d_h = upstream + norm_pull(h_normed, h_inv, vectors[4:5], d_c)
+    d_vec[4:5] = jnp.sum(d_c * h_normed, 0, keepdims=True)
+    d_vec[5:6] = jnp.sum(d_c, 0, keepdims=True)
+    t_normed = res[0]
+    dt_all[here.member] = norm_pull(t_normed, t_inv, vectors[2:3], d_h).astype(BF)
+    d_vec[2:3] = jnp.sum(d_h * t_normed, 0, keepdims=True)
+    d_vec[3:4] = jnp.sum(d_h, 0, keepdims=True)
+    d_res[...] = d_h
+    down_sum.hop()
+    group_gather(here, post, dt_all)
+    dt_flat = dt_all[...].reshape(512, WIDTH)
+    d_o = dot(wo_flat, dt_flat, 1, 1)
+    for head in range(4):
+        do_send[head] = d_o[HD * head : HD * (head + 1)].astype(BF)
+    late_local = Local(local_sems)
+    swapped = swap_along_z(here, post, late_local, do_send, do_heads)
+    down_sum.hop()
+    g_out[...] = dot(o_flat, dt_flat, 1, 0).astype(BF).reshape(SPOTS, 32, WIDTH)
+    down_sum.hop()
+    low_half, high_half = down_sum.total()
+    g_down[0:64] = low_half
+    g_down[64:128] = high_half
+    for sent, landing in swapped:
+        post.arrived(sent, landing)
+    late_local.finish()
+    post.finish()
+
+
+def call_middle(o_heads, tok, cot, wo_all, wu_own, wd_own, vectors):
+    vmem = pl.BlockSpec(memory_space=pltpu.VMEM)
+    anywhere = pl.BlockSpec(memory_space=pl.ANY)
+    shape = jax.ShapeDtypeStruct
+    dma = pltpu.SemaphoreType.DMA
+    return pl.pallas_call(
+        middle_kernel,
+        out_shape=[
+            shape((ROWS, WIDTH), BF),
+            shape((ROWS, WIDTH), F32),
+            shape((4, HD, 512), BF),
+            shape((ROWS, WIDTH), F32),
+            shape((SPOTS, ROWS, WIDTH), BF),
+            shape((SPOTS, 32, WIDTH), BF),
+            shape((8, WIDTH), F32),
+        ],
+        in_specs=[vmem] * 7,
+        out_specs=[vmem, vmem, anywhere, vmem, vmem, vmem, vmem],
+        scratch_shapes=[
+            pltpu.VMEM((4, HD, 512), BF),
+            pltpu.VMEM((SPOTS, ROWS, WIDTH), BF),
+            pltpu.VMEM((SPOTS, ROWS, WIDTH), BF),
+            pltpu.VMEM((GROUP, ROWS, WIDTH), BF),
+            pltpu.VMEM((GROUP, ROWS, WIDTH), BF),
+            pltpu.VMEM((GROUP, ROWS, WIDTH), BF),
+            pltpu.VMEM((GROUP, ROWS, WIDTH), BF),
+            pltpu.VMEM((GROUP, ROWS, WIDTH), F32),
+            pltpu.VMEM((GROUP, ROWS, WIDTH), BF),
+            pltpu.VMEM((4, HD, 512), BF),
+            pltpu.VMEM((3, 2, ROWS, WIDTH), BF),
+            pltpu.VMEM((3, 2, ROWS, WIDTH), BF),
+            pltpu.VMEM((3, ROWS, WIDTH), BF),
+            pltpu.VMEM((3, ROWS, WIDTH), BF),
+            pltpu.VMEM((SPOTS, ROWS, WIDTH), BF),
+            pltpu.VMEM((14, ROWS // 2, WIDTH), BF),
+            pltpu.VMEM((3, ROWS, WIDTH), F32),
+            dma((80,)),
+            dma((80,)),
+            dma((8,)),
+        ],
+        compiler_params=pltpu.CompilerParams(
+            collective_id=1, has_side_effects=True, vmem_limit_bytes=VMEM_BYTES
+        ),
+        name="feed_forward",
+    )(o_heads, tok, cot, wo_all, wu_own, wd_own, vectors)
+
+
+def last_kernel(
+    d_heads, a_t, wqkv, up_parts, out_parts, d_res, tok, vectors, d_vec,
+    in_grad, g_q, g_k, g_v, g_out, g_up, g_vec,
+    d_in, d_all, qkv_parts, up_in, out_in, qkv_in, near_send, near_in, far_send, far_in,
+    vec_send, vec_in, vec_group, up_send, up_got, qkv_end, qkv_got, out_end, out_got,
+    send_sems, recv_sems, local_sems, self_sems,
+):
+    here = Here()
+    post = Post(send_sems, recv_sems)
+    local = Local(local_sems)
+    out_to, out_from = out_rows_source(here), out_rows_target(here)
+    out_stays = same_place(here, out_to)
+    barrier = pltpu.get_barrier_semaphore()
+    partners = [place for _, place in here.mates()] + [here.plane(n)[1] for n in range(1, SPOTS)]
+    for place in partners:
+        pl.semaphore_signal(barrier, inc=1, device_id=place, device_id_type=MESH_ID)
+    pl.when(jnp.logical_not(out_stays))(
+        lambda: pl.semaphore_signal(
+            barrier, inc=1, device_id=here.place(*out_from), device_id_type=MESH_ID
+        )
+    )
+
+    @pl.when(out_stays)
+    def _():
+        pl.semaphore_wait(barrier, len(partners))
+
+    @pl.when(jnp.logical_not(out_stays))
+    def _():
+        pl.semaphore_wait(barrier, len(partners) + 1)
+
+    swapped = swap_along_z(here, post, local, d_heads, d_in)
+    up_sum = RingSum(here, post, up_parts, up_in)
+    out_sum = RingSum(here, post, out_parts, out_in)
+    qkv_sum = RingSum(here, post, qkv_parts, qkv_in)
+    up_sum.hop()
+    out_sum.hop()
+    for sent, landing in swapped:
+        post.arrived(sent, landing)
+    local.finish()
+    for part in range(3):
+        for head in range(4):
+            at = 256 * part + HD * head
+            d_all[at : at + HD] = d_in[head, HD * part : HD * (part + 1)]
+    wqkv_flat = wqkv[...].reshape(WIDTH, 768)
+
+    def in_term(member):
+        rows = pl.ds(pl.multiple_of(ROWS * member, ROWS), ROWS)
+        return dot(d_all[:, rows], wqkv_flat, 0, 1)
+
+    in_sum = GroupSum(here, post, near_send, near_in, far_send, far_in)
+    in_sum.start(in_term)
+    up_sum.hop()
+    for shard in range(SPOTS):
+        qkv_parts[shard] = dot(a_t[ROWS * shard : ROWS * (shard + 1)], d_all[...], 1, 1).astype(BF)
+    qkv_sum.hop()
+    out_sum.hop()
+    d_a = in_sum.total()
+    normed, inv_std = norm_parts(tok[...].astype(F32))
+    in_grad[...] = d_res[...] + norm_pull(normed, inv_std, vectors[0:1], d_a)
+    row = lax.broadcasted_iota(jnp.int32, (8, WIDTH), 0)
+    terms = jnp.where(
+        row == 0,
+        jnp.sum(d_a * normed, 0, keepdims=True),
+        jnp.where(row == 1, jnp.sum(d_a, 0, keepdims=True), d_vec[...]),
+    )
+    for shard in range(SPOTS):
+        vec_send[shard] = terms[:, ROWS * shard : ROWS * (shard + 1)]
+    vec_in[here.shard] = vec_send[here.shard]
+    vec_sent = []
+    for step in range(1, SPOTS):
+        shard, place = here.plane(step)
+        came = lax.rem(here.shard + SPOTS - step, SPOTS)
+        vec_sent.append((post.send(vec_send.at[shard], vec_in.at[here.shard], place), vec_in.at[came]))
+    up_sum.hop()
+    qkv_sum.hop()
+    out_sum.hop()
+    for sent, landing in vec_sent:
+        post.arrived(sent, landing)
+    total = vec_in[0]
+    for shard in range(1, SPOTS):
+        total = total + vec_in[shard]
+    vec_group[here.member] = total
+    vec_sent = []
+    for member, place in here.mates():
+        mine = vec_group.at[here.member]
+        vec_sent.append((post.send(mine, mine, place), vec_group.at[member]))
+    up_sum.hop()
+    qkv_sum.hop()
+    out_sum.hop()
+
+    low_half, high_half = up_sum.total()
+    for member in range(GROUP):
+        half = low_half if member < 2 else high_half
+        up_send[member] = half[32 * (member % 2) : 32 * (member % 2) + 32].astype(BF)
+    up_got[here.member] = up_send[here.member]
+    ends = []
+    for member, place in here.mates():
+        ends.append((post.send(up_send.at[member], up_got.at[here.member], place), up_got.at[member]))
+    qkv_sum.hop()
+    low_half, high_half = out_sum.total()
+    out_end[0:16] = low_half.astype(BF)
+    out_end[16:32] = high_half.astype(BF)
+    out_copy = pltpu.make_async_remote_copy(
+        src_ref=out_end, dst_ref=out_got, send_sem=self_sems.at[0], recv_sem=self_sems.at[1],
+        device_id=here.place(*out_to), device_id_type=MESH_ID,
+    )
+
+    @pl.when(out_stays)
+    def _():
+        out_got[...] = out_end[...]
+
+    pl.when(jnp.logical_not(out_stays))(out_copy.start)
+    low_half, high_half = qkv_sum.total()
+    for member in range(GROUP):
+        half = low_half if member < 2 else high_half
+        qkv_end[member] = half[32 * (member % 2) : 32 * (member % 2) + 32].astype(BF)
+    qkv_got[here.member] = qkv_end[here.member]
+    for member, place in here.mates():
+        ends.append((post.send(qkv_end.at[member], qkv_got.at[here.member], place), qkv_got.at[member]))
+    for sent, landing in vec_sent:
+        post.arrived(sent, landing)
+    g_vec[...] = vec_group[0] + vec_group[1] + vec_group[2] + vec_group[3]
+
+    for sent, landing in ends[:3]:
+        post.arrived(sent, landing)
+    for member in range(GROUP):
+        for shard in range(SPOTS):
+            at = 512 * shard + 128 * member
+            g_up[:, at : at + 128] = up_got[member, :, 128 * shard : 128 * (shard + 1)].astype(F32)
+
+    @pl.when(jnp.logical_not(out_stays))
+    def _():
+        out_copy.wait_recv()
+        out_copy.wait_send()
+
+    g_out[...] = out_got[...].astype(F32)
+    for sent, landing in ends[3:]:
+        post.arrived(sent, landing)
+    for member in range(GROUP):
+        base = 512 * (member % 2) + 256 * (member // 2)
+        for slot, out in enumerate((g_q, g_k, g_v)):
+            out[:, base : base + 256] = qkv_got[member, :, 256 * slot : 256 * (slot + 1)].astype(F32)
+    post.finish()
+
+
+def call_last(d_heads, a_t, wqkv, up_parts, out_parts, d_res, tok, vectors, d_vec):
+    vmem = pl.BlockSpec(memory_space=pltpu.VMEM)
+    shape = jax.ShapeDtypeStruct
+    dma = pltpu.SemaphoreType.DMA
+    return pl.pallas_call(
+        last_kernel,
+        out_shape=[
+            shape((ROWS, WIDTH), F32),
+            shape((32, WIDTH), F32),
+            shape((32, WIDTH), F32),
+            shape((32, WIDTH), F32),
+            shape((32, WIDTH), F32),
+            shape((32, 4 * WIDTH), F32),
+            shape((8, ROWS), F32),
+        ],
+        in_specs=[vmem] * 9,
+        out_specs=[vmem] * 7,
+        scratch_shapes=[
+            pltpu.VMEM((4, 192, 512), BF),
+            pltpu.VMEM((768, 512), BF),
+            pltpu.VMEM((SPOTS, ROWS, 768), BF),
+            pltpu.VMEM((14, ROWS // 2, WIDTH), BF),
+            pltpu.VMEM((14, 16, WIDTH), BF),
+            pltpu.VMEM((14, ROWS // 2, 768), BF),
+            pltpu.VMEM((2, ROWS, WIDTH), BF),
+            pltpu.VMEM((2, ROWS, WIDTH), BF),
+            pltpu.VMEM((ROWS, WIDTH), BF),
+            pltpu.VMEM((ROWS, WIDTH), BF),
+            pltpu.VMEM((SPOTS, 8, ROWS), F32),
+            pltpu.VMEM((SPOTS, 8, ROWS), F32),
+            pltpu.VMEM((GROUP, 8, ROWS), F32),
+            pltpu.VMEM((GROUP, 32, WIDTH), BF),
+            pltpu.VMEM((GROUP, 32, WIDTH), BF),
+            pltpu.VMEM((GROUP, 32, 768), BF),
+            pltpu.VMEM((GROUP, 32, 768), BF),
+            pltpu.VMEM((32, WIDTH), BF),
+            pltpu.VMEM((32, WIDTH), BF),
+            dma((80,)),
+            dma((80,)),
+            dma((8,)),
+            dma((2,)),
+        ],
+        compiler_params=pltpu.CompilerParams(
+            collective_id=2, has_side_effects=True, vmem_limit_bytes=VMEM_BYTES
+        ),
+        name="gradients",
+    )(d_heads, a_t, wqkv, up_parts, out_parts, d_res, tok, vectors, d_vec)
+
+
+def on_device_grouped(
+    tokens, segments, cotangent, w_query, w_key, w_value, w_out, w_up, w_down,
+    gain_attn_in, bias_attn_in, gain_attn_out, bias_attn_out,
+    gain_mlp_in, bias_mlp_in, gain_mlp_out, bias_mlp_out,
+):
+    member = lax.axis_index("ctx") % GROUP
+    norms = jnp.stack([
+        gain_attn_in, bias_attn_in, gain_attn_out, bias_attn_out,
+        gain_mlp_in, bias_mlp_in, gain_mlp_out, bias_mlp_out,
+    ]).astype(F32)
+    lane_member = jnp.arange(ROWS, dtype=jnp.int32)[None] // 32
+    spread = jnp.where(lane_member == member, jnp.tile(norms, (1, GROUP)), 0.0)
+    small = jnp.concatenate([spread, segments.astype(F32), jnp.zeros((7, ROWS), F32)], 0)
+    tok, cot = tokens[0], cotangent[0]
+    qkv_heads, a_t, wqkv, wo_all, wu_own, vectors, starts = call_first(
+        tok, small, w_query, w_key, w_value, w_out, w_up
+    )
+    halves = starts.reshape(16, 2, 64)
+    start = jnp.concatenate([halves[:, 0], halves[::-1, 1]], 0).reshape(1, 2048)
+    low = (start[0, ::STEP] * (1.0 / STEP)).astype(jnp.int32)
+    o_heads, o_true, lse, qkv = call_attend(low, qkv_heads, start)
+    act, d_res, do_heads, g_down, up_parts, out_parts, d_vec = call_middle(
+        o_heads, tok, cot, wo_all, wu_own.reshape(ROWS, WIDTH), w_down, vectors
+    )
+    d_heads = call_attend_back(low, qkv, o_true, lse, start, do_heads)
+    in_grad, g_q, g_k, g_v, g_out, g_up, g_vec = call_last(
+        d_heads, a_t, wqkv, up_parts, out_parts, d_res, tok, vectors, d_vec
+    )
+    g_vec = lax.dynamic_slice_in_dim(g_vec, member * 32, 32, 1)
+    return (act[None], in_grad[None], g_q, g_k, g_v, g_out, g_up, g_down) + tuple(
+        g_vec[row] for row in range(8)
+    )
+
+
 def solution(mesh):
     in_specs = (
         P("dp", "ctx", None),
@@ -404,6 +1414,7 @@
         P(("dp", "ctx")),
         P(("dp", "ctx")),
     )
+    grouped = mesh.shape["dp"] == 2 and mesh.shape["ctx"] == 16
     return jax.shard_map(
-        on_device, mesh=mesh, in_specs=in_specs, out_specs=out_specs, check_vma=False
-    )
+        on_device_grouped if grouped else on_device, mesh=mesh, in_specs=in_specs, out_specs=out_specs, check_vma=False
+    )

time: 1560 us -> 288 us (0.18)
  waiting for transfers between devices: 1140 us -> 0 us
  Pallas kernels: 0 us -> 272 us
  matrix products: 149 us -> 0 us
  blocking collectives: 143 us -> 0 us
  local copies, waits for them, and re-layouts: 82.2 us -> 12 us
    reduce_scatter x6 -> x0, waiting for transfers between devices: 780 us -> none  [the longest x1 187 us: on_device(): lax.psum_scatter(grad_up, ('dp', 'ctx'), scatter_dimension=0, tiled=True)]
    all_gather x10 -> x0, waiting for transfers between devices: 356 us -> none  [the longest x1 76.4 us: on_device(): lax.all_gather(w_up, ('dp', 'ctx'), axis=0, tiled=True)]
    pallas_call x0 -> x5, Pallas kernels: none -> 272 us  [the longest x1 123 us: call_middle(): pl.pallas_call(middle_kernel, out_shape=[shape((ROWS, WIDTH), BF), shape(...]
    dot_general x32 -> x0, matrix products: 149 us -> none  [the longest x6 28.8 us: score_block(): jnp.einsum('qhd,khd->hqk', queries, keys, preferred_element_type=jnp.floa...]
    unnamed x2 -> x0, blocking collectives: 82.2 us -> none
    all_gather x3 -> x0, blocking collectives: 60.7 us -> none  [the longest x1 21.1 us: on_device(): seg_all = lax.all_gather(segments, 'ctx', axis=1, tiled=True)[0]]
    dynamic_slice x22 -> x1, local copies, waits for them, and re-layouts: 36.5 us -> 0.86 us  [on_device_grouped(): g_vec = lax.dynamic_slice_in_dim(g_vec, member * 32, 32, 1)]
    unnamed x162 -> x20, local copies, waits for them, and re-layouts: 33.7 us -> 8.64 us
  transfers between devices with their start and end apart: 16 -> 0, of which waited for: 13 -> 0; matrix products, arithmetic and copies ran while one was open for 15% -> 0% of each run, Pallas kernels for 0% -> 0%
where the time goes in v1:
time: 288 us; the launch traced here: 286 us
  Pallas kernels  272 us (94%)
  local copies, waits for them, and re-layouts  12 us (4%)
    pallas_call x1, Pallas kernels, call_middle(): pl.pallas_call(middle_kernel, out_shape=[shape((ROWS, WIDTH), BF), shape(...  123 us
    pallas_call x1, Pallas kernels, call_last(): pl.pallas_call(last_kernel, out_shape=[shape((ROWS, WIDTH), F32), shape((...  75 us
    pallas_call x1, Pallas kernels, call_first(): pl.pallas_call(first_kernel, out_shape=[shape((4, 192, 512), BF), shape((...  50.9 us
    pallas_call x1, Pallas kernels, call_attend_back(): pl.pallas_call(attend_back_kernel, out_shape=jax.ShapeDtypeStruct((4, 192...  12.5 us
    pallas_call x1, Pallas kernels, call_attend(): pl.pallas_call(attend_kernel, out_shape=[shape((4, HD, 512), BF), shape((...  10.9 us
    unnamed x20, local copies, waits for them, and re-layouts  8.64 us

profile of v1, /device:TPU:0, one launch (start us, length us, event | category | flops | bytes accessed | tf_op | source)
XLA Modules:
  0.0 286.5 jit_solution(12382077102578214046)
XLA Ops:
  0.7 0.7 convert_element_type.16
  1.3 0.1 pad.4.clone
  1.4 0.8 stack.35
  2.2 0.1 tile.10
  2.3 0.7 maximum_maximum_fusion.small
  3.0 50.9 %gather_and_project.1 = (bf16[4,192,512]{2,1,0:T(8,128)(2,1)}, bf16[1024,512]{1,0:T(8,128)(2,1)}, bf16[8,128,768]{2,1,0:T(8,128)(2,1)}, bf16[8,32,1024]{2,1,0:T(...) custom-call(bf16[128,1024]{1,0:T(8,128)(2,1)} %bitcast.36, ...), custom_call_target="tpu_custom_call" | custom-call | tf_op jit(solution)/shard_map/gather_and_project/pallas_call | solution.py:812
  53.9 0.8 reshape.151
  54.7 0.1 reshape.152.start
  54.8 0.1 slice.35
  54.9 0.5 convert_bitcast_fusion.low
  55.4 0.0 copy-done.5
  55.4 10.9 %attend.1 = (bf16[4,64,512]{2,1,0:T(8,128)(2,1)}, f32[64,2048]{1,0:T(8,128)}, f32[1,2048]{1,0:T(1,128)}, bf16[192,2048]{1,0:T(8,128)(2,1)}) custom-call(s32[8]{0:T(128)} %convert_bitcast_fusion.low, bf16[4,192,512]{2,1,0:T(8,128)(2,1)} %get-tuple-element.42.qkv_heads, f32[1,2048]{1,0:T(1,128)} %copy-done.5), custom_call_target="tpu_custom_call" | custom-call | tf_op jit(solution)/shard_map/attend/pallas_call | solution.py:914
  66.3 122.6 %feed_forward.1 = (bf16[128,1024]{1,0:T(8,128)(2,1)}, f32[128,1024]{1,0:T(8,128)}, bf16[4,64,512]{2,1,0:T(8,128)(2,1)}, f32[128,1024]{1,0:T(8,128)}, bf16[8,128,...) custom-call(bf16[4,64,512]{2,1,0:T(8,128)(2,1)} %get-tuple-element.43.o_heads, ...), custom_call_target="tpu_custom_call" | custom-call | tf_op jit(solution)/shard_map/feed_forward/pallas_call | solution.py:1109
  188.9 12.5 %attend_back.1.d_heads = bf16[4,192,512]{2,1,0:T(8,128)(2,1)} custom-call(s32[8]{0:T(128)} %convert_bitcast_fusion.low, bf16[192,2048]{1,0:T(8,128)(2,1)} %get-tuple-element.48.qkv, f32[64,2048]{1,0:T(8,128)} %get-tuple-element.49.o_true, f32[1,2048]{1,0:T(1,128)} %get-tuple-element.50.lse, f32[1,2048]{1,0:T(1,128)} %copy-done.5, ...), custom_call_target="tpu_custom_call" | custom-call | tf_op jit(solution)/shard_map/attend_back/pallas_call | solution.py:968
  201.4 75.0 %gradients.1 = (f32[128,1024]{1,0:T(8,128)}, f32[32,1024]{1,0:T(8,128)}, f32[32,1024]{1,0:T(8,128)}, f32[32,1024]{1,0:T(8,128)}, f32[32,1024]{1,0:T(8,128)}, /*index=5*/f32[32,4096]{1,0:T(8,128)}, f32[8,128]{1,0:T(8,128)}) custom-call(bf16[4,192,512]{2,1,0:T(8,128)(2,1)} %attend_back.1.d_heads, bf16[1024,512]{1,0:T(8,128)(2,1)} %get-tuple-element.52.a_t, ...), custom_call_target="tpu_custom_call" | custom-call | tf_op jit(solution)/shard_map/gradients/pallas_call | solution.py:1300
  276.4 0.0 copy-start.4
  276.4 0.0 copy-start.3
  276.4 0.0 copy-start.1
  276.5 0.0 copy-start
  276.5 0.9 constant_dynamic-slice_fusion
  277.3 0.5 slice_bitcast_fusion
  277.9 0.0 copy-done.2
  277.9 0.7 copy.45
  278.6 1.9 copy.46
  280.5 1.6 copy.47
  282.0 1.6 copy.48
  283.6 0.0 copy-done.4
  283.6 0.7 copy.49
  284.2 0.0 copy-done.3
  284.3 0.7 copy.50
  284.9 0.8 copy.51
  285.7 0.8 copy.52
  (11 shorter events, 0.1 us)
Async XLA Ops:
  54.8 0.6 copy-start.5
  201.4 76.5 %copy-start.2 = (bf16[128,1024]{1,0:T(8,128)(2,1)S(1)}, bf16[128,1024]{1,0:T(8,128)(2,1)}, u32[]{:S(2)}) copy-start(bf16[128,1024]{1,0:T(8,128)(2,1)} %get-tuple-element.47) | copy-start | bytes 786436
  276.4 7.2 %copy-start.4 = (f32[32,1024]{1,0:T(8,128)S(1)}, f32[32,1024]{1,0:T(8,128)}, u32[]{:S(2)}) copy-start(f32[32,1024]{1,0:T(8,128)} %get-tuple-element.96) | copy-start | bytes 393220
  276.4 7.8 %copy-start.3 = (f32[32,1024]{1,0:T(8,128)S(1)}, f32[32,1024]{1,0:T(8,128)}, u32[]{:S(2)}) copy-start(f32[32,1024]{1,0:T(8,128)} %get-tuple-element.97) | copy-start | bytes 393220
  276.4 8.5 %copy-start.1 = (f32[32,4096]{1,0:T(8,128)S(1)}, f32[32,4096]{1,0:T(8,128)}, u32[]{:S(2)}) copy-start(f32[32,4096]{1,0:T(8,128)} %get-tuple-element.98) | copy-start | bytes 1572868
  276.5 9.3 %copy-start = (f32[128,1024]{1,0:T(8,128)S(1)}, f32[128,1024]{1,0:T(8,128)}, u32[]{:S(2)}) copy-start(f32[128,1024]{1,0:T(8,128)} %get-tuple-element.99) | copy-start | bytes 1572868

commit v2 on v0

--- a/solution.py
+++ b/solution.py
@@ -3,6 +3,8 @@
 import jax
 import jax.numpy as jnp
 from jax import lax
+from jax.experimental import pallas as pl
+from jax.experimental.pallas import tpu as pltpu
 from jax.sharding import PartitionSpec as P
 
 HEADS = 16
@@ -366,6 +368,909 @@
     return (result.astype(jnp.bfloat16)[None], input_grad) + tuple(shares)
 
 
+BF = jnp.bfloat16
+F32 = jnp.float32
+MESH_ID = pl.DeviceIdType.MESH
+GROUP = 4
+SPOTS = 8
+ROWS = 128
+WIDTH = 1024
+VMEM_BYTES = 60 << 20
+
+
+def dot(left, right, left_dim, right_dim):
+    return lax.dot_general(
+        left, right, (((left_dim,), (right_dim,)), ((), ())), preferred_element_type=F32
+    )
+
+
+class Here:
+    def __init__(self):
+        self.x = lax.axis_index("dp")
+        at = lax.axis_index("ctx")
+        self.z, self.y, self.c = at // 4, (at // 2) % 2, at % 2
+        self.member = at % 4
+        self.shard = 4 * self.x + self.z
+        self.spot = self.z + self.x * (7 - 2 * self.z)
+        self.core_mate = self.place(self.x, self.z, self.y, 1 - self.c)
+        self.link_mate = self.place(self.x, self.z, 1 - self.y, self.c)
+        self.far_mate = self.place(self.x, self.z, 1 - self.y, 1 - self.c)
+        self.core_member = 2 * self.y + (1 - self.c)
+        self.link_member = 2 * (1 - self.y) + self.c
+        self.far_member = 2 * (1 - self.y) + (1 - self.c)
+        self.right = self.on_ring(self.spot + 1)
+        self.left = self.on_ring(self.spot + SPOTS - 1)
+
+    @staticmethod
+    def place(x, z, y, c):
+        return (x, 4 * z + 2 * y + c)
+
+    def on_ring(self, spot):
+        spot = lax.rem(spot, SPOTS)
+        x = spot // 4
+        return self.place(x, spot + x * (7 - 2 * spot), self.y, self.c)
+
+    @staticmethod
+    def shard_at(spot):
+        spot = lax.rem(spot, SPOTS)
+        x = spot // 4
+        return 4 * x + spot + x * (7 - 2 * spot)
+
+    def plane(self, step):
+        shard = lax.rem(self.shard + step, SPOTS)
+        return shard, self.place(shard // 4, shard % 4, self.y, self.c)
+
+    def along_z(self, step):
+        z = lax.rem(self.z + step, 4)
+        return z, self.place(self.x, z, self.y, self.c)
+
+    def mates(self):
+        return (
+            (self.core_member, self.core_mate),
+            (self.link_member, self.link_mate),
+            (self.far_member, self.far_mate),
+        )
+
+
+class Post:
+    def __init__(self, send_sems, recv_sems):
+        self.send_sems, self.recv_sems = send_sems, recv_sems
+        self.count = 0
+        self.started = []
+
+    def send(self, src, dst, to):
+        copy = pltpu.make_async_remote_copy(
+            src_ref=src,
+            dst_ref=dst,
+            send_sem=self.send_sems.at[self.count],
+            recv_sem=self.recv_sems.at[self.count],
+            device_id=to,
+            device_id_type=MESH_ID,
+        )
+        copy.start()
+        self.started.append(copy)
+        self.count += 1
+        return self.count - 1, to
+
+    def arrived(self, sent, landing):
+        number, to = sent
+        pltpu.make_async_remote_copy(
+            src_ref=landing,
+            dst_ref=landing,
+            send_sem=self.send_sems.at[number],
+            recv_sem=self.recv_sems.at[number],
+            device_id=to,
+            device_id_type=MESH_ID,
+        ).wait_recv()
+
+    def finish(self):
+        for copy in self.started:
+            copy.wait_send()
+
+
+class Local:
+    def __init__(self, sems):
+        self.sems = sems
+        self.started = []
+
+    def copy(self, src, dst):
+        copy = pltpu.make_async_copy(src, dst, self.sems.at[len(self.started)])
+        copy.start()
+        self.started.append(copy)
+        return copy
+
+
+class RingGather:
+    STREAMS = ((1, 0, 4), (-1, 1, 4), (1, 1, 3), (-1, 0, 3))
+
+    def __init__(self, here, post, held, own):
+        self.here, self.post, self.held, self.own = here, post, held, own
+        self.half = held.shape[1] // 2
+        self.waiting = {}
+        self.hops = 0
+
+    def piece(self, shard, half):
+        return self.held.at[shard, pl.ds(half * self.half, self.half)]
+
+    def hop(self):
+        self.hops += 1
+        for way, half, length in self.STREAMS:
+            if self.hops > length:
+                continue
+            if self.hops > 1:
+                self.take(way, half)
+            origin = self.here.shard_at(self.here.spot + SPOTS - way * (self.hops - 1))
+            src = self.piece(origin, half)
+            if self.hops == 1:
+                src = self.own.at[pl.ds(half * self.half, self.half)]
+            sent = self.post.send(
+                src, self.piece(origin, half), self.here.right if way == 1 else self.here.left
+            )
+            came = self.here.shard_at(self.here.spot + SPOTS - way * self.hops)
+            self.waiting[way, half] = (sent, self.piece(came, half))
+
+    def take(self, way, half):
+        sent, landing = self.waiting.pop((way, half))
+        self.post.arrived(sent, landing)
+
+    def finish(self):
+        while self.hops < 4:
+            self.hop()
+        for key in list(self.waiting):
+            self.take(*key)
+
+
+class RingSum:
+    def __init__(self, here, post, parts, landing):
+        self.here, self.post, self.parts, self.landing = here, post, parts, landing
+        self.half = parts.shape[1] // 2
+        self.waiting = {}
+        self.slots = 0
+        self.hops = 0
+
+    def part(self, distance, half):
+        shard = self.here.shard_at(self.here.spot + SPOTS + distance)
+        return self.parts.at[shard, pl.ds(half * self.half, self.half)]
+
+    def hop(self):
+        self.hops += 1
+        distance = 5 - self.hops
+        for way, half, first in ((1, 0, 1), (-1, 1, 1), (1, 1, 2), (-1, 0, 2)):
+            if self.hops < first:
+                continue
+            src = self.part(way * distance, half)
+            if self.hops > first:
+                held = self.take(way, half)
+                held[...] = (held[...].astype(F32) + src[...].astype(F32)).astype(held.dtype)
+                src = held
+            slot = self.landing.at[self.slots]
+            self.slots += 1
+            sent = self.post.send(src, slot, self.here.right if way == 1 else self.here.left)
+            self.waiting[way, half] = (sent, slot)
+
+    def take(self, way, half):
+        sent, slot = self.waiting.pop((way, half))
+        self.post.arrived(sent, slot)
+        return slot
+
+    def total(self):
+        halves = []
+        for half in (0, 1):
+            value = self.part(0, half)[...].astype(F32)
+            for way in (1, -1):
+                value = value + self.take(way, half)[...].astype(F32)
+            halves.append(value)
+        return halves
+
+
+class GroupGather:
+    def __init__(self, here, post, held):
+        self.here, self.post, self.held = here, post, held
+        self.over = []
+        for half in (0, 1):
+            mine = self.piece(here.member, half)
+            self.over.append(post.send(mine, mine, here.link_mate))
+        mine = held.at[here.member]
+        self.core = post.send(mine, mine, here.core_mate)
+
+    def piece(self, member, half):
+        return self.held.at[member, pl.ds(64 * half, 64)]
+
+    def near(self):
+        self.post.arrived(self.core, self.held.at[self.here.core_member])
+
+    def rest(self):
+        here, passed = self.here, []
+        for half in (0, 1):
+            linked = self.piece(here.link_member, half)
+            self.post.arrived(self.over[half], linked)
+            passed.append(self.post.send(linked, linked, here.core_mate))
+        for half in (0, 1):
+            self.post.arrived(passed[half], self.piece(here.far_member, half))
+
+
+class GroupSum:
+    def __init__(self, here, post, near_send, near_in, far_send, far_in, terms):
+        self.here, self.post = here, post
+        self.near_send, self.near_in = near_send, near_in
+        self.far_send, self.far_in = far_send, far_in
+        self.terms = terms
+        self.near = [None, None]
+
+    def give(self, slot, value):
+        here = self.here
+        self.terms[slot] = value.reshape(2, ROWS, WIDTH)
+        self.near_send[slot] = self.terms[slot, 1 - here.c].astype(BF)
+        self.near[slot] = self.post.send(
+            self.near_send.at[slot], self.near_in.at[slot], here.core_mate
+        )
+
+    def cross(self):
+        here = self.here
+        self.post.arrived(self.near[0], self.near_in.at[0])
+        self.far_send[...] = (self.terms[0, here.c] + self.near_in[0].astype(F32)).astype(BF)
+        self.far = self.post.send(self.far_send, self.far_in, here.link_mate)
+
+    def total(self):
+        self.post.arrived(self.near[1], self.near_in.at[1])
+        value = self.terms[1, self.here.c] + self.near_in[1].astype(F32)
+        self.post.arrived(self.far, self.far_in)
+        return value + self.far_in[...].astype(F32)
+
+
+class SwapAlongZ:
+    def __init__(self, here, post, local, src, dst):
+        self.post = post
+        self.sent = []
+        for step in (2, 1, 3):
+            z, place = here.along_z(step)
+            came = lax.rem(here.z + 4 - step, 4)
+            self.sent.append((post.send(src.at[z], dst.at[here.z], place), dst.at[came]))
+        self.own = local.copy(src.at[here.z], dst.at[here.z])
+
+    def finish(self):
+        self.own.wait()
+        for sent, landing in self.sent:
+            self.post.arrived(sent, landing)
+
+
+def out_rows_target(here):
+    return here.z % 2, 2 * here.y + here.c, here.z // 2, here.x
+
+
+def out_rows_source(here):
+    return here.c, 2 * here.y + here.x, here.z // 2, here.z % 2
+
+
+def same_place(here, spot):
+    x, z, y, c = spot
+    return (x == here.x) & (z == here.z) & (y == here.y) & (c == here.c)
+
+
+def turn_tables(rot):
+    index = lax.broadcasted_iota(jnp.int32, (HD // 2, 1), 0).astype(F32)
+    angle = rot * jnp.exp(index * (-math.log(10000.0) / (HD // 2)))
+    return jnp.cos(angle), jnp.sin(angle)
+
+
+def norm_parts(value):
+    centred = value - jnp.mean(value, -1, keepdims=True)
+    inv_std = lax.rsqrt(jnp.mean(centred * centred, -1, keepdims=True) + norm_eps)
+    return centred * inv_std, inv_std
+
+
+def norm_pull(normed, inv_std, gain, upstream):
+    d_normed = upstream * gain
+    return inv_std * (
+        d_normed
+        - jnp.mean(d_normed, -1, keepdims=True)
+        - normed * jnp.mean(d_normed * normed, -1, keepdims=True)
+    )
+
+
+def true_group(ref, group):
+    def chunk(at, late):
+        tile = ref[at // 4, :, 128 * (at % 4) : 128 * (at % 4) + 128]
+        return tile[:, 64:] if late else tile[:, :64]
+
+    if group < 8:
+        return jnp.concatenate([chunk(2 * group, False), chunk(2 * group + 1, False)], 1)
+    return jnp.concatenate([chunk(31 - 2 * group, True), chunk(30 - 2 * group, True)], 1)
+
+
+def stored_group(ref, at):
+    def block(number):
+        tile = ref[:, 128 * (number // 2) : 128 * (number // 2) + 128]
+        return tile[:, 64:] if number % 2 else tile[:, :64]
+
+    return jnp.concatenate([block(at), block(31 - at)], 1)
+
+
+def allowed_pairs(key_at, keys, query_at, queries, start):
+    key_pos = key_at + lax.broadcasted_iota(jnp.int32, (keys, queries), 0)
+    allowed = key_pos >= start
+    if key_at + keys > query_at:
+        allowed &= key_pos <= query_at + lax.broadcasted_iota(jnp.int32, (keys, queries), 1)
+    return allowed
+
+
+def attend_block(qkv, start, o_true, lse, query_at, queries, keys):
+    here = slice(query_at, query_at + queries)
+    query, first = qkv[0:HD, here], start[:, here]
+    parts, top = [], None
+    for key_at in range(0, query_at + queries, keys):
+        scores = dot(qkv[HD : 2 * HD, key_at : key_at + keys], query, 0, 0)
+        scores = jnp.where(
+            allowed_pairs(key_at, keys, query_at, queries, first), scores, masked_value
+        )
+        peak = jnp.max(scores, 0, keepdims=True)
+        top = peak if top is None else jnp.maximum(top, peak)
+        parts.append((key_at, scores))
+    total, weighted = 0.0, 0.0
+    for key_at, scores in parts:
+        probs = jnp.exp(scores - top)
+        total = total + jnp.sum(probs, 0, keepdims=True)
+        weighted = weighted + dot(qkv[2 * HD :, key_at : key_at + keys], probs.astype(BF), 1, 0)
+    o_true[:, here] = weighted / total
+    lse[:, here] = top + jnp.log(total)
+
+
+def attend_back_block(qkv, start, o_true, lse, d_out, grads, query_at, queries):
+    here = slice(query_at, query_at + queries)
+    reach = slice(0, query_at + queries)
+    query, d_attn = qkv[0:HD, here], d_out[:, here]
+    key = qkv[HD : 2 * HD, reach]
+    delta = jnp.sum(d_attn.astype(F32) * o_true[:, here], 0, keepdims=True)
+    allowed = allowed_pairs(0, query_at + queries, query_at, queries, start[:, here])
+    probs = jnp.where(allowed, jnp.exp(dot(key, query, 0, 0) - lse[:, here]), 0.0)
+    d_probs = dot(qkv[2 * HD :, reach], d_attn, 0, 0)
+    d_scores = (probs * (d_probs - delta)).astype(BF)
+    grads[HD : 2 * HD, reach] += dot(query, d_scores, 1, 1)
+    grads[2 * HD :, reach] += dot(d_attn, probs.astype(BF), 1, 1)
+    grads[0:HD, here] = dot(key, d_scores, 1, 0) * HD**-0.5
+
+
+GELU_K = math.sqrt(2.0 / math.pi)
+
+
+def gelu_and_slope(pre):
+    square = pre * pre
+    bend = jnp.tanh(GELU_K * pre * (1.0 + 0.044715 * square))
+    half = 0.5 * (1.0 + bend)
+    slope = half + 0.5 * pre * (1.0 - bend * bend) * GELU_K * (1.0 + 3 * 0.044715 * square)
+    return pre * half, slope
+
+
+def layer_kernel(
+    tok_hbm, seg_hbm, cot_hbm, wq, wk, wv, wo, wu, wd, *rest
+):
+    norms = rest[:8]
+    act, in_grad, g_down, up_got, qkv_got, out_got, g_vec = rest[8:15]
+    (
+        tok, cot, wqkv_own, wu_own, seg_in,
+        x_all, wqkv, wqkv_send, wu_send, wu_in, small_in, small_all, wo_in, wo_all, wu_all, wd_all,
+        vectors, starts, start, a_t, qkv_send, qkv_heads, qkv, o_true, lse, o_send, o_all,
+        c_all, dm_all, dt_all, gl_all, slope_all, du_all, res,
+        near_send, near_in, far_send, far_in, terms,
+        do_send, do_heads, d_out, grads, d_send, d_in, d_all,
+        down_parts, down_in, up_parts, up_in, out_parts, out_in, qkv_parts, qkv_in,
+        vec_send, vec_in, vec_group, d_vec, up_send, qkv_end, out_end,
+        send_sems, recv_sems, local_sems, self_sems,
+    ) = rest[15:]
+    here = Here()
+    post = Post(send_sems, recv_sems)
+    local = Local(local_sems)
+    out_to, out_from = out_rows_target(here), out_rows_source(here)
+    out_stays = same_place(here, out_to)
+    out_moves = jnp.logical_not(out_stays)
+    barrier = pltpu.get_barrier_semaphore()
+    partners = [place for _, place in here.mates()] + [here.plane(n)[1] for n in range(1, SPOTS)]
+    for place in partners:
+        pl.semaphore_signal(barrier, inc=1, device_id=place, device_id_type=MESH_ID)
+
+    @pl.when(out_moves)
+    def _():
+        for spot in (out_from, out_to):
+            pl.semaphore_signal(
+                barrier, inc=1, device_id=here.place(*spot), device_id_type=MESH_ID
+            )
+
+    loads = [
+        local.copy(weight, wqkv_own.at[slot]) for slot, weight in enumerate((wq, wk, wv))
+    ]
+    load_wu = local.copy(wu, wu_own)
+    load_tok = local.copy(tok_hbm, tok)
+    load_seg = local.copy(seg_hbm, seg_in)
+    load_cot = local.copy(cot_hbm, cot)
+    load_wd = local.copy(wd, wd_all.at[here.shard])
+
+    lane = lax.broadcasted_iota(jnp.int32, (1, ROWS), 1)
+    for row, vector in enumerate(norms):
+        value = vector[...].astype(F32)
+        value = jnp.concatenate([value] * GROUP, 1)
+        small_in[here.member, row : row + 1] = jnp.where(lane // 32 == here.member, value, 0.0)
+    load_seg.wait()
+    small_in[here.member, 8:9] = seg_in[...].astype(F32)
+    for load in loads:
+        load.wait()
+    for member in range(GROUP):
+        base = 512 * (member % 2) + 256 * (member // 2)
+        for slot in range(3):
+            wqkv_send[member, :, 256 * slot : 256 * (slot + 1)] = wqkv_own[slot, :, base : base + 256]
+    wqkv[here.shard, pl.ds(pl.multiple_of(32 * here.member, 32), 32)] = wqkv_send[here.member]
+    load_tok.wait()
+    x_all[here.member] = tok[...]
+
+    @pl.when(out_stays)
+    def _():
+        pl.semaphore_wait(barrier, len(partners))
+
+    @pl.when(out_moves)
+    def _():
+        pl.semaphore_wait(barrier, len(partners) + 2)
+
+    small_sent, wqkv_sent, wu_sent = [], [], []
+    for member, place in here.mates():
+        mine = small_in.at[here.member]
+        small_sent.append((post.send(mine, mine, place), small_in.at[member]))
+    for member, place in here.mates():
+        mine = wqkv.at[here.shard, pl.ds(pl.multiple_of(32 * here.member, 32), 32)]
+        theirs = wqkv.at[here.shard, pl.ds(pl.multiple_of(32 * member, 32), 32)]
+        wqkv_sent.append((post.send(wqkv_send.at[member], mine, place), theirs))
+    x_gather = GroupGather(here, post, x_all)
+    down_ring = RingGather(here, post, wd_all, wd)
+    down_ring.hop()
+    wo_copy = pltpu.make_async_remote_copy(
+        src_ref=wo, dst_ref=wo_in, send_sem=self_sems.at[0], recv_sem=self_sems.at[1],
+        device_id=here.place(*out_to), device_id_type=MESH_ID,
+    )
+    wo_keep = pltpu.make_async_copy(wo, wo_in, self_sems.at[2])
+    pl.when(out_moves)(wo_copy.start)
+    pl.when(out_stays)(wo_keep.start)
+    load_wu.wait()
+    for member in range(GROUP):
+        for shard in range(SPOTS):
+            at = 512 * shard + 128 * member
+            wu_send[member, :, 128 * shard : 128 * (shard + 1)] = wu_own[:, at : at + 128]
+    wu_in[pl.ds(pl.multiple_of(32 * here.member, 32), 32)] = wu_send[here.member]
+    for member, place in here.mates():
+        mine = wu_in.at[pl.ds(pl.multiple_of(32 * here.member, 32), 32)]
+        theirs = wu_in.at[pl.ds(pl.multiple_of(32 * member, 32), 32)]
+        wu_sent.append((post.send(wu_send.at[member], mine, place), theirs))
+
+    for sent, landing in small_sent:
+        post.arrived(sent, landing)
+    small_all[here.shard, 0:8] = (
+        small_in[0, 0:8] + small_in[1, 0:8] + small_in[2, 0:8] + small_in[3, 0:8]
+    )
+    for member in range(GROUP):
+        small_all[here.shard, 8 + member : 9 + member] = small_in[member, 8:9]
+    plane_sent = []
+    for step in range(1, SPOTS):
+        _, place = here.plane(step)
+        came = lax.rem(here.shard + SPOTS - step, SPOTS)
+        mine = small_all.at[here.shard]
+        plane_sent.append((post.send(mine, mine, place), small_all.at[came]))
+
+    for sent, landing in wqkv_sent:
+        post.arrived(sent, landing)
+    qkv_ring = RingGather(here, post, wqkv, wqkv.at[here.shard])
+    qkv_ring.hop()
+    x_gather.near()
+    for sent, landing in plane_sent:
+        post.arrived(sent, landing)
+    for shard in range(SPOTS):
+        vectors[:, 128 * shard : 128 * (shard + 1)] = small_all[shard, 0:8]
+    gain, bias = vectors[0:1], vectors[1:2]
+
+    def put_a(member):
+        normed, _ = norm_parts(x_all[member].astype(F32))
+        at = pl.ds(pl.multiple_of(ROWS * member, ROWS), ROWS)
+        a_t[:, at] = (normed * gain + bias).astype(BF).T
+
+    x_gather.rest()
+    qkv_ring.hop()
+
+    @pl.when(out_moves)
+    def _():
+        wo_copy.wait_recv()
+        wo_copy.wait_send()
+
+    pl.when(out_stays)(wo_keep.wait)
+    out_ring = RingGather(here, post, wo_all, wo_in)
+    wo_all[here.shard] = wo_in[...]
+    out_ring.hop()
+    put_a(here.member)
+    put_a(here.core_member)
+    qkv_ring.hop()
+    out_ring.hop()
+    put_a(here.link_member)
+    put_a(here.far_member)
+
+    segs = jnp.concatenate([small_all[4 * here.x + z, 8:12] for z in range(4)], 0)
+    begin = jnp.zeros_like(segs)
+    for doc in range(1, 8):
+        size = jnp.sum(
+            jnp.sum((segs == doc - 1.0).astype(F32), 1, keepdims=True), 0, keepdims=True
+        )
+        begin = begin + jnp.where(segs >= doc, size, 0.0)
+    starts[...] = begin
+    for group in range(16):
+        a, b, cut = 2 * group, 2 * group + 1, slice(0, 64)
+        if group >= 8:
+            a, b, cut = 31 - a, 31 - b, slice(64, 128)
+        start[:, ROWS * group : ROWS * (group + 1)] = jnp.concatenate(
+            [starts[a : a + 1, cut], starts[b : b + 1, cut]], 1
+        ).astype(jnp.int32)
+    rots = []
+    for member in range(GROUP):
+        at = 4 * here.z + member
+        position = jnp.where(lane < 64, 64 * at + lane, 64 * (31 - at) + lane - 64)
+        rots.append(position.astype(F32) - starts[pl.ds(at, 1)])
+    cos_t, sin_t = turn_tables(jnp.concatenate(rots, 1))
+    qkv_ring.hop()
+    out_ring.hop()
+    for sent, landing in wu_sent:
+        post.arrived(sent, landing)
+    up_ring = RingGather(here, post, wu_all, wu_in)
+    wu_all[here.shard] = wu_in[...]
+    up_ring.hop()
+    qkv_ring.finish()
+
+    wqkv_flat = wqkv[...].reshape(WIDTH, 768)
+    for part in range(3):
+        product = dot(wqkv_flat[:, 256 * part : 256 * (part + 1)], a_t[...], 0, 0)
+        for head in range(4):
+            rows = product[HD * head : HD * (head + 1)]
+            if part < 2:
+                first, second = rows[: HD // 2], rows[HD // 2 :]
+                rows = jnp.concatenate(
+                    [first * cos_t - second * sin_t, second * cos_t + first * sin_t], 0
+                )
+            if part == 0:
+                rows = rows * HD**-0.5
+            qkv_send[head, HD * part : HD * (part + 1)] = rows.astype(BF)
+    swap = SwapAlongZ(here, post, local, qkv_send, qkv_heads)
+    out_ring.finish()
+    swap.finish()
+    down_ring.hop()
+    up_ring.hop()
+    for group in range(16):
+        qkv[:, ROWS * group : ROWS * (group + 1)] = true_group(qkv_heads, group)
+    for query_at in range(0, 2048, 512):
+        attend_block(qkv, start, o_true, lse, query_at, 512, 512)
+    for at in range(16):
+        o_send[at // 4, :, 128 * (at % 4) : 128 * (at % 4) + 128] = stored_group(o_true, at).astype(BF)
+    swap = SwapAlongZ(here, post, local, o_send, o_all)
+    swap.finish()
+    down_ring.hop()
+    up_ring.hop()
+
+    sums = [
+        GroupSum(here, post, near_send.at[n], near_in.at[n], far_send.at[n], far_in.at[n], terms)
+        for n in range(4)
+    ]
+    wo_flat = wo_all[...].reshape(256, WIDTH)
+
+    def half_lanes(y):
+        return pl.ds(pl.multiple_of(256 * y, 256), 256)
+
+    def out_half(y):
+        heads = [o_all[z, :, half_lanes(y)] for z in range(4)]
+        return dot(jnp.concatenate(heads, 0), wo_flat, 0, 0)
+
+    sums[0].give(0, out_half(1 - here.y))
+    sums[0].give(1, out_half(here.y))
+    sums[0].cross()
+    branch = sums[0].total()
+    t_normed, t_inv = norm_parts(branch)
+    hres = tok[...].astype(F32) + t_normed * vectors[2:3] + vectors[3:4]
+    res[0] = t_normed
+    h_normed, h_inv = norm_parts(hres)
+    res[1] = h_normed
+    res[2] = hres
+    c_all[here.member] = (h_normed * vectors[4:5] + vectors[5:6]).astype(BF)
+    gather = GroupGather(here, post, c_all)
+    down_ring.hop()
+    up_ring.hop()
+    gather.near()
+    up_ring.finish()
+    wu_flat = wu_all[...].reshape(WIDTH, WIDTH)
+
+    def half(held, y):
+        return held[pl.ds(2 * y, 2)].reshape(2 * ROWS, WIDTH)
+
+    def up_half(y):
+        gl, slope = gelu_and_slope(dot(half(c_all, y), wu_flat, 1, 0))
+        gl_all[pl.ds(2 * y, 2)] = gl.astype(BF).reshape(2, ROWS, WIDTH)
+        slope_all[pl.ds(2 * y, 2)] = slope.reshape(2, ROWS, WIDTH)
+
+    up_half(here.y)
+    load_wd.wait()
+    down_ring.finish()
+    wd_flat = wd_all[...].reshape(WIDTH, WIDTH)
+    sums[1].give(1, dot(half(gl_all, here.y), wd_flat, 1, 0))
+    gather.rest()
+    up_half(1 - here.y)
+    sums[1].give(0, dot(half(gl_all, 1 - here.y), wd_flat, 1, 0))
+    sums[1].cross()
+    branch = sums[1].total()
+    m_normed, m_inv = norm_parts(branch)
+    act[...] = (res[2] + m_normed * vectors[6:7] + vectors[7:8]).astype(BF)
+    load_cot.wait()
+    upstream = cot[...].astype(F32)
+    dm_all[here.member] = norm_pull(m_normed, m_inv, vectors[6:7], upstream).astype(BF)
+    gather = GroupGather(here, post, dm_all)
+    d_vec[6:7] = jnp.sum(upstream * m_normed, 0, keepdims=True)
+    d_vec[7:8] = jnp.sum(upstream, 0, keepdims=True)
+    gather.near()
+
+    def du_half(y):
+        d_gl = dot(half(dm_all, y), wd_flat, 1, 1)
+        slope = slope_all[pl.ds(2 * y, 2)].reshape(2 * ROWS, WIDTH)
+        du_all[pl.ds(2 * y, 2)] = (d_gl * slope).astype(BF).reshape(2, ROWS, WIDTH)
+
+    du_half(here.y)
+    sums[2].give(1, dot(half(du_all, here.y), wu_flat, 1, 1))
+    gather.rest()
+    du_half(1 - here.y)
+    sums[2].give(0, dot(half(du_all, 1 - here.y), wu_flat, 1, 1))
+    sums[2].cross()
+    gl_flat = gl_all[...].reshape(512, WIDTH)
+    dm_flat = dm_all[...].reshape(512, WIDTH)
+    for shard in range(SPOTS):
+        down_parts[shard] = dot(gl_flat[:, ROWS * shard : ROWS * (shard + 1)], dm_flat, 0, 0).astype(BF)
+    down_sum = RingSum(here, post, down_parts, down_in)
+    up_sum = RingSum(here, post, up_parts, up_in)
+    out_sum = RingSum(here, post, out_parts, out_in)
+    qkv_sum = RingSum(here, post, qkv_parts, qkv_in)
+    down_sum.hop()
+    du_flat = du_all[...].reshape(512, WIDTH)
+    c_flat = c_all[...].reshape(512, WIDTH)
+    for shard in range(SPOTS):
+        up_parts[shard] = dot(c_flat[:, ROWS * shard : ROWS * (shard + 1)], du_flat, 0, 0).astype(BF)
+    up_sum.hop()
+    d_c = sums[2].total()
+    h_normed = res[1]
+    d_h = upstream + norm_pull(h_normed, h_inv, vectors[4:5], d_c)
+    t_normed = res[0]
+    dt_all[here.member] = norm_pull(t_normed, t_inv, vectors[2:3], d_h).astype(BF)
+    gather = GroupGather(here, post, dt_all)
+    d_vec[4:5] = jnp.sum(d_c * h_normed, 0, keepdims=True)
+    d_vec[5:6] = jnp.sum(d_c, 0, keepdims=True)
+    d_vec[2:3] = jnp.sum(d_h * t_normed, 0, keepdims=True)
+    d_vec[3:4] = jnp.sum(d_h, 0, keepdims=True)
+    res[2] = d_h
+    down_sum.hop()
+    gather.near()
+    gather.rest()
+    dt_flat = dt_all[...].reshape(512, WIDTH)
+    d_o = dot(wo_flat, dt_flat, 1, 1)
+    for head in range(4):
+        do_send[head] = d_o[HD * head : HD * (head + 1)].astype(BF)
+    swap = SwapAlongZ(here, post, local, do_send, do_heads)
+    o_flat = o_all[...].reshape(256, 512)
+    out_parts[...] = dot(o_flat, dt_flat, 1, 0).astype(BF).reshape(SPOTS, 32, WIDTH)
+    up_sum.hop()
+    out_sum.hop()
+    swap.finish()
+    down_sum.hop()
+    for group in range(16):
+        d_out[:, ROWS * group : ROWS * (group + 1)] = true_group(do_heads, group)
+    grads[HD:] = jnp.zeros((2 * HD, 2048), F32)
+    for query_at in range(0, 2048, 256):
+        attend_back_block(qkv, start, o_true, lse, d_out, grads, query_at, 256)
+        if query_at == 768:
+            up_sum.hop()
+        if query_at == 1280:
+            down_sum.hop()
+            out_sum.hop()
+        if query_at == 1792:
+            up_sum.hop()
+    position = lax.broadcasted_iota(jnp.int32, (1, 2048), 1) - start[...]
+    cos_t, sin_t = turn_tables(position.astype(F32))
+    for part in range(2):
+        first = grads[HD * part : HD * part + HD // 2]
+        second = grads[HD * part + HD // 2 : HD * (part + 1)]
+        grads[HD * part : HD * part + HD // 2] = first * cos_t + second * sin_t
+        grads[HD * part + HD // 2 : HD * (part + 1)] = second * cos_t - first * sin_t
+    for at in range(16):
+        d_send[at // 4, :, 128 * (at % 4) : 128 * (at % 4) + 128] = stored_group(grads, at).astype(BF)
+    swap = SwapAlongZ(here, post, local, d_send, d_in)
+    out_sum.hop()
+    low_half, high_half = down_sum.total()
+    g_down[0:64] = low_half
+    g_down[64:128] = high_half
+    low_half, high_half = up_sum.total()
+    for member in range(GROUP):
+        halved = low_half if member < 2 else high_half
+        up_send[member] = halved[32 * (member % 2) : 32 * (member % 2) + 32].astype(BF)
+    up_got[here.member] = up_send[here.member]
+    ends = []
+    for member, place in here.mates():
+        ends.append((post.send(up_send.at[member], up_got.at[here.member], place), up_got.at[member]))
+    out_sum.hop()
+    swap.finish()
+    for part in range(3):
+        for head in range(4):
+            at = 256 * part + HD * head
+            d_all[at : at + HD] = d_in[head, HD * part : HD * (part + 1)]
+    for shard in range(SPOTS):
+        qkv_parts[shard] = dot(a_t[ROWS * shard : ROWS * (shard + 1)], d_all[...], 1, 1).astype(BF)
+    qkv_sum.hop()
+
+    def in_half(y):
+        return dot(d_all[:, half_lanes(y)], wqkv_flat, 0, 1)
+
+    sums[3].give(0, in_half(1 - here.y))
+    sums[3].give(1, in_half(here.y))
+    sums[3].cross()
+    qkv_sum.hop()
+    low_half, high_half = out_sum.total()
+    out_end[0:16] = low_half.astype(BF)
+    out_end[16:32] = high_half.astype(BF)
+    out_copy = pltpu.make_async_remote_copy(
+        src_ref=out_end, dst_ref=out_got, send_sem=self_sems.at[3], recv_sem=self_sems.at[4],
+        device_id=here.place(*out_from), device_id_type=MESH_ID,
+    )
+    pl.when(out_moves)(out_copy.start)
+
+    @pl.when(out_stays)
+    def _():
+        out_got[...] = out_end[...]
+
+    d_a = sums[3].total()
+    normed, inv_std = norm_parts(tok[...].astype(F32))
+    in_grad[...] = res[2] + norm_pull(normed, inv_std, vectors[0:1], d_a)
+    d_vec[0:1] = jnp.sum(d_a * normed, 0, keepdims=True)
+    d_vec[1:2] = jnp.sum(d_a, 0, keepdims=True)
+    for shard in range(SPOTS):
+        vec_send[shard] = d_vec[:, ROWS * shard : ROWS * (shard + 1)]
+    vec_in[here.shard] = vec_send[here.shard]
+    vec_sent = []
+    for step in range(1, SPOTS):
+        shard, place = here.plane(step)
+        came = lax.rem(here.shard + SPOTS - step, SPOTS)
+        vec_sent.append((post.send(vec_send.at[shard], vec_in.at[here.shard], place), vec_in.at[came]))
+    qkv_sum.hop()
+    for sent, landing in vec_sent:
+        post.arrived(sent, landing)
+    total = vec_in[0]
+    for shard in range(1, SPOTS):
+        total = total + vec_in[shard]
+    vec_group[here.member] = total
+    vec_sent = []
+    for member, place in here.mates():
+        mine = vec_group.at[here.member]
+        vec_sent.append((post.send(mine, mine, place), vec_group.at[member]))
+    qkv_sum.hop()
+    for sent, landing in ends:
+        post.arrived(sent, landing)
+
+    @pl.when(out_moves)
+    def _():
+        out_copy.wait_recv()
+        out_copy.wait_send()
+
+    for sent, landing in vec_sent:
+        post.arrived(sent, landing)
+    total = vec_group[0] + vec_group[1] + vec_group[2] + vec_group[3]
+    mine = total[:, 0:32]
+    for member in range(1, GROUP):
+        mine = jnp.where(here.member == member, total[:, 32 * member : 32 * (member + 1)], mine)
+    g_vec[...] = mine
+    low_half, high_half = qkv_sum.total()
+    for member in range(GROUP):
+        halved = low_half if member < 2 else high_half
+        qkv_end[member] = halved[32 * (member % 2) : 32 * (member % 2) + 32].astype(BF)
+    qkv_got[here.member] = qkv_end[here.member]
+    ends = []
+    for member, place in here.mates():
+        ends.append((post.send(qkv_end.at[member], qkv_got.at[here.member], place), qkv_got.at[member]))
+    for sent, landing in ends:
+        post.arrived(sent, landing)
+    post.finish()
+
+
+def call_layer(*args):
+    vmem = pl.BlockSpec(memory_space=pltpu.VMEM)
+    anywhere = pl.BlockSpec(memory_space=pl.ANY)
+    shape = jax.ShapeDtypeStruct
+    dma = pltpu.SemaphoreType.DMA
+
+    def held(*dims, kind=BF):
+        return pltpu.VMEM(dims, kind)
+
+    rows = (GROUP, ROWS, WIDTH)
+    return pl.pallas_call(
+        layer_kernel,
+        out_shape=[
+            shape((ROWS, WIDTH), BF),
+            shape((ROWS, WIDTH), F32),
+            shape((ROWS, WIDTH), F32),
+            shape((GROUP, 32, WIDTH), BF),
+            shape((GROUP, 32, 768), BF),
+            shape((32, WIDTH), BF),
+            shape((8, 32), F32),
+        ],
+        in_specs=[anywhere] * 9 + [vmem] * 8,
+        out_specs=[vmem] * 7,
+        scratch_shapes=[
+            held(ROWS, WIDTH), held(ROWS, WIDTH), held(3, 32, WIDTH), held(32, 4 * WIDTH),
+            held(1, ROWS, kind=jnp.int32),
+            held(*rows), held(SPOTS, ROWS, 768), held(GROUP, 32, 768), held(GROUP, 32, WIDTH),
+            held(ROWS, WIDTH), held(GROUP, 16, ROWS, kind=F32), held(SPOTS, 16, ROWS, kind=F32),
+            held(32, WIDTH), held(SPOTS, 32, WIDTH), held(SPOTS, ROWS, WIDTH), held(SPOTS, ROWS, WIDTH),
+            held(8, WIDTH, kind=F32), held(16, ROWS, kind=F32), held(1, 2048, kind=jnp.int32),
+            held(WIDTH, 512), held(4, 192, 512), held(4, 192, 512), held(192, 2048),
+            held(HD, 2048, kind=F32), held(1, 2048, kind=F32), held(4, HD, 512), held(4, HD, 512),
+            held(*rows), held(*rows), held(*rows), held(*rows), held(*rows, kind=F32), held(*rows),
+            held(3, ROWS, WIDTH, kind=F32),
+            held(4, 2, ROWS, WIDTH), held(4, 2, ROWS, WIDTH), held(4, ROWS, WIDTH), held(4, ROWS, WIDTH),
+            held(2, 2, ROWS, WIDTH, kind=F32),
+            held(4, HD, 512), held(4, HD, 512), held(HD, 2048), held(192, 2048, kind=F32),
+            held(4, 192, 512), held(4, 192, 512), held(768, 512),
+            held(SPOTS, ROWS, WIDTH), held(14, ROWS // 2, WIDTH),
+            held(SPOTS, ROWS, WIDTH), held(14, ROWS // 2, WIDTH),
+            held(SPOTS, 32, WIDTH), held(14, 16, WIDTH),
+            held(SPOTS, ROWS, 768), held(14, ROWS // 2, 768),
+            held(SPOTS, 8, ROWS, kind=F32), held(SPOTS, 8, ROWS, kind=F32), held(GROUP, 8, ROWS, kind=F32),
+            held(8, WIDTH, kind=F32), held(GROUP, 32, WIDTH), held(GROUP, 32, 768), held(32, WIDTH),
+            dma((200,)), dma((200,)), dma((24,)), dma((5,)),
+        ],
+        compiler_params=pltpu.CompilerParams(
+            collective_id=0, has_side_effects=True, vmem_limit_bytes=VMEM_BYTES
+        ),
+        name="layer",
+    )(*args)
+
+
+def finish_kernel(
+    act_in, grad_in, down_in, up_got, qkv_got, out_got, vec,
+    act, in_grad, g_q, g_k, g_v, g_out, g_up, g_down, *g_norms
+):
+    act[...] = act_in[...]
+    in_grad[...] = grad_in[...]
+    g_down[...] = down_in[...]
+    g_out[...] = out_got[...].astype(F32)
+    for member in range(GROUP):
+        for shard in range(SPOTS):
+            at = 512 * shard + 128 * member
+            g_up[:, at : at + 128] = up_got[member, :, 128 * shard : 128 * (shard + 1)].astype(F32)
+        base = 512 * (member % 2) + 256 * (member // 2)
+        for slot, out in enumerate((g_q, g_k, g_v)):
+            out[:, base : base + 256] = qkv_got[member, :, 256 * slot : 256 * (slot + 1)].astype(F32)
+    for row, out in enumerate(g_norms):
+        out[...] = vec[row : row + 1]
+
+
+def call_finish(*args):
+    vmem = pl.BlockSpec(memory_space=pltpu.VMEM)
+    shape = jax.ShapeDtypeStruct
+    narrow = shape((32, WIDTH), F32)
+    return pl.pallas_call(
+        finish_kernel,
+        out_shape=[
+            shape((ROWS, WIDTH), BF), shape((ROWS, WIDTH), F32), narrow, narrow, narrow, narrow,
+            shape((32, 4 * WIDTH), F32), shape((ROWS, WIDTH), F32),
+        ] + [shape((1, 32), F32)] * 8,
+        in_specs=[vmem] * 7,
+        out_specs=[vmem] * 16,
+        compiler_params=pltpu.CompilerParams(vmem_limit_bytes=VMEM_BYTES // 2),
+        name="finish",
+    )(*args)
+
+
+def on_device_grouped(tokens, segments, cotangent, *params):
+    weights, norms = params[:6], params[6:]
+    results = call_layer(
+        tokens[0], segments, cotangent[0], *weights, *[vector[None] for vector in norms]
+    )
+    outs = call_finish(*results)
+    act, in_grad, *rest = outs
+    return (act[None], in_grad[None], *rest[:6]) + tuple(vector[0] for vector in rest[6:])
+
+
 def solution(mesh):
     in_specs = (
         P("dp", "ctx", None),
@@ -404,6 +1309,7 @@
         P(("dp", "ctx")),
         P(("dp", "ctx")),
     )
+    grouped = mesh.shape["dp"] == 2 and mesh.shape["ctx"] == 16
     return jax.shard_map(
-        on_device, mesh=mesh, in_specs=in_specs, out_specs=out_specs, check_vma=False
-    )
+        on_device_grouped if grouped else on_device, mesh=mesh, in_specs=in_specs, out_specs=out_specs, check_vma=False
+    )

time: 1560 us -> 233 us (0.15)
  waiting for transfers between devices: 1140 us -> 0 us
  Pallas kernels: 0 us -> 225 us
  matrix products: 149 us -> 0 us
  blocking collectives: 143 us -> 0 us
  local copies, waits for them, and re-layouts: 82.2 us -> 6.41 us
  other arithmetic: 17.4 us -> 0 us
    reduce_scatter x6 -> x0, waiting for transfers between devices: 780 us -> none  [the longest x1 187 us: on_device(): lax.psum_scatter(grad_up, ('dp', 'ctx'), scatter_dimension=0, tiled=True)]
    all_gather x10 -> x0, waiting for transfers between devices: 356 us -> none  [the longest x1 76.4 us: on_device(): lax.all_gather(w_up, ('dp', 'ctx'), axis=0, tiled=True)]
    pallas_call x0 -> x2, Pallas kernels: none -> 225 us  [the longest x1 224 us: call_layer(): pl.pallas_call(layer_kernel, out_shape=[shape((ROWS, WIDTH), BF), shape((...]
    dot_general x32 -> x0, matrix products: 149 us -> none  [the longest x6 28.8 us: score_block(): jnp.einsum('qhd,khd->hqk', queries, keys, preferred_element_type=jnp.floa...]
    unnamed x2 -> x0, blocking collectives: 82.2 us -> none
    all_gather x3 -> x0, blocking collectives: 60.7 us -> none  [the longest x1 21.1 us: on_device(): seg_all = lax.all_gather(segments, 'ctx', axis=1, tiled=True)[0]]
    dynamic_slice x22 -> x0, local copies, waits for them, and re-layouts: 36.5 us -> none  [the longest x16 36.2 us: on_device(): row_top, row_total, weighted = lax.scan(visit, start_state, blocks)[0]]
    unnamed x162 -> x14, local copies, waits for them, and re-layouts: 33.7 us -> 6.41 us
  transfers between devices with their start and end apart: 16 -> 0, of which waited for: 13 -> 0; matrix products, arithmetic and copies ran while one was open for 15% -> 0% of each run, Pallas kernels for 0% -> 0%
where the time goes in v2:
time: 233 us
  Pallas kernels  225 us (97%)
  local copies, waits for them, and re-layouts  6.41 us (3%)
    pallas_call x1, Pallas kernels, call_layer(): pl.pallas_call(layer_kernel, out_shape=[shape((ROWS, WIDTH), BF), shape((...  224 us
    unnamed x14, local copies, waits for them, and re-layouts  6.41 us

profile of v2, /device:TPU:0, one launch (start us, length us, event | category | flops | bytes accessed | tf_op | source)
XLA Modules:
  0.0 232.7 jit_solution(13120070745293938808)
XLA Ops:
  0.7 223.9 %layer.1 = (bf16[128,1024]{1,0:T(8,128)(2,1)}, f32[128,1024]{1,0:T(8,128)}, f32[128,1024]{1,0:T(8,128)}, bf16[4,32,1024]{2,1,0:T(8,128)(2,1)}, bf16[4,32,768]{2,...) custom-call(bf16[128,1024]{1,0:T(8,128)(2,1)} %bitcast.20, s32[1,128]{1,0:T(1,128)} %seg_hbm.1, ...), custom_call_target="tpu_custom_call" | custom-call | tf_op jit(solution)/shard_map/layer/pallas_call | solution.py:1185
  224.6 0.0 copy-start.6
  224.6 0.7 copy-done.6
  225.3 0.0 copy-start
  225.3 1.0 copy-done
  226.3 0.0 copy-start.1
  226.3 1.0 copy-done.1
  227.4 0.0 copy-start.2
  227.4 0.9 copy-done.2
  228.3 0.0 copy-start.3
  228.3 0.9 copy-done.3
  229.3 0.0 copy-start.4
  229.3 0.9 copy-done.4
  230.2 0.0 copy-start.5
  230.2 0.8 copy-done.5
  231.0 1.5 finish.1
Async XLA Ops:
  224.6 0.7 copy-start.6
  225.3 1.0 copy-start
  226.3 1.0 copy-start.1
  227.4 0.9 copy-start.2
  228.3 0.9 copy-start.3
  229.3 0.9 copy-start.4
  230.2 0.8 copy-start.5

commit v3 on v2

--- a/solution.py
+++ b/solution.py
@@ -388,41 +388,34 @@
     def __init__(self):
         self.x = lax.axis_index("dp")
         at = lax.axis_index("ctx")
-        self.z, self.y, self.c = at // 4, (at // 2) % 2, at % 2
-        self.member = at % 4
-        self.shard = 4 * self.x + self.z
-        self.spot = self.z + self.x * (7 - 2 * self.z)
-        self.core_mate = self.place(self.x, self.z, self.y, 1 - self.c)
-        self.link_mate = self.place(self.x, self.z, 1 - self.y, self.c)
-        self.far_mate = self.place(self.x, self.z, 1 - self.y, 1 - self.c)
-        self.core_member = 2 * self.y + (1 - self.c)
-        self.link_member = 2 * (1 - self.y) + self.c
-        self.far_member = 2 * (1 - self.y) + (1 - self.c)
-        self.right = self.on_ring(self.spot + 1)
-        self.left = self.on_ring(self.spot + SPOTS - 1)
+        self.high, self.low, self.y, self.c = at // 8, (at // 4) % 2, (at // 2) % 2, at % 2
+        self.member = 2 * self.low + self.c
+        self.tokens = 2 * self.high + self.y
+        self.shard = 4 * self.x + self.tokens
+        self.core_mate = self.place(self.x, self.high, self.low, self.y, 1 - self.c)
+        self.link_mate = self.place(self.x, self.high, 1 - self.low, self.y, self.c)
+        self.far_mate = self.place(self.x, self.high, 1 - self.low, self.y, 1 - self.c)
+        self.core_member = 2 * self.low + (1 - self.c)
+        self.link_member = 2 * (1 - self.low) + self.c
+        self.far_member = 2 * (1 - self.low) + (1 - self.c)
 
     @staticmethod
-    def place(x, z, y, c):
-        return (x, 4 * z + 2 * y + c)
-
-    def on_ring(self, spot):
-        spot = lax.rem(spot, SPOTS)
-        x = spot // 4
-        return self.place(x, spot + x * (7 - 2 * spot), self.y, self.c)
-
-    @staticmethod
-    def shard_at(spot):
-        spot = lax.rem(spot, SPOTS)
-        x = spot // 4
-        return 4 * x + spot + x * (7 - 2 * spot)
+    def place(x, high, low, y, c):
+        return (x, 8 * high + 4 * low + 2 * y + c)
+
+    def across(self, axes):
+        x = 1 - self.x if "x" in axes else self.x
+        y = 1 - self.y if "y" in axes else self.y
+        high = 1 - self.high if "z" in axes else self.high
+        return 4 * x + 2 * high + y, self.place(x, high, self.low, y, self.c)
 
     def plane(self, step):
         shard = lax.rem(self.shard + step, SPOTS)
-        return shard, self.place(shard // 4, shard % 4, self.y, self.c)
-
-    def along_z(self, step):
-        z = lax.rem(self.z + step, 4)
-        return z, self.place(self.x, z, self.y, self.c)
+        return shard, self.place(shard // 4, (shard // 2) % 2, self.low, shard % 2, self.c)
+
+    def in_sequence(self, step):
+        group = lax.rem(self.tokens + step, 4)
+        return group, self.place(self.x, group // 2, self.low, group % 2, self.c)
 
     def mates(self):
         return (
@@ -430,6 +423,18 @@
             (self.link_member, self.link_mate),
             (self.far_member, self.far_mate),
         )
+
+
+def device_of(shard, member):
+    return 8 * (shard // 2) + 4 * (member // 2) + 2 * (shard % 2) + member % 2
+
+
+def row_piece(held, shard, half):
+    return held.at[shard, half]
+
+
+def group_piece(held, shard, half):
+    return held.at[shard // 2, half, shard % 2]
 
 
 class Post:
@@ -450,6 +455,7 @@
         copy.start()
         self.started.append(copy)
         self.count += 1
+        assert self.count <= self.send_sems.shape[0]
         return self.count - 1, to
 
     def arrived(self, sent, landing):
@@ -480,85 +486,99 @@
         return copy
 
 
-class RingGather:
-    STREAMS = ((1, 0, 4), (-1, 1, 4), (1, 1, 3), (-1, 0, 3))
-
-    def __init__(self, here, post, held, own):
-        self.here, self.post, self.held, self.own = here, post, held, own
-        self.half = held.shape[1] // 2
+class CubeGather:
+    def __init__(self, here, post, held, piece, own=None):
+        self.here, self.post, self.held, self.piece, self.own = here, post, held, piece, own
         self.waiting = {}
-        self.hops = 0
-
-    def piece(self, shard, half):
-        return self.held.at[shard, pl.ds(half * self.half, self.half)]
-
-    def hop(self):
-        self.hops += 1
-        for way, half, length in self.STREAMS:
-            if self.hops > length:
-                continue
-            if self.hops > 1:
-                self.take(way, half)
-            origin = self.here.shard_at(self.here.spot + SPOTS - way * (self.hops - 1))
-            src = self.piece(origin, half)
-            if self.hops == 1:
-                src = self.own.at[pl.ds(half * self.half, self.half)]
-            sent = self.post.send(
-                src, self.piece(origin, half), self.here.right if way == 1 else self.here.left
-            )
-            came = self.here.shard_at(self.here.spot + SPOTS - way * self.hops)
-            self.waiting[way, half] = (sent, self.piece(came, half))
-
-    def take(self, way, half):
-        sent, landing = self.waiting.pop((way, half))
-        self.post.arrived(sent, landing)
+
+    def move(self, axes, half, way):
+        here = self.here
+        mine = self.piece(self.held, here.across(axes)[0], half)
+        src = mine if axes or self.own is None else self.own(half)
+        sent = self.post.send(src, mine, here.across(way)[1])
+        axes = "".join(sorted(set(axes) ^ set(way)))
+        self.waiting[axes, half] = (sent, self.piece(self.held, here.across(axes)[0], half))
+
+    def take(self, axes, half):
+        self.post.arrived(*self.waiting.pop((axes, half)))
+
+    def start(self, ways="zxy"):
+        for way in ways:
+            for half in (0, 1):
+                self.move("", half, way)
+
+    def corners(self):
+        self.take("x", 0)
+        self.move("x", 0, "y")
+        self.take("y", 1)
+        self.move("y", 1, "x")
+
+    def spread(self):
+        for half in (0, 1):
+            self.take("z", half)
+            self.move("z", half, "x")
+            self.move("z", half, "y")
+
+    def last(self):
+        self.take("xz", 0)
+        self.move("xz", 0, "y")
+        self.take("yz", 1)
+        self.move("yz", 1, "x")
 
     def finish(self):
-        while self.hops < 4:
-            self.hop()
         for key in list(self.waiting):
             self.take(*key)
 
 
-class RingSum:
-    def __init__(self, here, post, parts, landing):
-        self.here, self.post, self.parts, self.landing = here, post, parts, landing
-        self.half = parts.shape[1] // 2
+class CubeSum:
+    def __init__(self, here, post, parts, piece, landing):
+        self.here, self.post, self.parts, self.piece, self.landing = here, post, parts, piece, landing
         self.waiting = {}
         self.slots = 0
         self.hops = 0
 
-    def part(self, distance, half):
-        shard = self.here.shard_at(self.here.spot + SPOTS + distance)
-        return self.parts.at[shard, pl.ds(half * self.half, self.half)]
+    def part(self, axes, half):
+        return self.piece(self.parts, self.here.across(axes)[0], half)
+
+    def move(self, axes, half, way):
+        src = self.part(axes, half)
+        came = self.waiting.pop((axes, half), [])
+        if came:
+            value = src[...].astype(F32)
+            for sent, slot in came:
+                self.post.arrived(sent, slot)
+                value = value + slot[...].astype(F32)
+            src = came[0][1]
+            src[...] = value.astype(src.dtype)
+        slot = self.landing.at[self.slots]
+        self.slots += 1
+        sent = self.post.send(src, slot, self.here.across(way)[1])
+        axes = "".join(sorted(set(axes) ^ set(way)))
+        self.waiting.setdefault((axes, half), []).append((sent, slot))
 
     def hop(self):
         self.hops += 1
-        distance = 5 - self.hops
-        for way, half, first in ((1, 0, 1), (-1, 1, 1), (1, 1, 2), (-1, 0, 2)):
-            if self.hops < first:
-                continue
-            src = self.part(way * distance, half)
-            if self.hops > first:
-                held = self.take(way, half)
-                held[...] = (held[...].astype(F32) + src[...].astype(F32)).astype(held.dtype)
-                src = held
-            slot = self.landing.at[self.slots]
-            self.slots += 1
-            sent = self.post.send(src, slot, self.here.right if way == 1 else self.here.left)
-            self.waiting[way, half] = (sent, slot)
-
-    def take(self, way, half):
-        sent, slot = self.waiting.pop((way, half))
-        self.post.arrived(sent, slot)
-        return slot
+        if self.hops == 1:
+            for axes in ("xyz", "xy"):
+                self.move(axes, 0, "y")
+                self.move(axes, 1, "x")
+        if self.hops == 2:
+            for axes in ("z", ""):
+                self.move("x" + axes, 1, "x")
+                self.move("y" + axes, 0, "y")
+                self.move("x" + axes, 0, "x")
+                self.move("y" + axes, 1, "y")
+        if self.hops == 3:
+            self.move("z", 0, "z")
+            self.move("z", 1, "z")
 
     def total(self):
         halves = []
         for half in (0, 1):
-            value = self.part(0, half)[...].astype(F32)
-            for way in (1, -1):
-                value = value + self.take(way, half)[...].astype(F32)
+            value = self.part("", half)[...].astype(F32)
+            for sent, slot in self.waiting.pop(("", half)):
+                self.post.arrived(sent, slot)
+                value = value + slot[...].astype(F32)
             halves.append(value)
         return halves
 
@@ -618,15 +638,15 @@
         return value + self.far_in[...].astype(F32)
 
 
-class SwapAlongZ:
+class Swap:
     def __init__(self, here, post, local, src, dst):
         self.post = post
         self.sent = []
         for step in (2, 1, 3):
-            z, place = here.along_z(step)
-            came = lax.rem(here.z + 4 - step, 4)
-            self.sent.append((post.send(src.at[z], dst.at[here.z], place), dst.at[came]))
-        self.own = local.copy(src.at[here.z], dst.at[here.z])
+            group, place = here.in_sequence(step)
+            came = lax.rem(here.tokens + 4 - step, 4)
+            self.sent.append((post.send(src.at[group], dst.at[here.tokens], place), dst.at[came]))
+        self.own = local.copy(src.at[here.tokens], dst.at[here.tokens])
 
     def finish(self):
         self.own.wait()
@@ -635,16 +655,16 @@
 
 
 def out_rows_target(here):
-    return here.z % 2, 2 * here.y + here.c, here.z // 2, here.x
+    return here.low, here.y, here.x, here.c, here.high
 
 
 def out_rows_source(here):
-    return here.c, 2 * here.y + here.x, here.z // 2, here.z % 2
+    return here.low, here.c, here.x, here.high, here.y
 
 
 def same_place(here, spot):
-    x, z, y, c = spot
-    return (x == here.x) & (z == here.z) & (y == here.y) & (c == here.c)
+    x, high, low, y, c = spot
+    return (x == here.x) & (high == here.high) & (low == here.low) & (y == here.y) & (c == here.c)
 
 
 def turn_tables(rot):
@@ -668,9 +688,14 @@
     )
 
 
+def stored_at(at):
+    return 2 * (at // 8) + (at // 2) % 2, 2 * ((at // 4) % 2) + at % 2
+
+
 def true_group(ref, group):
     def chunk(at, late):
-        tile = ref[at // 4, :, 128 * (at % 4) : 128 * (at % 4) + 128]
+        tokens, member = stored_at(at)
+        tile = ref[tokens, :, ROWS * member : ROWS * (member + 1)]
         return tile[:, 64:] if late else tile[:, :64]
 
     if group < 8:
@@ -678,12 +703,15 @@
     return jnp.concatenate([chunk(31 - 2 * group, True), chunk(30 - 2 * group, True)], 1)
 
 
-def stored_group(ref, at):
+def put_stored(ref, at, values):
     def block(number):
-        tile = ref[:, 128 * (number // 2) : 128 * (number // 2) + 128]
+        tile = values[:, ROWS * (number // 2) : ROWS * (number // 2) + ROWS]
         return tile[:, 64:] if number % 2 else tile[:, :64]
 
-    return jnp.concatenate([block(at), block(31 - at)], 1)
+    tokens, member = stored_at(at)
+    ref[tokens, :, ROWS * member : ROWS * (member + 1)] = jnp.concatenate(
+        [block(at), block(31 - at)], 1
+    ).astype(BF)
 
 
 def allowed_pairs(key_at, keys, query_at, queries, start):
@@ -744,11 +772,11 @@
 def layer_kernel(
     tok_hbm, seg_hbm, cot_hbm, wq, wk, wv, wo, wu, wd, *rest
 ):
-    norms = rest[:8]
+    norms_hbm = rest[:8]
     act, in_grad, g_down, up_got, qkv_got, out_got, g_vec = rest[8:15]
     (
-        tok, cot, wqkv_own, wu_own, seg_in,
-        x_all, wqkv, wqkv_send, wu_send, wu_in, small_in, small_all, wo_in, wo_all, wu_all, wd_all,
+        tok, cot, wqkv_own, wu_own, seg_in, norms_in,
+        x_all, wqkv, wqkv_send, wu_send, small_in, small_all, wo_in, wo_all, wu_all, wd_all,
         vectors, starts, start, a_t, qkv_send, qkv_heads, qkv, o_true, lse, o_send, o_all,
         c_all, dm_all, dt_all, gl_all, slope_all, du_all, res,
         near_send, near_in, far_send, far_in, terms,
@@ -779,14 +807,18 @@
         local.copy(weight, wqkv_own.at[slot]) for slot, weight in enumerate((wq, wk, wv))
     ]
     load_wu = local.copy(wu, wu_own)
+    load_seg = local.copy(seg_hbm, seg_in)
+    load_norms = [local.copy(vector, norms_in.at[row]) for row, vector in enumerate(norms_hbm)]
     load_tok = local.copy(tok_hbm, tok)
-    load_seg = local.copy(seg_hbm, seg_in)
     load_cot = local.copy(cot_hbm, cot)
-    load_wd = local.copy(wd, wd_all.at[here.shard])
+    load_wd = [
+        local.copy(wd.at[pl.ds(64 * half, 64)], wd_all.at[here.shard, half]) for half in (0, 1)
+    ]
 
     lane = lax.broadcasted_iota(jnp.int32, (1, ROWS), 1)
-    for row, vector in enumerate(norms):
-        value = vector[...].astype(F32)
+    for row, load in enumerate(load_norms):
+        load.wait()
+        value = norms_in[row].astype(F32)
         value = jnp.concatenate([value] * GROUP, 1)
         small_in[here.member, row : row + 1] = jnp.where(lane // 32 == here.member, value, 0.0)
     load_seg.wait()
@@ -794,10 +826,15 @@
     for load in loads:
         load.wait()
     for member in range(GROUP):
-        base = 512 * (member % 2) + 256 * (member // 2)
-        for slot in range(3):
-            wqkv_send[member, :, 256 * slot : 256 * (slot + 1)] = wqkv_own[slot, :, base : base + 256]
-    wqkv[here.shard, pl.ds(pl.multiple_of(32 * here.member, 32), 32)] = wqkv_send[here.member]
+        base = 256 * member
+        for part in range(3):
+            wqkv_send[part, member] = wqkv_own[part, :, base : base + 256]
+    def member_rows(held, member):
+        at = pl.ds(pl.multiple_of(32 * (member % 2), 32), 32)
+        return held.at[here.shard // 2, member // 2, here.shard % 2, at]
+
+    for part in range(3):
+        member_rows(wqkv.at[part], here.member)[...] = wqkv_send[part, here.member]
     load_tok.wait()
     x_all[here.member] = tok[...]
 
@@ -813,13 +850,13 @@
     for member, place in here.mates():
         mine = small_in.at[here.member]
         small_sent.append((post.send(mine, mine, place), small_in.at[member]))
-    for member, place in here.mates():
-        mine = wqkv.at[here.shard, pl.ds(pl.multiple_of(32 * here.member, 32), 32)]
-        theirs = wqkv.at[here.shard, pl.ds(pl.multiple_of(32 * member, 32), 32)]
-        wqkv_sent.append((post.send(wqkv_send.at[member], mine, place), theirs))
+    for part in range(3):
+        for member, place in here.mates():
+            mine, theirs = (member_rows(wqkv.at[part], who) for who in (here.member, member))
+            wqkv_sent.append((post.send(wqkv_send.at[part, member], mine, place), theirs))
+    down_ring = CubeGather(here, post, wd_all, row_piece, lambda half: wd.at[pl.ds(64 * half, 64)])
+    down_ring.start("xy")
     x_gather = GroupGather(here, post, x_all)
-    down_ring = RingGather(here, post, wd_all, wd)
-    down_ring.hop()
     wo_copy = pltpu.make_async_remote_copy(
         src_ref=wo, dst_ref=wo_in, send_sem=self_sems.at[0], recv_sem=self_sems.at[1],
         device_id=here.place(*out_to), device_id_type=MESH_ID,
@@ -830,12 +867,11 @@
     load_wu.wait()
     for member in range(GROUP):
         for shard in range(SPOTS):
-            at = 512 * shard + 128 * member
+            at = ROWS * device_of(shard, member)
             wu_send[member, :, 128 * shard : 128 * (shard + 1)] = wu_own[:, at : at + 128]
-    wu_in[pl.ds(pl.multiple_of(32 * here.member, 32), 32)] = wu_send[here.member]
+    member_rows(wu_all, here.member)[...] = wu_send[here.member]
     for member, place in here.mates():
-        mine = wu_in.at[pl.ds(pl.multiple_of(32 * here.member, 32), 32)]
-        theirs = wu_in.at[pl.ds(pl.multiple_of(32 * member, 32), 32)]
+        mine, theirs = member_rows(wu_all, here.member), member_rows(wu_all, member)
         wu_sent.append((post.send(wu_send.at[member], mine, place), theirs))
 
     for sent, landing in small_sent:
@@ -852,15 +888,21 @@
         mine = small_all.at[here.shard]
         plane_sent.append((post.send(mine, mine, place), small_all.at[came]))
 
-    for sent, landing in wqkv_sent:
-        post.arrived(sent, landing)
-    qkv_ring = RingGather(here, post, wqkv, wqkv.at[here.shard])
-    qkv_ring.hop()
+    qkv_rings = []
+    for part in range(3):
+        for sent, landing in wqkv_sent[3 * part : 3 * part + 3]:
+            post.arrived(sent, landing)
+        qkv_rings.append(CubeGather(here, post, wqkv.at[part], group_piece))
+        qkv_rings[part].start()
+    down_ring.start("z")
     x_gather.near()
     for sent, landing in plane_sent:
         post.arrived(sent, landing)
-    for shard in range(SPOTS):
-        vectors[:, 128 * shard : 128 * (shard + 1)] = small_all[shard, 0:8]
+    for block in range(SPOTS):
+        first, cut = 2 * (block // 2), slice(64 * (block % 2), 64 * (block % 2) + 64)
+        vectors[:, ROWS * block : ROWS * (block + 1)] = jnp.concatenate(
+            [small_all[first, 0:8, cut], small_all[first + 1, 0:8, cut]], 1
+        )
     gain, bias = vectors[0:1], vectors[1:2]
 
     def put_a(member):
@@ -868,8 +910,11 @@
         at = pl.ds(pl.multiple_of(ROWS * member, ROWS), ROWS)
         a_t[:, at] = (normed * gain + bias).astype(BF).T
 
+    put_a(here.member)
+    put_a(here.core_member)
+    for ring in qkv_rings:
+        ring.corners()
     x_gather.rest()
-    qkv_ring.hop()
 
     @pl.when(out_moves)
     def _():
@@ -877,17 +922,15 @@
         wo_copy.wait_send()
 
     pl.when(out_stays)(wo_keep.wait)
-    out_ring = RingGather(here, post, wo_all, wo_in)
-    wo_all[here.shard] = wo_in[...]
-    out_ring.hop()
-    put_a(here.member)
-    put_a(here.core_member)
-    qkv_ring.hop()
-    out_ring.hop()
+    out_ring = CubeGather(here, post, wo_all, row_piece)
+    wo_all[here.shard] = wo_in[...].reshape(2, 16, WIDTH)
+    for ring in qkv_rings:
+        ring.spread()
+    out_ring.start()
     put_a(here.link_member)
     put_a(here.far_member)
 
-    segs = jnp.concatenate([small_all[4 * here.x + z, 8:12] for z in range(4)], 0)
+    segs = jnp.concatenate([small_all[4 * here.x + group, 8:12] for group in range(4)], 0)
     begin = jnp.zeros_like(segs)
     for doc in range(1, 8):
         size = jnp.sum(
@@ -895,31 +938,21 @@
         )
         begin = begin + jnp.where(segs >= doc, size, 0.0)
     starts[...] = begin
-    for group in range(16):
-        a, b, cut = 2 * group, 2 * group + 1, slice(0, 64)
-        if group >= 8:
-            a, b, cut = 31 - a, 31 - b, slice(64, 128)
-        start[:, ROWS * group : ROWS * (group + 1)] = jnp.concatenate(
-            [starts[a : a + 1, cut], starts[b : b + 1, cut]], 1
-        ).astype(jnp.int32)
     rots = []
     for member in range(GROUP):
-        at = 4 * here.z + member
+        at = 8 * here.high + 4 * (member // 2) + 2 * here.y + member % 2
         position = jnp.where(lane < 64, 64 * at + lane, 64 * (31 - at) + lane - 64)
-        rots.append(position.astype(F32) - starts[pl.ds(at, 1)])
+        rots.append(position.astype(F32) - starts[pl.ds(4 * here.tokens + member, 1)])
     cos_t, sin_t = turn_tables(jnp.concatenate(rots, 1))
-    qkv_ring.hop()
-    out_ring.hop()
     for sent, landing in wu_sent:
         post.arrived(sent, landing)
-    up_ring = RingGather(here, post, wu_all, wu_in)
-    wu_all[here.shard] = wu_in[...]
-    up_ring.hop()
-    qkv_ring.finish()
-
-    wqkv_flat = wqkv[...].reshape(WIDTH, 768)
+    up_ring = CubeGather(here, post, wu_all, group_piece)
+    for ring in qkv_rings:
+        ring.last()
+    swaps = []
     for part in range(3):
-        product = dot(wqkv_flat[:, 256 * part : 256 * (part + 1)], a_t[...], 0, 0)
+        qkv_rings[part].finish()
+        product = dot(wqkv[part].reshape(WIDTH, 256), a_t[...], 0, 0)
         for head in range(4):
             rows = product[HD * head : HD * (head + 1)]
             if part < 2:
@@ -929,22 +962,38 @@
                 )
             if part == 0:
                 rows = rows * HD**-0.5
-            qkv_send[head, HD * part : HD * (part + 1)] = rows.astype(BF)
-    swap = SwapAlongZ(here, post, local, qkv_send, qkv_heads)
-    out_ring.finish()
-    swap.finish()
-    down_ring.hop()
-    up_ring.hop()
+            qkv_send[part, head] = rows.astype(BF)
+        swaps.append(Swap(here, post, local, qkv_send.at[part], qkv_heads.at[part]))
+    up_ring.start("xy")
     for group in range(16):
-        qkv[:, ROWS * group : ROWS * (group + 1)] = true_group(qkv_heads, group)
+        a, b, cut = 2 * group, 2 * group + 1, slice(0, 64)
+        if group >= 8:
+            a, b, cut = 31 - a, 31 - b, slice(64, 128)
+        a, b = (4 * tokens + member for tokens, member in (stored_at(a), stored_at(b)))
+        start[:, ROWS * group : ROWS * (group + 1)] = jnp.concatenate(
+            [starts[a : a + 1, cut], starts[b : b + 1, cut]], 1
+        ).astype(jnp.int32)
+    down_ring.corners()
+    down_ring.spread()
+    out_ring.corners()
+    out_ring.spread()
+    for part in range(3):
+        swaps[part].finish()
+        for group in range(16):
+            at = slice(ROWS * group, ROWS * (group + 1))
+            qkv[HD * part : HD * (part + 1), at] = true_group(qkv_heads.at[part], group)
+    up_ring.start("z")
+    up_ring.corners()
     for query_at in range(0, 2048, 512):
         attend_block(qkv, start, o_true, lse, query_at, 512, 512)
     for at in range(16):
-        o_send[at // 4, :, 128 * (at % 4) : 128 * (at % 4) + 128] = stored_group(o_true, at).astype(BF)
-    swap = SwapAlongZ(here, post, local, o_send, o_all)
+        put_stored(o_send, at, o_true)
+    swap = Swap(here, post, local, o_send, o_all)
+    down_ring.last()
+    out_ring.last()
+    up_ring.spread()
+    out_ring.finish()
     swap.finish()
-    down_ring.hop()
-    up_ring.hop()
 
     sums = [
         GroupSum(here, post, near_send.at[n], near_in.at[n], far_send.at[n], far_in.at[n], terms)
@@ -952,16 +1001,17 @@
     ]
     wo_flat = wo_all[...].reshape(256, WIDTH)
 
-    def half_lanes(y):
-        return pl.ds(pl.multiple_of(256 * y, 256), 256)
-
-    def out_half(y):
-        heads = [o_all[z, :, half_lanes(y)] for z in range(4)]
+    def half_lanes(low):
+        return pl.ds(pl.multiple_of(256 * low, 256), 256)
+
+    def out_half(low):
+        heads = [o_all[group, :, half_lanes(low)] for group in range(4)]
         return dot(jnp.concatenate(heads, 0), wo_flat, 0, 0)
 
-    sums[0].give(0, out_half(1 - here.y))
-    sums[0].give(1, out_half(here.y))
+    sums[0].give(0, out_half(1 - here.low))
+    sums[0].give(1, out_half(here.low))
     sums[0].cross()
+    up_ring.last()
     branch = sums[0].total()
     t_normed, t_inv = norm_parts(branch)
     hres = tok[...].astype(F32) + t_normed * vectors[2:3] + vectors[3:4]
@@ -971,28 +1021,27 @@
     res[2] = hres
     c_all[here.member] = (h_normed * vectors[4:5] + vectors[5:6]).astype(BF)
     gather = GroupGather(here, post, c_all)
-    down_ring.hop()
-    up_ring.hop()
     gather.near()
     up_ring.finish()
     wu_flat = wu_all[...].reshape(WIDTH, WIDTH)
 
-    def half(held, y):
-        return held[pl.ds(2 * y, 2)].reshape(2 * ROWS, WIDTH)
-
-    def up_half(y):
-        gl, slope = gelu_and_slope(dot(half(c_all, y), wu_flat, 1, 0))
-        gl_all[pl.ds(2 * y, 2)] = gl.astype(BF).reshape(2, ROWS, WIDTH)
-        slope_all[pl.ds(2 * y, 2)] = slope.reshape(2, ROWS, WIDTH)
-
-    up_half(here.y)
-    load_wd.wait()
+    def half(held, low):
+        return held[pl.ds(2 * low, 2)].reshape(2 * ROWS, WIDTH)
+
+    def up_half(low):
+        gl, slope = gelu_and_slope(dot(half(c_all, low), wu_flat, 1, 0))
+        gl_all[pl.ds(2 * low, 2)] = gl.astype(BF).reshape(2, ROWS, WIDTH)
+        slope_all[pl.ds(2 * low, 2)] = slope.reshape(2, ROWS, WIDTH)
+
+    up_half(here.low)
+    for load in load_wd:
+        load.wait()
     down_ring.finish()
     wd_flat = wd_all[...].reshape(WIDTH, WIDTH)
-    sums[1].give(1, dot(half(gl_all, here.y), wd_flat, 1, 0))
+    sums[1].give(1, dot(half(gl_all, here.low), wd_flat, 1, 0))
     gather.rest()
-    up_half(1 - here.y)
-    sums[1].give(0, dot(half(gl_all, 1 - here.y), wd_flat, 1, 0))
+    up_half(1 - here.low)
+    sums[1].give(0, dot(half(gl_all, 1 - here.low), wd_flat, 1, 0))
     sums[1].cross()
     branch = sums[1].total()
     m_normed, m_inv = norm_parts(branch)
@@ -1005,30 +1054,34 @@
     d_vec[7:8] = jnp.sum(upstream, 0, keepdims=True)
     gather.near()
 
-    def du_half(y):
-        d_gl = dot(half(dm_all, y), wd_flat, 1, 1)
-        slope = slope_all[pl.ds(2 * y, 2)].reshape(2 * ROWS, WIDTH)
-        du_all[pl.ds(2 * y, 2)] = (d_gl * slope).astype(BF).reshape(2, ROWS, WIDTH)
-
-    du_half(here.y)
-    sums[2].give(1, dot(half(du_all, here.y), wu_flat, 1, 1))
+    def du_half(low):
+        d_gl = dot(half(dm_all, low), wd_flat, 1, 1)
+        slope = slope_all[pl.ds(2 * low, 2)].reshape(2 * ROWS, WIDTH)
+        du_all[pl.ds(2 * low, 2)] = (d_gl * slope).astype(BF).reshape(2, ROWS, WIDTH)
+
+    du_half(here.low)
+    sums[2].give(1, dot(half(du_all, here.low), wu_flat, 1, 1))
     gather.rest()
-    du_half(1 - here.y)
-    sums[2].give(0, dot(half(du_all, 1 - here.y), wu_flat, 1, 1))
+    du_half(1 - here.low)
+    sums[2].give(0, dot(half(du_all, 1 - here.low), wu_flat, 1, 1))
     sums[2].cross()
     gl_flat = gl_all[...].reshape(512, WIDTH)
     dm_flat = dm_all[...].reshape(512, WIDTH)
     for shard in range(SPOTS):
-        down_parts[shard] = dot(gl_flat[:, ROWS * shard : ROWS * (shard + 1)], dm_flat, 0, 0).astype(BF)
-    down_sum = RingSum(here, post, down_parts, down_in)
-    up_sum = RingSum(here, post, up_parts, up_in)
-    out_sum = RingSum(here, post, out_parts, out_in)
-    qkv_sum = RingSum(here, post, qkv_parts, qkv_in)
+        term = dot(gl_flat[:, ROWS * shard : ROWS * (shard + 1)], dm_flat, 0, 0)
+        down_parts[shard] = term.astype(BF).reshape(2, 64, WIDTH)
+    down_sum = CubeSum(here, post, down_parts, row_piece, down_in)
+    up_sum = CubeSum(here, post, up_parts, group_piece, up_in)
+    out_sum = CubeSum(here, post, out_parts, row_piece, out_in)
+    qkv_sums = [
+        CubeSum(here, post, qkv_parts.at[part], group_piece, qkv_in.at[part]) for part in range(3)
+    ]
     down_sum.hop()
     du_flat = du_all[...].reshape(512, WIDTH)
     c_flat = c_all[...].reshape(512, WIDTH)
-    for shard in range(SPOTS):
-        up_parts[shard] = dot(c_flat[:, ROWS * shard : ROWS * (shard + 1)], du_flat, 0, 0).astype(BF)
+    for block in range(SPOTS):
+        term = dot(c_flat[:, ROWS * block : ROWS * (block + 1)], du_flat, 0, 0)
+        up_parts[block // 2, block % 2] = term.astype(BF).reshape(2, 64, WIDTH)
     up_sum.hop()
     d_c = sums[2].total()
     h_normed = res[1]
@@ -1048,9 +1101,9 @@
     d_o = dot(wo_flat, dt_flat, 1, 1)
     for head in range(4):
         do_send[head] = d_o[HD * head : HD * (head + 1)].astype(BF)
-    swap = SwapAlongZ(here, post, local, do_send, do_heads)
+    swap = Swap(here, post, local, do_send, do_heads)
     o_flat = o_all[...].reshape(256, 512)
-    out_parts[...] = dot(o_flat, dt_flat, 1, 0).astype(BF).reshape(SPOTS, 32, WIDTH)
+    out_parts[...] = dot(o_flat, dt_flat, 1, 0).astype(BF).reshape(SPOTS, 2, 16, WIDTH)
     up_sum.hop()
     out_sum.hop()
     swap.finish()
@@ -1060,27 +1113,48 @@
     grads[HD:] = jnp.zeros((2 * HD, 2048), F32)
     for query_at in range(0, 2048, 256):
         attend_back_block(qkv, start, o_true, lse, d_out, grads, query_at, 256)
-        if query_at == 768:
-            up_sum.hop()
-        if query_at == 1280:
-            down_sum.hop()
+        if query_at == 1536:
             out_sum.hop()
-        if query_at == 1792:
-            up_sum.hop()
+    for at in range(16):
+        put_stored(d_send.at[2], at, grads[2 * HD :])
+    swaps = [Swap(here, post, local, d_send.at[2], d_in.at[2])]
     position = lax.broadcasted_iota(jnp.int32, (1, 2048), 1) - start[...]
     cos_t, sin_t = turn_tables(position.astype(F32))
-    for part in range(2):
+    for part in (1, 0):
         first = grads[HD * part : HD * part + HD // 2]
         second = grads[HD * part + HD // 2 : HD * (part + 1)]
-        grads[HD * part : HD * part + HD // 2] = first * cos_t + second * sin_t
-        grads[HD * part + HD // 2 : HD * (part + 1)] = second * cos_t - first * sin_t
-    for at in range(16):
-        d_send[at // 4, :, 128 * (at % 4) : 128 * (at % 4) + 128] = stored_group(grads, at).astype(BF)
-    swap = SwapAlongZ(here, post, local, d_send, d_in)
-    out_sum.hop()
+        turned = jnp.concatenate([first * cos_t + second * sin_t, second * cos_t - first * sin_t], 0)
+        for at in range(16):
+            put_stored(d_send.at[part], at, turned)
+        swaps.append(Swap(here, post, local, d_send.at[part], d_in.at[part]))
+    up_sum.hop()
     low_half, high_half = down_sum.total()
     g_down[0:64] = low_half
     g_down[64:128] = high_half
+    out_sum.hop()
+    for number, part in enumerate((2, 1, 0)):
+        swaps[number].finish()
+        d_all[256 * part : 256 * (part + 1)] = d_in[part].reshape(256, 512)
+        for block in range(SPOTS):
+            term = dot(
+                a_t[ROWS * block : ROWS * (block + 1)], d_all[256 * part : 256 * (part + 1)], 1, 1
+            )
+            qkv_parts[part, block // 2, block % 2] = term.astype(BF).reshape(2, 64, 256)
+        qkv_sums[part].hop()
+    wqkv_flat = [wqkv[part].reshape(WIDTH, 256) for part in range(3)]
+
+    def in_half(low):
+        terms = [
+            dot(d_all[256 * part : 256 * (part + 1), half_lanes(low)], wqkv_flat[part], 0, 1)
+            for part in range(3)
+        ]
+        return terms[0] + terms[1] + terms[2]
+
+    sums[3].give(0, in_half(1 - here.low))
+    sums[3].give(1, in_half(here.low))
+    sums[3].cross()
+    for part in (2, 1, 0):
+        qkv_sums[part].hop()
     low_half, high_half = up_sum.total()
     for member in range(GROUP):
         halved = low_half if member < 2 else high_half
@@ -1089,23 +1163,6 @@
     ends = []
     for member, place in here.mates():
         ends.append((post.send(up_send.at[member], up_got.at[here.member], place), up_got.at[member]))
-    out_sum.hop()
-    swap.finish()
-    for part in range(3):
-        for head in range(4):
-            at = 256 * part + HD * head
-            d_all[at : at + HD] = d_in[head, HD * part : HD * (part + 1)]
-    for shard in range(SPOTS):
-        qkv_parts[shard] = dot(a_t[ROWS * shard : ROWS * (shard + 1)], d_all[...], 1, 1).astype(BF)
-    qkv_sum.hop()
-
-    def in_half(y):
-        return dot(d_all[:, half_lanes(y)], wqkv_flat, 0, 1)
-
-    sums[3].give(0, in_half(1 - here.y))
-    sums[3].give(1, in_half(here.y))
-    sums[3].cross()
-    qkv_sum.hop()
     low_half, high_half = out_sum.total()
     out_end[0:16] = low_half.astype(BF)
     out_end[16:32] = high_half.astype(BF)
@@ -1125,14 +1182,18 @@
     d_vec[0:1] = jnp.sum(d_a * normed, 0, keepdims=True)
     d_vec[1:2] = jnp.sum(d_a, 0, keepdims=True)
     for shard in range(SPOTS):
-        vec_send[shard] = d_vec[:, ROWS * shard : ROWS * (shard + 1)]
+        at = 256 * (shard // 2) + 64 * (shard % 2)
+        vec_send[shard] = jnp.concatenate(
+            [d_vec[:, at : at + 64], d_vec[:, at + ROWS : at + ROWS + 64]], 1
+        )
     vec_in[here.shard] = vec_send[here.shard]
     vec_sent = []
     for step in range(1, SPOTS):
         shard, place = here.plane(step)
         came = lax.rem(here.shard + SPOTS - step, SPOTS)
         vec_sent.append((post.send(vec_send.at[shard], vec_in.at[here.shard], place), vec_in.at[came]))
-    qkv_sum.hop()
+    for part in (2, 1, 0):
+        qkv_sums[part].hop()
     for sent, landing in vec_sent:
         post.arrived(sent, landing)
     total = vec_in[0]
@@ -1143,7 +1204,6 @@
     for member, place in here.mates():
         mine = vec_group.at[here.member]
         vec_sent.append((post.send(mine, mine, place), vec_group.at[member]))
-    qkv_sum.hop()
     for sent, landing in ends:
         post.arrived(sent, landing)
 
@@ -1159,14 +1219,16 @@
     for member in range(1, GROUP):
         mine = jnp.where(here.member == member, total[:, 32 * member : 32 * (member + 1)], mine)
     g_vec[...] = mine
-    low_half, high_half = qkv_sum.total()
-    for member in range(GROUP):
-        halved = low_half if member < 2 else high_half
-        qkv_end[member] = halved[32 * (member % 2) : 32 * (member % 2) + 32].astype(BF)
-    qkv_got[here.member] = qkv_end[here.member]
     ends = []
-    for member, place in here.mates():
-        ends.append((post.send(qkv_end.at[member], qkv_got.at[here.member], place), qkv_got.at[member]))
+    for part in (2, 1, 0):
+        low_half, high_half = qkv_sums[part].total()
+        for member in range(GROUP):
+            halved = low_half if member < 2 else high_half
+            qkv_end[part, member] = halved[32 * (member % 2) : 32 * (member % 2) + 32].astype(BF)
+        qkv_got[part, here.member] = qkv_end[part, here.member]
+        for member, place in here.mates():
+            sent = post.send(qkv_end.at[part, member], qkv_got.at[part, here.member], place)
+            ends.append((sent, qkv_got.at[part, member]))
     for sent, landing in ends:
         post.arrived(sent, landing)
     post.finish()
@@ -1189,34 +1251,34 @@
             shape((ROWS, WIDTH), F32),
             shape((ROWS, WIDTH), F32),
             shape((GROUP, 32, WIDTH), BF),
-            shape((GROUP, 32, 768), BF),
+            shape((3, GROUP, 32, 256), BF),
             shape((32, WIDTH), BF),
             shape((8, 32), F32),
         ],
-        in_specs=[anywhere] * 9 + [vmem] * 8,
+        in_specs=[anywhere] * 17,
         out_specs=[vmem] * 7,
         scratch_shapes=[
             held(ROWS, WIDTH), held(ROWS, WIDTH), held(3, 32, WIDTH), held(32, 4 * WIDTH),
-            held(1, ROWS, kind=jnp.int32),
-            held(*rows), held(SPOTS, ROWS, 768), held(GROUP, 32, 768), held(GROUP, 32, WIDTH),
-            held(ROWS, WIDTH), held(GROUP, 16, ROWS, kind=F32), held(SPOTS, 16, ROWS, kind=F32),
-            held(32, WIDTH), held(SPOTS, 32, WIDTH), held(SPOTS, ROWS, WIDTH), held(SPOTS, ROWS, WIDTH),
+            held(1, ROWS, kind=jnp.int32), held(8, 1, 32),
+            held(*rows), held(3, 4, 2, 2, 64, 256), held(3, GROUP, 32, 256), held(GROUP, 32, WIDTH),
+            held(GROUP, 16, ROWS, kind=F32), held(SPOTS, 16, ROWS, kind=F32),
+            held(32, WIDTH), held(SPOTS, 2, 16, WIDTH), held(4, 2, 2, 64, WIDTH), held(SPOTS, 2, 64, WIDTH),
             held(8, WIDTH, kind=F32), held(16, ROWS, kind=F32), held(1, 2048, kind=jnp.int32),
-            held(WIDTH, 512), held(4, 192, 512), held(4, 192, 512), held(192, 2048),
+            held(WIDTH, 512), held(3, 4, HD, 512), held(3, 4, HD, 512), held(192, 2048),
             held(HD, 2048, kind=F32), held(1, 2048, kind=F32), held(4, HD, 512), held(4, HD, 512),
             held(*rows), held(*rows), held(*rows), held(*rows), held(*rows, kind=F32), held(*rows),
             held(3, ROWS, WIDTH, kind=F32),
             held(4, 2, ROWS, WIDTH), held(4, 2, ROWS, WIDTH), held(4, ROWS, WIDTH), held(4, ROWS, WIDTH),
             held(2, 2, ROWS, WIDTH, kind=F32),
             held(4, HD, 512), held(4, HD, 512), held(HD, 2048), held(192, 2048, kind=F32),
-            held(4, 192, 512), held(4, 192, 512), held(768, 512),
-            held(SPOTS, ROWS, WIDTH), held(14, ROWS // 2, WIDTH),
-            held(SPOTS, ROWS, WIDTH), held(14, ROWS // 2, WIDTH),
-            held(SPOTS, 32, WIDTH), held(14, 16, WIDTH),
-            held(SPOTS, ROWS, 768), held(14, ROWS // 2, 768),
+            held(3, 4, HD, 512), held(3, 4, HD, 512), held(768, 512),
+            held(SPOTS, 2, 64, WIDTH), held(14, 64, WIDTH),
+            held(4, 2, 2, 64, WIDTH), held(14, 64, WIDTH),
+            held(SPOTS, 2, 16, WIDTH), held(14, 16, WIDTH),
+            held(3, 4, 2, 2, 64, 256), held(3, 14, 64, 256),
             held(SPOTS, 8, ROWS, kind=F32), held(SPOTS, 8, ROWS, kind=F32), held(GROUP, 8, ROWS, kind=F32),
-            held(8, WIDTH, kind=F32), held(GROUP, 32, WIDTH), held(GROUP, 32, 768), held(32, WIDTH),
-            dma((200,)), dma((200,)), dma((24,)), dma((5,)),
+            held(8, WIDTH, kind=F32), held(GROUP, 32, WIDTH), held(3, GROUP, 32, 256), held(32, WIDTH),
+            dma((300,)), dma((300,)), dma((40,)), dma((5,)),
         ],
         compiler_params=pltpu.CompilerParams(
             collective_id=0, has_side_effects=True, vmem_limit_bytes=VMEM_BYTES
@@ -1235,11 +1297,11 @@
     g_out[...] = out_got[...].astype(F32)
     for member in range(GROUP):
         for shard in range(SPOTS):
-            at = 512 * shard + 128 * member
+            at = ROWS * device_of(shard, member)
             g_up[:, at : at + 128] = up_got[member, :, 128 * shard : 128 * (shard + 1)].astype(F32)
-        base = 512 * (member % 2) + 256 * (member // 2)
+        base = 256 * member
         for slot, out in enumerate((g_q, g_k, g_v)):
-            out[:, base : base + 256] = qkv_got[member, :, 256 * slot : 256 * (slot + 1)].astype(F32)
+            out[:, base : base + 256] = qkv_got[slot, member].astype(F32)
     for row, out in enumerate(g_norms):
         out[...] = vec[row : row + 1]
 
@@ -1256,7 +1318,7 @@
         ] + [shape((1, 32), F32)] * 8,
         in_specs=[vmem] * 7,
         out_specs=[vmem] * 16,
-        compiler_params=pltpu.CompilerParams(vmem_limit_bytes=VMEM_BYTES // 2),
+        compiler_params=pltpu.CompilerParams(vmem_limit_bytes=VMEM_BYTES),
         name="finish",
     )(*args)
 

time: 233 us -> 215 us (0.923)
  Pallas kernels: 225 us -> 214 us
  local copies, waits for them, and re-layouts: 6.41 us -> 0 us
    pallas_call x1, Pallas kernels: 224 us -> 211 us  [call_layer(): pl.pallas_call(layer_kernel, out_shape=[shape((ROWS, WIDTH), BF), shape((...]
    unnamed x14 -> x0, local copies, waits for them, and re-layouts: 6.41 us -> none
where the time goes in v3:
time: 215 us
  Pallas kernels  214 us (100%)
    pallas_call x1, Pallas kernels, call_layer(): pl.pallas_call(layer_kernel, out_shape=[shape((ROWS, WIDTH), BF), shape((...  211 us

profile of v3, /device:TPU:0, one launch (start us, length us, event | category | flops | bytes accessed | tf_op | source)
XLA Modules:
  0.0 214.7 jit_solution(11600824916924169943)
XLA Ops:
  0.7 211.0 %layer.1 = (bf16[128,1024]{1,0:T(8,128)(2,1)}, f32[128,1024]{1,0:T(8,128)}, f32[128,1024]{1,0:T(8,128)}, bf16[4,32,1024]{2,1,0:T(8,128)(2,1)}, bf16[3,4,32,256]{...) custom-call(bf16[128,1024]{1,0:T(8,128)(2,1)} %bitcast.20, s32[1,128]{1,0:T(1,128)} %seg_hbm.1, ...), custom_call_target="tpu_custom_call" | custom-call | tf_op jit(solution)/shard_map/layer/pallas_call | solution.py:1247
  211.6 2.9 %finish.1 = (bf16[128,1024]{1,0:T(8,128)(2,1)}, f32[128,1024]{1,0:T(8,128)}, f32[32,1024]{1,0:T(8,128)}, f32[32,1024]{1,0:T(8,128)}, f32[32,1024]{1,0:T(8,128)},...) custom-call(bf16[128,1024]{1,0:T(8,128)(2,1)} %get-tuple-element.39., ...), custom_call_target="tpu_custom_call" | custom-call | tf_op jit(solution)/shard_map/finish/pallas_call | solution.py:1313

commit v4 on v3

--- a/solution.py
+++ b/solution.py
@@ -486,9 +486,13 @@
         return copy
 
 
+OTHER = {"x": "y", "y": "x"}
+
+
 class CubeGather:
-    def __init__(self, here, post, held, piece, own=None):
+    def __init__(self, here, post, held, piece, own=None, corner_ways="yx"):
         self.here, self.post, self.held, self.piece, self.own = here, post, held, piece, own
+        self.corner_ways = corner_ways
         self.waiting = {}
 
     def move(self, axes, half, way):
@@ -502,16 +506,15 @@
     def take(self, axes, half):
         self.post.arrived(*self.waiting.pop((axes, half)))
 
-    def start(self, ways="zxy"):
+    def start(self, ways="zxy", halves=(0, 1)):
         for way in ways:
-            for half in (0, 1):
+            for half in halves:
                 self.move("", half, way)
 
     def corners(self):
-        self.take("x", 0)
-        self.move("x", 0, "y")
-        self.take("y", 1)
-        self.move("y", 1, "x")
+        for half, way in enumerate(self.corner_ways):
+            self.take(OTHER[way], half)
+            self.move(OTHER[way], half, way)
 
     def spread(self):
         for half in (0, 1):
@@ -520,10 +523,9 @@
             self.move("z", half, "y")
 
     def last(self):
-        self.take("xz", 0)
-        self.move("xz", 0, "y")
-        self.take("yz", 1)
-        self.move("yz", 1, "x")
+        for half, way in enumerate(self.corner_ways):
+            self.take(OTHER[way] + "z", half)
+            self.move(OTHER[way] + "z", half, way)
 
     def finish(self):
         for key in list(self.waiting):
@@ -531,8 +533,9 @@
 
 
 class CubeSum:
-    def __init__(self, here, post, parts, piece, landing):
+    def __init__(self, here, post, parts, piece, landing, corner_ways="yx"):
         self.here, self.post, self.parts, self.piece, self.landing = here, post, parts, piece, landing
+        self.corner_ways = corner_ways
         self.waiting = {}
         self.slots = 0
         self.hops = 0
@@ -560,14 +563,15 @@
         self.hops += 1
         if self.hops == 1:
             for axes in ("xyz", "xy"):
-                self.move(axes, 0, "y")
-                self.move(axes, 1, "x")
+                for half, way in enumerate(self.corner_ways):
+                    self.move(axes, half, way)
+            for axes in ("z", ""):
+                for half, way in enumerate(self.corner_ways):
+                    self.move(way + axes, half, way)
         if self.hops == 2:
             for axes in ("z", ""):
-                self.move("x" + axes, 1, "x")
-                self.move("y" + axes, 0, "y")
-                self.move("x" + axes, 0, "x")
-                self.move("y" + axes, 1, "y")
+                for half, way in enumerate(self.corner_ways):
+                    self.move(OTHER[way] + axes, half, OTHER[way])
         if self.hops == 3:
             self.move("z", 0, "z")
             self.move("z", 1, "z")
@@ -583,30 +587,32 @@
         return halves
 
 
+HALVES = (slice(0, 64), slice(64, 128))
+
+
 class GroupGather:
     def __init__(self, here, post, held):
         self.here, self.post, self.held = here, post, held
-        self.over = []
+        self.over, self.core, self.passed = [], [], []
+
+    def put(self, half):
+        mine = self.piece(self.here.member, half)
+        self.over.append(self.post.send(mine, mine, self.here.link_mate))
+        self.core.append(self.post.send(mine, mine, self.here.core_mate))
+
+    def piece(self, member, half):
+        return self.held.at[member, HALVES[half]]
+
+    def near(self):
         for half in (0, 1):
-            mine = self.piece(here.member, half)
-            self.over.append(post.send(mine, mine, here.link_mate))
-        mine = held.at[here.member]
-        self.core = post.send(mine, mine, here.core_mate)
-
-    def piece(self, member, half):
-        return self.held.at[member, pl.ds(64 * half, 64)]
-
-    def near(self):
-        self.post.arrived(self.core, self.held.at[self.here.core_member])
-
-    def rest(self):
-        here, passed = self.here, []
-        for half in (0, 1):
-            linked = self.piece(here.link_member, half)
-            self.post.arrived(self.over[half], linked)
-            passed.append(self.post.send(linked, linked, here.core_mate))
-        for half in (0, 1):
-            self.post.arrived(passed[half], self.piece(here.far_member, half))
+            self.post.arrived(self.core[half], self.piece(self.here.core_member, half))
+
+    def rest(self, half):
+        here = self.here
+        linked = self.piece(here.link_member, half)
+        self.post.arrived(self.over[half], linked)
+        passed = self.post.send(linked, linked, here.core_mate)
+        self.post.arrived(passed, self.piece(here.far_member, half))
 
 
 class GroupSum:
@@ -615,27 +621,33 @@
         self.near_send, self.near_in = near_send, near_in
         self.far_send, self.far_in = far_send, far_in
         self.terms = terms
-        self.near = [None, None]
-
-    def give(self, slot, value):
+        self.near, self.far = {}, {}
+
+    def give(self, slot, half, value):
         here = self.here
-        self.terms[slot] = value.reshape(2, ROWS, WIDTH)
-        self.near_send[slot] = self.terms[slot, 1 - here.c].astype(BF)
-        self.near[slot] = self.post.send(
-            self.near_send.at[slot], self.near_in.at[slot], here.core_mate
+        self.terms[slot, :, HALVES[half]] = value.reshape(2, 64, WIDTH)
+        self.near_send[slot, half] = self.terms[slot, 1 - here.c, HALVES[half]].astype(BF)
+        self.near[slot, half] = self.post.send(
+            self.near_send.at[slot, half], self.near_in.at[slot, half], here.core_mate
         )
 
-    def cross(self):
+    def give_all(self, slot, value):
+        value = value.reshape(2, ROWS, WIDTH)
+        for half in (0, 1):
+            self.give(slot, half, value[:, HALVES[half]])
+
+    def cross(self, half):
         here = self.here
-        self.post.arrived(self.near[0], self.near_in.at[0])
-        self.far_send[...] = (self.terms[0, here.c] + self.near_in[0].astype(F32)).astype(BF)
-        self.far = self.post.send(self.far_send, self.far_in, here.link_mate)
-
-    def total(self):
-        self.post.arrived(self.near[1], self.near_in.at[1])
-        value = self.terms[1, self.here.c] + self.near_in[1].astype(F32)
-        self.post.arrived(self.far, self.far_in)
-        return value + self.far_in[...].astype(F32)
+        self.post.arrived(self.near[0, half], self.near_in.at[0, half])
+        value = self.terms[0, here.c, HALVES[half]] + self.near_in[0, half].astype(F32)
+        self.far_send[half] = value.astype(BF)
+        self.far[half] = self.post.send(self.far_send.at[half], self.far_in.at[half], here.link_mate)
+
+    def total(self, half):
+        self.post.arrived(self.near[1, half], self.near_in.at[1, half])
+        value = self.terms[1, self.here.c, HALVES[half]] + self.near_in[1, half].astype(F32)
+        self.post.arrived(self.far[half], self.far_in.at[half])
+        return value + self.far_in[half].astype(F32)
 
 
 class Swap:
@@ -857,6 +869,8 @@
     down_ring = CubeGather(here, post, wd_all, row_piece, lambda half: wd.at[pl.ds(64 * half, 64)])
     down_ring.start("xy")
     x_gather = GroupGather(here, post, x_all)
+    x_gather.put(0)
+    x_gather.put(1)
     wo_copy = pltpu.make_async_remote_copy(
         src_ref=wo, dst_ref=wo_in, send_sem=self_sems.at[0], recv_sem=self_sems.at[1],
         device_id=here.place(*out_to), device_id_type=MESH_ID,
@@ -914,7 +928,8 @@
     put_a(here.core_member)
     for ring in qkv_rings:
         ring.corners()
-    x_gather.rest()
+    x_gather.rest(0)
+    x_gather.rest(1)
 
     @pl.when(out_moves)
     def _():
@@ -982,16 +997,15 @@
         for group in range(16):
             at = slice(ROWS * group, ROWS * (group + 1))
             qkv[HD * part : HD * (part + 1), at] = true_group(qkv_heads.at[part], group)
-    up_ring.start("z")
     up_ring.corners()
     for query_at in range(0, 2048, 512):
         attend_block(qkv, start, o_true, lse, query_at, 512, 512)
     for at in range(16):
         put_stored(o_send, at, o_true)
     swap = Swap(here, post, local, o_send, o_all)
+    up_ring.start("z")
     down_ring.last()
     out_ring.last()
-    up_ring.spread()
     out_ring.finish()
     swap.finish()
 
@@ -1008,95 +1022,126 @@
         heads = [o_all[group, :, half_lanes(low)] for group in range(4)]
         return dot(jnp.concatenate(heads, 0), wo_flat, 0, 0)
 
-    sums[0].give(0, out_half(1 - here.low))
-    sums[0].give(1, out_half(here.low))
-    sums[0].cross()
+    sums[0].give_all(0, out_half(1 - here.low))
+    sums[0].give_all(1, out_half(here.low))
+    sums[0].cross(0)
+    sums[0].cross(1)
+    up_ring.spread()
     up_ring.last()
-    branch = sums[0].total()
-    t_normed, t_inv = norm_parts(branch)
-    hres = tok[...].astype(F32) + t_normed * vectors[2:3] + vectors[3:4]
-    res[0] = t_normed
-    h_normed, h_inv = norm_parts(hres)
-    res[1] = h_normed
-    res[2] = hres
-    c_all[here.member] = (h_normed * vectors[4:5] + vectors[5:6]).astype(BF)
+    t_inv, h_inv = [None, None], [None, None]
     gather = GroupGather(here, post, c_all)
+    for part, rows in enumerate(HALVES):
+        t_normed, t_inv[part] = norm_parts(sums[0].total(part))
+        hres = tok[rows].astype(F32) + t_normed * vectors[2:3] + vectors[3:4]
+        res[0, rows] = t_normed
+        h_normed, h_inv[part] = norm_parts(hres)
+        res[1, rows] = h_normed
+        res[2, rows] = hres
+        c_all[here.member, rows] = (h_normed * vectors[4:5] + vectors[5:6]).astype(BF)
+        gather.put(part)
     gather.near()
     up_ring.finish()
     wu_flat = wu_all[...].reshape(WIDTH, WIDTH)
 
-    def half(held, low):
-        return held[pl.ds(2 * low, 2)].reshape(2 * ROWS, WIDTH)
-
-    def up_half(low):
-        gl, slope = gelu_and_slope(dot(half(c_all, low), wu_flat, 1, 0))
-        gl_all[pl.ds(2 * low, 2)] = gl.astype(BF).reshape(2, ROWS, WIDTH)
-        slope_all[pl.ds(2 * low, 2)] = slope.reshape(2, ROWS, WIDTH)
-
-    up_half(here.low)
-    for load in load_wd:
-        load.wait()
-    down_ring.finish()
-    wd_flat = wd_all[...].reshape(WIDTH, WIDTH)
-    sums[1].give(1, dot(half(gl_all, here.low), wd_flat, 1, 0))
-    gather.rest()
-    up_half(1 - here.low)
-    sums[1].give(0, dot(half(gl_all, 1 - here.low), wd_flat, 1, 0))
-    sums[1].cross()
-    branch = sums[1].total()
-    m_normed, m_inv = norm_parts(branch)
-    act[...] = (res[2] + m_normed * vectors[6:7] + vectors[7:8]).astype(BF)
+    def pair(held, low, rows=slice(0, ROWS)):
+        value = held[pl.ds(2 * low, 2), rows]
+        return value.reshape(-1, WIDTH)
+
+    def set_pair(held, low, rows, value):
+        held[pl.ds(2 * low, 2), rows] = value.reshape(2, -1, WIDTH)
+
+    whole = slice(0, ROWS)
+
+    def up_rows(low, rows):
+        gl, slope = gelu_and_slope(dot(pair(c_all, low, rows), wu_flat, 1, 0))
+        set_pair(gl_all, low, rows, gl.astype(BF))
+        set_pair(slope_all, low, rows, slope)
+
+    up_rows(here.low, whole)
+    for part, rows in enumerate(HALVES):
+        gather.rest(part)
+        up_rows(1 - here.low, rows)
+        if part == 0:
+            for load in load_wd:
+                load.wait()
+            down_ring.finish()
+            wd_flat = wd_all[...].reshape(WIDTH, WIDTH)
+        sums[1].give(0, part, dot(pair(gl_all, 1 - here.low, rows), wd_flat, 1, 0))
+        sums[1].cross(part)
+    sums[1].give_all(1, dot(pair(gl_all, here.low), wd_flat, 1, 0))
     load_cot.wait()
-    upstream = cot[...].astype(F32)
-    dm_all[here.member] = norm_pull(m_normed, m_inv, vectors[6:7], upstream).astype(BF)
     gather = GroupGather(here, post, dm_all)
-    d_vec[6:7] = jnp.sum(upstream * m_normed, 0, keepdims=True)
-    d_vec[7:8] = jnp.sum(upstream, 0, keepdims=True)
+    d_gain, d_bias = 0.0, 0.0
+    for part, rows in enumerate(HALVES):
+        m_normed, m_inv = norm_parts(sums[1].total(part))
+        upstream = cot[rows].astype(F32)
+        dm_all[here.member, rows] = norm_pull(m_normed, m_inv, vectors[6:7], upstream).astype(BF)
+        gather.put(part)
+        act[rows] = (res[2, rows] + m_normed * vectors[6:7] + vectors[7:8]).astype(BF)
+        d_gain = d_gain + jnp.sum(upstream * m_normed, 0, keepdims=True)
+        d_bias = d_bias + jnp.sum(upstream, 0, keepdims=True)
+    d_vec[6:7] = d_gain
+    d_vec[7:8] = d_bias
     gather.near()
 
-    def du_half(low):
-        d_gl = dot(half(dm_all, low), wd_flat, 1, 1)
-        slope = slope_all[pl.ds(2 * low, 2)].reshape(2 * ROWS, WIDTH)
-        du_all[pl.ds(2 * low, 2)] = (d_gl * slope).astype(BF).reshape(2, ROWS, WIDTH)
-
-    du_half(here.low)
-    sums[2].give(1, dot(half(du_all, here.low), wu_flat, 1, 1))
-    gather.rest()
-    du_half(1 - here.low)
-    sums[2].give(0, dot(half(du_all, 1 - here.low), wu_flat, 1, 1))
-    sums[2].cross()
-    gl_flat = gl_all[...].reshape(512, WIDTH)
-    dm_flat = dm_all[...].reshape(512, WIDTH)
-    for shard in range(SPOTS):
-        term = dot(gl_flat[:, ROWS * shard : ROWS * (shard + 1)], dm_flat, 0, 0)
-        down_parts[shard] = term.astype(BF).reshape(2, 64, WIDTH)
+    def du_rows(low, rows):
+        d_gl = dot(pair(dm_all, low, rows), wd_flat, 1, 1)
+        set_pair(du_all, low, rows, (d_gl * pair(slope_all, low, rows)).astype(BF))
+
+    def put_down(axes):
+        shard = here.across(axes)[0]
+        gl = gl_all[:, :, pl.ds(pl.multiple_of(ROWS * shard, ROWS), ROWS)].reshape(512, ROWS)
+        down_parts[shard] = dot(gl, dm_flat, 0, 0).astype(BF).reshape(2, 64, WIDTH)
+
     down_sum = CubeSum(here, post, down_parts, row_piece, down_in)
+    du_rows(here.low, whole)
+    sums[2].give_all(1, dot(pair(du_all, here.low), wu_flat, 1, 1))
+    for part, rows in enumerate(HALVES):
+        gather.rest(part)
+        if part == 1:
+            dm_flat = dm_all[...].reshape(512, WIDTH)
+            for axes in ("xyz", "xy", "xz", "yz", "x", "y"):
+                put_down(axes)
+            down_sum.hop()
+        du_rows(1 - here.low, rows)
+        sums[2].give(0, part, dot(pair(du_all, 1 - here.low, rows), wu_flat, 1, 1))
+        if part == 0:
+            sums[2].cross(part)
+    sums[2].cross(1)
+    for axes in ("", "z"):
+        put_down(axes)
     up_sum = CubeSum(here, post, up_parts, group_piece, up_in)
     out_sum = CubeSum(here, post, out_parts, row_piece, out_in)
     qkv_sums = [
         CubeSum(here, post, qkv_parts.at[part], group_piece, qkv_in.at[part]) for part in range(3)
     ]
-    down_sum.hop()
     du_flat = du_all[...].reshape(512, WIDTH)
     c_flat = c_all[...].reshape(512, WIDTH)
+    down_sum.hop()
     for block in range(SPOTS):
         term = dot(c_flat[:, ROWS * block : ROWS * (block + 1)], du_flat, 0, 0)
         up_parts[block // 2, block % 2] = term.astype(BF).reshape(2, 64, WIDTH)
     up_sum.hop()
-    d_c = sums[2].total()
-    h_normed = res[1]
-    d_h = upstream + norm_pull(h_normed, h_inv, vectors[4:5], d_c)
-    t_normed = res[0]
-    dt_all[here.member] = norm_pull(t_normed, t_inv, vectors[2:3], d_h).astype(BF)
     gather = GroupGather(here, post, dt_all)
-    d_vec[4:5] = jnp.sum(d_c * h_normed, 0, keepdims=True)
-    d_vec[5:6] = jnp.sum(d_c, 0, keepdims=True)
-    d_vec[2:3] = jnp.sum(d_h * t_normed, 0, keepdims=True)
-    d_vec[3:4] = jnp.sum(d_h, 0, keepdims=True)
-    res[2] = d_h
+    d_mi = [0.0, 0.0]
+    d_ao = [0.0, 0.0]
+    for part, rows in enumerate(HALVES):
+        d_c = sums[2].total(part)
+        h_normed, t_normed = res[1, rows], res[0, rows]
+        d_h = cot[rows].astype(F32) + norm_pull(h_normed, h_inv[part], vectors[4:5], d_c)
+        dt_all[here.member, rows] = norm_pull(t_normed, t_inv[part], vectors[2:3], d_h).astype(BF)
+        gather.put(part)
+        res[2, rows] = d_h
+        d_mi[0] = d_mi[0] + jnp.sum(d_c * h_normed, 0, keepdims=True)
+        d_mi[1] = d_mi[1] + jnp.sum(d_c, 0, keepdims=True)
+        d_ao[0] = d_ao[0] + jnp.sum(d_h * t_normed, 0, keepdims=True)
+        d_ao[1] = d_ao[1] + jnp.sum(d_h, 0, keepdims=True)
+    d_vec[4:5], d_vec[5:6] = d_mi
+    d_vec[2:3], d_vec[3:4] = d_ao
     down_sum.hop()
     gather.near()
-    gather.rest()
+    gather.rest(0)
+    gather.rest(1)
     dt_flat = dt_all[...].reshape(512, WIDTH)
     d_o = dot(wo_flat, dt_flat, 1, 1)
     for head in range(4):
@@ -1104,10 +1149,9 @@
     swap = Swap(here, post, local, do_send, do_heads)
     o_flat = o_all[...].reshape(256, 512)
     out_parts[...] = dot(o_flat, dt_flat, 1, 0).astype(BF).reshape(SPOTS, 2, 16, WIDTH)
+    out_sum.hop()
     up_sum.hop()
-    out_sum.hop()
     swap.finish()
-    down_sum.hop()
     for group in range(16):
         d_out[:, ROWS * group : ROWS * (group + 1)] = true_group(do_heads, group)
     grads[HD:] = jnp.zeros((2 * HD, 2048), F32)
@@ -1127,13 +1171,14 @@
         for at in range(16):
             put_stored(d_send.at[part], at, turned)
         swaps.append(Swap(here, post, local, d_send.at[part], d_in.at[part]))
-    up_sum.hop()
     low_half, high_half = down_sum.total()
     g_down[0:64] = low_half
     g_down[64:128] = high_half
-    out_sum.hop()
     for number, part in enumerate((2, 1, 0)):
         swaps[number].finish()
+        if number == 2:
+            up_sum.hop()
+            out_sum.hop()
         d_all[256 * part : 256 * (part + 1)] = d_in[part].reshape(256, 512)
         for block in range(SPOTS):
             term = dot(
@@ -1141,6 +1186,9 @@
             )
             qkv_parts[part, block // 2, block % 2] = term.astype(BF).reshape(2, 64, 256)
         qkv_sums[part].hop()
+        if number:
+            qkv_sums[part + 1].hop()
+    qkv_sums[2].hop()
     wqkv_flat = [wqkv[part].reshape(WIDTH, 256) for part in range(3)]
 
     def in_half(low):
@@ -1150,11 +1198,12 @@
         ]
         return terms[0] + terms[1] + terms[2]
 
-    sums[3].give(0, in_half(1 - here.low))
-    sums[3].give(1, in_half(here.low))
-    sums[3].cross()
-    for part in (2, 1, 0):
-        qkv_sums[part].hop()
+    sums[3].give_all(0, in_half(1 - here.low))
+    sums[3].give_all(1, in_half(here.low))
+    sums[3].cross(0)
+    sums[3].cross(1)
+    qkv_sums[0].hop()
+    qkv_sums[1].hop()
     low_half, high_half = up_sum.total()
     for member in range(GROUP):
         halved = low_half if member < 2 else high_half
@@ -1176,11 +1225,15 @@
     def _():
         out_got[...] = out_end[...]
 
-    d_a = sums[3].total()
-    normed, inv_std = norm_parts(tok[...].astype(F32))
-    in_grad[...] = res[2] + norm_pull(normed, inv_std, vectors[0:1], d_a)
-    d_vec[0:1] = jnp.sum(d_a * normed, 0, keepdims=True)
-    d_vec[1:2] = jnp.sum(d_a, 0, keepdims=True)
+    d_gain, d_bias = 0.0, 0.0
+    for part, rows in enumerate(HALVES):
+        d_a = sums[3].total(part)
+        normed, inv_std = norm_parts(tok[rows].astype(F32))
+        in_grad[rows] = res[2, rows] + norm_pull(normed, inv_std, vectors[0:1], d_a)
+        d_gain = d_gain + jnp.sum(d_a * normed, 0, keepdims=True)
+        d_bias = d_bias + jnp.sum(d_a, 0, keepdims=True)
+    d_vec[0:1] = d_gain
+    d_vec[1:2] = d_bias
     for shard in range(SPOTS):
         at = 256 * (shard // 2) + 64 * (shard % 2)
         vec_send[shard] = jnp.concatenate(
@@ -1192,8 +1245,7 @@
         shard, place = here.plane(step)
         came = lax.rem(here.shard + SPOTS - step, SPOTS)
         vec_sent.append((post.send(vec_send.at[shard], vec_in.at[here.shard], place), vec_in.at[came]))
-    for part in (2, 1, 0):
-        qkv_sums[part].hop()
+    qkv_sums[0].hop()
     for sent, landing in vec_sent:
         post.arrived(sent, landing)
     total = vec_in[0]
@@ -1212,13 +1264,6 @@
         out_copy.wait_recv()
         out_copy.wait_send()
 
-    for sent, landing in vec_sent:
-        post.arrived(sent, landing)
-    total = vec_group[0] + vec_group[1] + vec_group[2] + vec_group[3]
-    mine = total[:, 0:32]
-    for member in range(1, GROUP):
-        mine = jnp.where(here.member == member, total[:, 32 * member : 32 * (member + 1)], mine)
-    g_vec[...] = mine
     ends = []
     for part in (2, 1, 0):
         low_half, high_half = qkv_sums[part].total()
@@ -1229,6 +1274,13 @@
         for member, place in here.mates():
             sent = post.send(qkv_end.at[part, member], qkv_got.at[part, here.member], place)
             ends.append((sent, qkv_got.at[part, member]))
+    for sent, landing in vec_sent:
+        post.arrived(sent, landing)
+    total = vec_group[0] + vec_group[1] + vec_group[2] + vec_group[3]
+    mine = total[:, 0:32]
+    for member in range(1, GROUP):
+        mine = jnp.where(here.member == member, total[:, 32 * member : 32 * (member + 1)], mine)
+    g_vec[...] = mine
     for sent, landing in ends:
         post.arrived(sent, landing)
     post.finish()
@@ -1268,7 +1320,7 @@
             held(HD, 2048, kind=F32), held(1, 2048, kind=F32), held(4, HD, 512), held(4, HD, 512),
             held(*rows), held(*rows), held(*rows), held(*rows), held(*rows, kind=F32), held(*rows),
             held(3, ROWS, WIDTH, kind=F32),
-            held(4, 2, ROWS, WIDTH), held(4, 2, ROWS, WIDTH), held(4, ROWS, WIDTH), held(4, ROWS, WIDTH),
+            held(4, 2, 2, 64, WIDTH), held(4, 2, 2, 64, WIDTH), held(4, 2, 64, WIDTH), held(4, 2, 64, WIDTH),
             held(2, 2, ROWS, WIDTH, kind=F32),
             held(4, HD, 512), held(4, HD, 512), held(HD, 2048), held(192, 2048, kind=F32),
             held(3, 4, HD, 512), held(3, 4, HD, 512), held(768, 512),

time: 215 us -> 207 us (0.963)
  Pallas kernels: 214 us -> 206 us
    pallas_call x1, Pallas kernels: 211 us -> 203 us  [call_layer(): pl.pallas_call(layer_kernel, out_shape=[shape((ROWS, WIDTH), BF), shape((...]
where the time goes in v4:
time: 207 us
  Pallas kernels  206 us (100%)
    pallas_call x1, Pallas kernels, call_layer(): pl.pallas_call(layer_kernel, out_shape=[shape((ROWS, WIDTH), BF), shape((...  203 us

profile of v4, /device:TPU:0, one launch (start us, length us, event | category | flops | bytes accessed | tf_op | source)
XLA Modules:
  0.0 206.7 jit_solution(4731620746940527066)
XLA Ops:
  0.7 203.0 %layer.1 = (bf16[128,1024]{1,0:T(8,128)(2,1)}, f32[128,1024]{1,0:T(8,128)}, f32[128,1024]{1,0:T(8,128)}, bf16[4,32,1024]{2,1,0:T(8,128)(2,1)}, bf16[3,4,32,256]{...) custom-call(bf16[128,1024]{1,0:T(8,128)(2,1)} %bitcast.20, s32[1,128]{1,0:T(1,128)} %seg_hbm.1, ...), custom_call_target="tpu_custom_call" | custom-call | tf_op jit(solution)/shard_map/layer/pallas_call | solution.py:1299
  203.6 2.9 %finish.1 = (bf16[128,1024]{1,0:T(8,128)(2,1)}, f32[128,1024]{1,0:T(8,128)}, f32[32,1024]{1,0:T(8,128)}, f32[32,1024]{1,0:T(8,128)}, f32[32,1024]{1,0:T(8,128)},...) custom-call(bf16[128,1024]{1,0:T(8,128)(2,1)} %get-tuple-element.39., ...), custom_call_target="tpu_custom_call" | custom-call | tf_op jit(solution)/shard_map/finish/pallas_call | solution.py:1365

commit v5 on v4

--- a/solution.py
+++ b/solution.py
@@ -785,8 +785,9 @@
     tok_hbm, seg_hbm, cot_hbm, wq, wk, wv, wo, wu, wd, *rest
 ):
     norms_hbm = rest[:8]
-    act, in_grad, g_down, up_got, qkv_got, out_got, g_vec = rest[8:15]
+    act_hbm, in_grad_hbm, g_down_hbm, up_got, qkv_got, out_got, g_vec = rest[8:15]
     (
+        in_grad, g_down, act,
         tok, cot, wqkv_own, wu_own, seg_in, norms_in,
         x_all, wqkv, wqkv_send, wu_send, small_in, small_all, wo_in, wo_all, wu_all, wd_all,
         vectors, starts, start, a_t, qkv_send, qkv_heads, qkv, o_true, lse, o_send, o_all,
@@ -1080,6 +1081,7 @@
         act[rows] = (res[2, rows] + m_normed * vectors[6:7] + vectors[7:8]).astype(BF)
         d_gain = d_gain + jnp.sum(upstream * m_normed, 0, keepdims=True)
         d_bias = d_bias + jnp.sum(upstream, 0, keepdims=True)
+    writes = [local.copy(act, act_hbm)]
     d_vec[6:7] = d_gain
     d_vec[7:8] = d_bias
     gather.near()
@@ -1121,7 +1123,6 @@
     for block in range(SPOTS):
         term = dot(c_flat[:, ROWS * block : ROWS * (block + 1)], du_flat, 0, 0)
         up_parts[block // 2, block % 2] = term.astype(BF).reshape(2, 64, WIDTH)
-    up_sum.hop()
     gather = GroupGather(here, post, dt_all)
     d_mi = [0.0, 0.0]
     d_ao = [0.0, 0.0]
@@ -1138,7 +1139,6 @@
         d_ao[1] = d_ao[1] + jnp.sum(d_h, 0, keepdims=True)
     d_vec[4:5], d_vec[5:6] = d_mi
     d_vec[2:3], d_vec[3:4] = d_ao
-    down_sum.hop()
     gather.near()
     gather.rest(0)
     gather.rest(1)
@@ -1147,16 +1147,19 @@
     for head in range(4):
         do_send[head] = d_o[HD * head : HD * (head + 1)].astype(BF)
     swap = Swap(here, post, local, do_send, do_heads)
+    down_sum.hop()
     o_flat = o_all[...].reshape(256, 512)
     out_parts[...] = dot(o_flat, dt_flat, 1, 0).astype(BF).reshape(SPOTS, 2, 16, WIDTH)
+    up_sum.hop()
     out_sum.hop()
-    up_sum.hop()
     swap.finish()
     for group in range(16):
         d_out[:, ROWS * group : ROWS * (group + 1)] = true_group(do_heads, group)
     grads[HD:] = jnp.zeros((2 * HD, 2048), F32)
     for query_at in range(0, 2048, 256):
         attend_back_block(qkv, start, o_true, lse, d_out, grads, query_at, 256)
+        if query_at == 1024:
+            up_sum.hop()
         if query_at == 1536:
             out_sum.hop()
     for at in range(16):
@@ -1174,6 +1177,7 @@
     low_half, high_half = down_sum.total()
     g_down[0:64] = low_half
     g_down[64:128] = high_half
+    writes.append(local.copy(g_down, g_down_hbm))
     for number, part in enumerate((2, 1, 0)):
         swaps[number].finish()
         if number == 2:
@@ -1204,27 +1208,6 @@
     sums[3].cross(1)
     qkv_sums[0].hop()
     qkv_sums[1].hop()
-    low_half, high_half = up_sum.total()
-    for member in range(GROUP):
-        halved = low_half if member < 2 else high_half
-        up_send[member] = halved[32 * (member % 2) : 32 * (member % 2) + 32].astype(BF)
-    up_got[here.member] = up_send[here.member]
-    ends = []
-    for member, place in here.mates():
-        ends.append((post.send(up_send.at[member], up_got.at[here.member], place), up_got.at[member]))
-    low_half, high_half = out_sum.total()
-    out_end[0:16] = low_half.astype(BF)
-    out_end[16:32] = high_half.astype(BF)
-    out_copy = pltpu.make_async_remote_copy(
-        src_ref=out_end, dst_ref=out_got, send_sem=self_sems.at[3], recv_sem=self_sems.at[4],
-        device_id=here.place(*out_from), device_id_type=MESH_ID,
-    )
-    pl.when(out_moves)(out_copy.start)
-
-    @pl.when(out_stays)
-    def _():
-        out_got[...] = out_end[...]
-
     d_gain, d_bias = 0.0, 0.0
     for part, rows in enumerate(HALVES):
         d_a = sums[3].total(part)
@@ -1232,6 +1215,7 @@
         in_grad[rows] = res[2, rows] + norm_pull(normed, inv_std, vectors[0:1], d_a)
         d_gain = d_gain + jnp.sum(d_a * normed, 0, keepdims=True)
         d_bias = d_bias + jnp.sum(d_a, 0, keepdims=True)
+    writes.append(local.copy(in_grad, in_grad_hbm))
     d_vec[0:1] = d_gain
     d_vec[1:2] = d_bias
     for shard in range(SPOTS):
@@ -1256,15 +1240,27 @@
     for member, place in here.mates():
         mine = vec_group.at[here.member]
         vec_sent.append((post.send(mine, mine, place), vec_group.at[member]))
-    for sent, landing in ends:
-        post.arrived(sent, landing)
-
-    @pl.when(out_moves)
+    low_half, high_half = up_sum.total()
+    for member in range(GROUP):
+        halved = low_half if member < 2 else high_half
+        up_send[member] = halved[32 * (member % 2) : 32 * (member % 2) + 32].astype(BF)
+    up_got[here.member] = up_send[here.member]
+    ends = []
+    for member, place in here.mates():
+        ends.append((post.send(up_send.at[member], up_got.at[here.member], place), up_got.at[member]))
+    low_half, high_half = out_sum.total()
+    out_end[0:16] = low_half.astype(BF)
+    out_end[16:32] = high_half.astype(BF)
+    out_copy = pltpu.make_async_remote_copy(
+        src_ref=out_end, dst_ref=out_got, send_sem=self_sems.at[3], recv_sem=self_sems.at[4],
+        device_id=here.place(*out_from), device_id_type=MESH_ID,
+    )
+    pl.when(out_moves)(out_copy.start)
+
+    @pl.when(out_stays)
     def _():
-        out_copy.wait_recv()
-        out_copy.wait_send()
-
-    ends = []
+        out_got[...] = out_end[...]
+
     for part in (2, 1, 0):
         low_half, high_half = qkv_sums[part].total()
         for member in range(GROUP):
@@ -1281,8 +1277,16 @@
     for member in range(1, GROUP):
         mine = jnp.where(here.member == member, total[:, 32 * member : 32 * (member + 1)], mine)
     g_vec[...] = mine
+
+    @pl.when(out_moves)
+    def _():
+        out_copy.wait_recv()
+        out_copy.wait_send()
+
     for sent, landing in ends:
         post.arrived(sent, landing)
+    for write in writes:
+        write.wait()
     post.finish()
 
 
@@ -1308,8 +1312,9 @@
             shape((8, 32), F32),
         ],
         in_specs=[anywhere] * 17,
-        out_specs=[vmem] * 7,
+        out_specs=[anywhere] * 3 + [vmem] * 4,
         scratch_shapes=[
+            held(ROWS, WIDTH, kind=F32), held(ROWS, WIDTH, kind=F32), held(ROWS, WIDTH),
             held(ROWS, WIDTH), held(ROWS, WIDTH), held(3, 32, WIDTH), held(32, 4 * WIDTH),
             held(1, ROWS, kind=jnp.int32), held(8, 1, 32),
             held(*rows), held(3, 4, 2, 2, 64, 256), held(3, GROUP, 32, 256), held(GROUP, 32, WIDTH),

time: 207 us -> 203 us (0.981)
  Pallas kernels: 206 us -> 202 us
    pallas_call x1, Pallas kernels: 203 us -> 199 us  [call_layer(): pl.pallas_call(layer_kernel, out_shape=[shape((ROWS, WIDTH), BF), shape((...]
where the time goes in v5:
time: 203 us
  Pallas kernels  202 us (100%)
    pallas_call x1, Pallas kernels, call_layer(): pl.pallas_call(layer_kernel, out_shape=[shape((ROWS, WIDTH), BF), shape((...  199 us

profile of v5, /device:TPU:0, one launch (start us, length us, event | category | flops | bytes accessed | tf_op | source)
XLA Modules:
  0.0 203.2 jit_solution(6860641379052697168)
XLA Ops:
  0.7 199.4 %layer.1 = (bf16[128,1024]{1,0:T(8,128)(2,1)}, f32[128,1024]{1,0:T(8,128)}, f32[128,1024]{1,0:T(8,128)}, bf16[4,32,1024]{2,1,0:T(8,128)(2,1)}, bf16[3,4,32,256]{...) custom-call(bf16[128,1024]{1,0:T(8,128)(2,1)} %bitcast.20, s32[1,128]{1,0:T(1,128)} %seg_hbm.1, ...), custom_call_target="tpu_custom_call" | custom-call | tf_op jit(solution)/shard_map/layer/pallas_call | solution.py:1303
  200.1 2.9 %finish.1 = (bf16[128,1024]{1,0:T(8,128)(2,1)}, f32[128,1024]{1,0:T(8,128)}, f32[32,1024]{1,0:T(8,128)}, f32[32,1024]{1,0:T(8,128)}, f32[32,1024]{1,0:T(8,128)},...) custom-call(bf16[128,1024]{1,0:T(8,128)(2,1)} %get-tuple-element.39., ...), custom_call_target="tpu_custom_call" | custom-call | tf_op jit(solution)/shard_map/finish/pallas_call | solution.py:1370

commit v6 on v5

--- a/solution.py
+++ b/solution.py
@@ -965,6 +965,7 @@
     up_ring = CubeGather(here, post, wu_all, group_piece)
     for ring in qkv_rings:
         ring.last()
+    up_ring.start("x")
     swaps = []
     for part in range(3):
         qkv_rings[part].finish()
@@ -980,7 +981,7 @@
                 rows = rows * HD**-0.5
             qkv_send[part, head] = rows.astype(BF)
         swaps.append(Swap(here, post, local, qkv_send.at[part], qkv_heads.at[part]))
-    up_ring.start("xy")
+    up_ring.start("y")
     for group in range(16):
         a, b, cut = 2 * group, 2 * group + 1, slice(0, 64)
         if group >= 8:
@@ -1346,11 +1347,15 @@
 
 def finish_kernel(
     act_in, grad_in, down_in, up_got, qkv_got, out_got, vec,
-    act, in_grad, g_q, g_k, g_v, g_out, g_up, g_down, *g_norms
+    act, in_grad, g_q, g_k, g_v, g_out, g_up, g_down, *rest
 ):
-    act[...] = act_in[...]
-    in_grad[...] = grad_in[...]
-    g_down[...] = down_in[...]
+    g_norms, (held_grad, held_down, held_act), local = rest[:8], rest[8:11], Local(rest[11])
+    stages = ((grad_in, held_grad, in_grad), (down_in, held_down, g_down), (act_in, held_act, act))
+    loads = [local.copy(src, held) for src, held, _ in stages]
+    stores = []
+    for load, (_, held, dst) in zip(loads, stages):
+        load.wait()
+        stores.append(local.copy(held, dst))
     g_out[...] = out_got[...].astype(F32)
     for member in range(GROUP):
         for shard in range(SPOTS):
@@ -1361,10 +1366,13 @@
             out[:, base : base + 256] = qkv_got[slot, member].astype(F32)
     for row, out in enumerate(g_norms):
         out[...] = vec[row : row + 1]
+    for store in stores:
+        store.wait()
 
 
 def call_finish(*args):
     vmem = pl.BlockSpec(memory_space=pltpu.VMEM)
+    anywhere = pl.BlockSpec(memory_space=pl.ANY)
     shape = jax.ShapeDtypeStruct
     narrow = shape((32, WIDTH), F32)
     return pl.pallas_call(
@@ -1373,8 +1381,12 @@
             shape((ROWS, WIDTH), BF), shape((ROWS, WIDTH), F32), narrow, narrow, narrow, narrow,
             shape((32, 4 * WIDTH), F32), shape((ROWS, WIDTH), F32),
         ] + [shape((1, 32), F32)] * 8,
-        in_specs=[vmem] * 7,
-        out_specs=[vmem] * 16,
+        in_specs=[anywhere] * 3 + [vmem] * 4,
+        out_specs=[anywhere] * 2 + [vmem] * 5 + [anywhere] + [vmem] * 8,
+        scratch_shapes=[
+            pltpu.VMEM((ROWS, WIDTH), F32), pltpu.VMEM((ROWS, WIDTH), F32), pltpu.VMEM((ROWS, WIDTH), BF),
+            pltpu.SemaphoreType.DMA((6,)),
+        ],
         compiler_params=pltpu.CompilerParams(vmem_limit_bytes=VMEM_BYTES),
         name="finish",
     )(*args)

time: 203 us -> 205 us (level)
  no operation moved by 1% of the time
where the time goes in v6:
time: 205 us; the launch traced here: 204 us
  Pallas kernels  204 us (100%)
    pallas_call x1, Pallas kernels, call_layer(): pl.pallas_call(layer_kernel, out_shape=[shape((ROWS, WIDTH), BF), shape((...  199 us
    pallas_call x1, Pallas kernels, call_finish(): pl.pallas_call(finish_kernel, out_shape=[shape((ROWS, WIDTH), BF), shape(...  4.2 us

profile of v6, /device:TPU:0, one launch (start us, length us, event | category | flops | bytes accessed | tf_op | source)
XLA Modules:
  0.0 204.5 jit_solution(3633550322183663496)
XLA Ops:
  0.7 199.4 %layer.1 = (bf16[128,1024]{1,0:T(8,128)(2,1)}, f32[128,1024]{1,0:T(8,128)}, f32[128,1024]{1,0:T(8,128)}, bf16[4,32,1024]{2,1,0:T(8,128)(2,1)}, bf16[3,4,32,256]{...) custom-call(bf16[128,1024]{1,0:T(8,128)(2,1)} %bitcast.20, s32[1,128]{1,0:T(1,128)} %seg_hbm.1, ...), custom_call_target="tpu_custom_call" | custom-call | tf_op jit(solution)/shard_map/layer/pallas_call | solution.py:1304
  200.1 4.2 %finish.1 = (bf16[128,1024]{1,0:T(8,128)(2,1)}, f32[128,1024]{1,0:T(8,128)}, f32[32,1024]{1,0:T(8,128)}, f32[32,1024]{1,0:T(8,128)}, f32[32,1024]{1,0:T(8,128)},...) custom-call(bf16[128,1024]{1,0:T(8,128)(2,1)} %get-tuple-element.39., ...), custom_call_target="tpu_custom_call" | custom-call | tf_op jit(solution)/shard_map/finish/pallas_call | solution.py:1378
